TPU v7x, 32 devices: a whole 2x2x4 slice. The times are simulated.
32 devices in a mesh: samp: 4 (over y, x), proto: 8 (over z, core).
Axes of the slice: x: 2, y: 2, z: 4, core: 2. Of those that a mesh axis runs over, the one named last changes fastest.
Arguments:
- embeddings: bfloat16 [2, 2048, 256], P(None, 'samp'), may hold values from -60 to 60
- prototypes: bfloat16 [4096, 256], P('proto'), may hold values from -12 to 12
Outputs:
- grad_embed: bfloat16 [2, 2048, 256], P(None, 'samp')
- grad_proto: bfloat16 [4096, 256], P('proto')
- loss: float32 [2, 2048], P(None, 'samp')
All inputs are finite; a program needn't handle non-finite values.
Results may differ from a plain program's by a relative error of at most 0.001.
The roundings to bfloat16 on the way count: a program that leaves them out, or rounds other values in their place, can miss the bound.
Values may be sent and summed in bfloat16 or wider, within the bound.
No kernel may reach another device: no remote copies, remote signals or barrier semaphores. Data moves between devices by JAX's collectives and lax.ppermute only.
A program may use at most 64 MiB of HBM per device.

v0:
```python
import jax
import jax.numpy as jnp
from jax import lax
from jax.sharding import PartitionSpec as P

ITERS = 3


EPS_SINK = 0.05
TEMPER = 0.1


def normalize_rows(values):
    as_float = values.astype(jnp.float32)
    inverse = lax.rsqrt(jnp.sum(as_float * as_float, axis=-1, keepdims=True) + 1e-06)
    return (as_float * inverse, inverse)


def project(summed, unit_rows, inverse):
    return (summed - unit_rows * jnp.sum(unit_rows * summed, axis=-1, keepdims=True)) * inverse


def body(embeddings, prototypes):
    per_view = embeddings.shape[1]
    unit_emb, inverse_emb = normalize_rows(embeddings)
    unit_proto, inverse_proto = normalize_rows(prototypes)
    emb_b = unit_emb.astype(jnp.bfloat16)
    proto_b = unit_proto.astype(jnp.bfloat16)
    scores = jnp.einsum("vbd,kd->vbk", emb_b, proto_b, preferred_element_type=jnp.float32)
    sink_exp = jnp.exp(scores / EPS_SINK)
    soft_exp = jnp.exp(scores / TEMPER)
    weights = jnp.ones((2, per_view), jnp.float32)
    proto_scale = jnp.ones((2, scores.shape[2]), jnp.float32)
    soft_total = weights
    cross_total = weights
    for sweep in range(ITERS):
        column_sums = jnp.sum(sink_exp * weights[:, :, None], axis=1)
        proto_scale = 1.0 / lax.psum(column_sums, "samp")
        row_sums = jnp.sum(sink_exp * proto_scale[:, None, :], axis=2)
        extras = []
        if sweep == 0:
            extras.append(jnp.sum(soft_exp, axis=2))
        if sweep == ITERS - 1:
            scaled_swap = (sink_exp * proto_scale[:, None, :])[::-1]
            extras.append(jnp.sum(scaled_swap * scores, axis=2))
        totals = lax.psum(jnp.stack([row_sums] + extras), "proto")
        weights = 1.0 / totals[0]
        if sweep == 0:
            soft_total = totals[1]
        if sweep == ITERS - 1:
            cross_total = totals[len(extras)]
    loss = jnp.log(soft_total) - cross_total * weights[::-1] / TEMPER
    assign = sink_exp * proto_scale[:, None, :] * weights[:, :, None]
    softmax_p = soft_exp / soft_total[:, :, None]
    slope_bf = ((softmax_p - assign[::-1]) / TEMPER).astype(jnp.bfloat16)
    proto_part = jnp.einsum("vbk,vbd->kd", slope_bf, emb_b, preferred_element_type=jnp.float32)
    proto_grad = lax.psum(proto_part, "samp")
    grad_proto = project(proto_grad, unit_proto, inverse_proto).astype(jnp.bfloat16)
    emb_part = jnp.einsum("vbk,kd->vbd", slope_bf, proto_b, preferred_element_type=jnp.float32)
    emb_grad = lax.psum(emb_part, "proto")
    grad_embed = project(emb_grad, unit_emb, inverse_emb).astype(jnp.bfloat16)
    return (grad_embed, grad_proto, loss)


def solution(mesh):
    return jax.shard_map(
        body,
        mesh=mesh,
        in_specs=(P(None, "samp", None), P("proto", None)),
        out_specs=(P(None, "samp", None), P("proto", None), P(None, "samp")),
        check_vma=False,
    )
```

profile of v0, /device:TPU:1, one launch (start us, length us, event | category | flops | bytes accessed | tf_op | source)
XLA Modules:
  0.0 201.8 jit_solution(880246192839506283)
XLA Ops:
  7.2 0.0 all-reduce.3.cloned.1.call-start
  7.2 1.1 fusion.21
  8.3 1.3 fusion.12
  9.6 1.8 fusion.13
  11.4 8.7 %psum.56 = f32[2,512]{1,0:T(2,128)S(1)} all-reduce(f32[2,512]{1,0:T(2,128)S(1)} %get-tuple-element.11), channel_id=1, replica_groups=mesh['samp'=4,'proto'=8] {'samp'}, use_global_device_ids=true, to_apply=%region_3.0 | all-reduce | flops 1024 | bytes 8192 | tf_op jit(solution)/shard_map/psum | solution.py:38
  20.1 0.7 multiply_reduce_fusion.4
  20.8 16.0 %psum.57 = f32[2,2,512]{2,1,0:T(2,128)S(1)} all-reduce(f32[2,2,512]{2,1,0:T(2,128)S(1)} %pad_maximum_fusion), channel_id=1, replica_groups=mesh['samp'=4,'proto'=8] {'proto'}, use_global_device_ids=true, to_apply=%region_6.0 | all-reduce | flops 2048 | bytes 16384 | tf_op jit(solution)/shard_map/psum | solution.py:46
  36.9 0.4 multiply_reduce_fusion.3
  37.3 5.9 %psum.58 = f32[2,512]{1,0:T(2,128)S(1)} all-reduce(f32[2,512]{1,0:T(2,128)S(1)} %multiply_reduce_fusion.3), channel_id=1, replica_groups=mesh['samp'=4,'proto'=8] {'samp'}, use_global_device_ids=true, to_apply=%region_8.0 | all-reduce | flops 1024 | bytes 8192 | tf_op jit(solution)/shard_map/psum | solution.py:38
  43.2 0.4 multiply_reduce_fusion.2
  43.6 16.8 %psum.59 = f32[1,2,512]{2,1,0:T(2,128)S(1)} all-reduce(f32[1,2,512]{2,1,0:T(2,128)S(1)} %bitcast.33), channel_id=1, replica_groups=mesh['samp'=4,'proto'=8] {'proto'}, use_global_device_ids=true, to_apply=%region_10.0 | all-reduce | flops 1024 | bytes 8192 | tf_op jit(solution)/shard_map/psum | solution.py:46
  60.5 0.4 multiply_reduce_fusion.1
  60.9 6.9 %psum.60 = f32[2,512]{1,0:T(2,128)S(1)} all-reduce(f32[2,512]{1,0:T(2,128)S(1)} %multiply_reduce_fusion.1), channel_id=1, replica_groups=mesh['samp'=4,'proto'=8] {'samp'}, use_global_device_ids=true, to_apply=%region_12.0 | all-reduce | flops 1024 | bytes 8192 | tf_op jit(solution)/shard_map/psum | solution.py:38
  67.8 0.3 broadcast_multiply_fusion.1
  68.1 0.6 fusion.31
  68.7 15.8 %psum.61 = f32[2,2,512]{2,1,0:T(2,128)S(1)} all-reduce(f32[2,2,512]{2,1,0:T(2,128)S(1)} %pad_maximum_fusion.1), channel_id=1, replica_groups=mesh['samp'=4,'proto'=8] {'proto'}, use_global_device_ids=true, to_apply=%region_15.0 | all-reduce | flops 2048 | bytes 16384 | tf_op jit(solution)/shard_map/psum | solution.py:46
  84.5 0.1 reverse.3
  84.7 0.6 multiply_subtract_fusion
  85.3 0.4 broadcast_multiply_fusion
  85.6 0.0 copy-start
  85.7 0.6 multiply_convert_fusion
  86.2 0.4 copy-done
  86.6 1.6 fusion.27
  88.2 0.0 all-reduce.3.cloned.1.call-update
  88.2 0.0 all-reduce.5.cloned.1.call-start
  88.3 1.4 convolution_bitcast_fusion
  89.7 0.0 all-reduce.5.cloned.1.call-update
  89.7 53.0 %all-reduce.3.cloned.1.call-done = f32[2,512,256]{2,1,0:T(8,128)} async-done(((f32[2,512,256]{2,1,0:T(8,128)}), f32[2,512,256]{2,1,0:T(8,128)}) %all-reduce.3.cloned.1.call-update) | async-done | bytes 1048592 | tf_op jit(solution)/shard_map/psum | solution.py:60
  142.7 7.6 %fusion.9 = bf16[2,512,256]{2,1,0:T(8,128)(2,1)} fusion(f32[2,512,256]{2,1,0:T(8,128)} %all-reduce.3.cloned.1.call-done, bf16[2,512,256]{2,1,0:T(8,128)(2,1)S(1)} %copy-done.1, f32[2,512]{1,0:T(2,128)S(1)} %add_rsqrt_fusion), kind=kOutput, calls=%fused_computation.18 | output fusion | flops 2360575 | bytes 2101248 | tf_op jit(solution)/shard_map/mul | solution.py:20
  150.2 41.4 %all-reduce.5.cloned.1.call-done = f32[512,256]{1,0:T(8,128)} async-done(((f32[512,256]{1,0:T(8,128)}), f32[512,256]{1,0:T(8,128)}) %all-reduce.5.cloned.1.call-update) | async-done | bytes 524304 | tf_op jit(solution)/shard_map/psum | solution.py:57
  191.7 1.3 fusion.17
  193.0 2.0 fusion.20
  (12 shorter events, 0.1 us)
Async XLA Ops:
  7.2 135.5 %all-reduce.3.cloned.1.call-start = ((), (), s32[]{:S(2)}) async-start(), calls=%async_computation | async-start | bytes 2097152 | tf_op jit(solution)/shard_map/psum | solution.py:60
  85.6 1.0 copy-start
  86.6 1.7 copy-start.1
  88.2 103.5 %all-reduce.5.cloned.1.call-start = ((), (), s32[]{:S(2)}) async-start(), calls=%async_computation.1 | async-start | bytes 1048576 | tf_op jit(solution)/shard_map/psum | solution.py:57
Sparse Core Ops, SparseCore 0:
  88.4 54.2 all-reduce.2
  145.6 46.0 all-reduce.4
where the time goes:
time: 203 us; the launch traced here: 202 us
  waiting for transfers between devices  94.5 us (47%)
  blocking collectives  70.2 us (35%)
  other arithmetic  17.6 us (9%)
  between operations  14.1 us (7%)
  matrix products  4.77 us (2%)
    psum x1, waiting for transfers between devices, body(): emb_grad = lax.psum(emb_part, 'proto')  53 us
    psum x3, blocking collectives, body(): totals = lax.psum(jnp.stack([row_sums] + extras), 'proto')  48.7 us
    psum x1, waiting for transfers between devices, body(): proto_grad = lax.psum(proto_part, 'samp')  41.4 us
    psum x3, blocking collectives, body(): proto_scale = 1.0 / lax.psum(column_sums, 'samp')  21.5 us
    mul x1, other arithmetic, project(): unit_rows * jnp.sum(unit_rows * summed, axis=-1, keepdims=True)  7.59 us
  transfers between devices with their start and end apart: 2, of which 2 were waited for; matrix products, arithmetic and copies ran while one was open for 4% of the time, Pallas kernels for 0%

commit v1 on v0

v1 whole, which is shorter than its diff:
```python
import functools
import math

import jax
import jax.numpy as jnp
from jax import lax
from jax.experimental import pallas as pl
from jax.experimental.pallas import tpu as pltpu
from jax.sharding import PartitionSpec as P

ITERS = 3


EPS_SINK = 0.05
TEMPER = 0.1
RADIX = 8
STEP = 2
LOG2E = math.log2(math.e)
VMEM = pl.BlockSpec(memory_space=pltpu.VMEM)
SMEM = pl.BlockSpec(memory_space=pltpu.SMEM)
ANY = pl.BlockSpec(memory_space=pl.ANY)
PARAMS = pltpu.CompilerParams(vmem_limit_bytes=24 << 20)
SMALL = pltpu.CompilerParams(vmem_limit_bytes=8 << 20)


def normalize_rows(values):
    as_float = values.astype(jnp.float32)
    inverse = lax.rsqrt(jnp.sum(as_float * as_float, axis=-1, keepdims=True) + 1e-06)
    return (as_float * inverse, inverse)


def project(summed, unit_rows, inverse):
    return (summed - unit_rows * jnp.sum(unit_rows * summed, axis=-1, keepdims=True)) * inverse


def groups_of(size, first, later=RADIX):
    found, stride, limit = [], 1, first
    while stride < size:
        radix = min(limit, size // stride)
        found.append((stride, radix))
        stride, limit = stride * radix, later
    return found


def swap(value, axis, size, mask):
    return lax.ppermute(value, axis, [(i, i ^ mask) for i in range(size)])


def tree_sum(parts):
    while len(parts) > 1:
        parts = [parts[i] + parts[i + 1] for i in range(0, len(parts), 2)]
    return parts[0]


def sum_all(value, axis, size):
    for stride, radix in groups_of(size, STEP, STEP):
        value = tree_sum([value] + [swap(value, axis, size, stride * j) for j in range(1, radix)])
    return value


def digit_of(axis, stride, radix):
    return (lax.axis_index(axis) // stride) % radix


def scatter_sum(value, axis, size, first):
    value = value[None]
    for stride, radix in groups_of(size, first):
        digit = digit_of(axis, stride, radix)
        value = value.reshape((radix, -1) + value.shape[2:]) if value.shape[0] == 1 else value
        parts = [lax.dynamic_index_in_dim(value, digit ^ j, 0, keepdims=False) for j in range(radix)]
        got = [parts[0]] + [swap(parts[j], axis, size, stride * j) for j in range(1, radix)]
        value = tree_sum(got)[None]
    return value[0, 0]


def own_entry(axis, size, first):
    entry, left = 0, size
    for stride, radix in groups_of(size, first):
        left //= radix
        entry = entry + digit_of(axis, stride, radix) * left
    return entry


def gather_all(value, axis, size, first):
    value = value[None]
    for stride, radix in reversed(groups_of(size, first)):
        digit = digit_of(axis, stride, radix)
        got = [value] + [swap(value, axis, size, stride * j) for j in range(1, radix)]
        whole = jnp.zeros((radix,) + value.shape, value.dtype)
        for j in range(radix):
            whole = lax.dynamic_update_index_in_dim(whole, got[j], digit ^ j, 0)
        value = whole.reshape((-1,) + value.shape[1:])
    return value


def body_large(samp, proto, embeddings, prototypes):
    per_view = embeddings.shape[1]
    width = embeddings.shape[2]
    unit_emb, inverse_emb = normalize_rows(embeddings)
    unit_proto, inverse_proto = normalize_rows(prototypes)
    emb_b = unit_emb.astype(jnp.bfloat16)
    proto_b = unit_proto.astype(jnp.bfloat16)
    scores = jnp.einsum("vbd,kd->vbk", emb_b, proto_b, preferred_element_type=jnp.float32)
    sink_exp = jnp.exp(scores / EPS_SINK)
    soft_exp = jnp.exp(scores / TEMPER)
    weights = jnp.ones((2, per_view), jnp.float32)
    proto_scale = jnp.ones((2, scores.shape[2]), jnp.float32)
    soft_total = weights
    cross_total = weights
    for sweep in range(ITERS):
        column_sums = jnp.sum(sink_exp * weights[:, :, None], axis=1)
        proto_scale = 1.0 / sum_all(column_sums, "samp", samp)
        row_sums = jnp.sum(sink_exp * proto_scale[:, None, :], axis=2)
        extras = []
        if sweep == 0:
            extras.append(jnp.sum(soft_exp, axis=2))
        if sweep == ITERS - 1:
            scaled_swap = (sink_exp * proto_scale[:, None, :])[::-1]
            extras.append(jnp.sum(scaled_swap * scores, axis=2))
        totals = sum_all(jnp.stack([row_sums] + extras), "proto", proto)
        weights = 1.0 / totals[0]
        if sweep == 0:
            soft_total = totals[1]
        if sweep == ITERS - 1:
            cross_total = totals[len(extras)]
    loss = jnp.log(soft_total) - cross_total * weights[::-1] / TEMPER
    assign = sink_exp * proto_scale[:, None, :] * weights[:, :, None]
    softmax_p = soft_exp / soft_total[:, :, None]
    slope_bf = ((softmax_p - assign[::-1]) / TEMPER).astype(jnp.bfloat16)

    emb_part = jnp.einsum("vbk,kd->vbd", slope_bf, proto_b, preferred_element_type=jnp.float32)
    rows = per_view // proto
    emb_part = emb_part.reshape(2, proto, rows, width).transpose(1, 0, 2, 3)
    emb_grad = scatter_sum(emb_part, "proto", proto, 2)
    entry = own_entry("proto", proto, 2)
    own_unit = lax.dynamic_slice_in_dim(unit_emb, entry * rows, rows, 1)
    own_inverse = lax.dynamic_slice_in_dim(inverse_emb, entry * rows, rows, 1)
    own_embed = project(emb_grad, own_unit, own_inverse).astype(jnp.bfloat16)

    proto_part = jnp.einsum("vbk,vbd->kd", slope_bf, emb_b, preferred_element_type=jnp.float32)
    lines = prototypes.shape[0] // samp
    proto_grad = scatter_sum(proto_part.reshape(samp, lines, width), "samp", samp, RADIX)
    entry = own_entry("samp", samp, RADIX)
    own_unit = lax.dynamic_slice_in_dim(unit_proto, entry * lines, lines, 0)
    own_inverse = lax.dynamic_slice_in_dim(inverse_proto, entry * lines, lines, 0)
    own_proto = project(proto_grad, own_unit, own_inverse).astype(jnp.bfloat16)

    grad_proto = gather_all(own_proto, "samp", samp, RADIX).reshape(prototypes.shape)
    grad_embed = gather_all(own_embed, "proto", proto, 2)
    grad_embed = grad_embed.transpose(1, 0, 2, 3).reshape(embeddings.shape)
    return (grad_embed, grad_proto, loss)


def dot_t(a, b):
    return lax.dot_general(a, b, (((1,), (1,)), ((), ())), preferred_element_type=jnp.float32)


def dot_n(a, b):
    return lax.dot_general(a, b, (((1,), (0,)), ((), ())), preferred_element_type=jnp.float32)


def unit_kernel(*refs):
    half = len(refs) // 2
    for raw_ref, out_ref in zip(refs[:half], refs[half:]):
        out_ref[...] = normalize_rows(raw_ref[...])[0].astype(jnp.bfloat16)


def score_kernel(tile, emb_ref, proto_ref, sink_ref, soft_ref, *column_refs):
    rows = emb_ref.shape[0] // 2
    for view in range(2):
        emb = emb_ref[view * rows:(view + 1) * rows]
        total = jnp.zeros((8, rows), jnp.float32)
        for at in range(0, proto_ref.shape[0], tile):
            soft = jnp.exp2(dot_t(proto_ref[at:at + tile], emb) * (LOG2E / TEMPER))
            sink = soft * soft
            sink_ref[view, at:at + tile] = sink
            total = total + jnp.sum(soft.reshape(-1, 8, rows), axis=0)
            for column_ref in column_refs:
                lanes = sum(sink[:, lane:lane + 128] for lane in range(0, rows, 128))
                column_ref[view:view + 1, at:at + tile] = jnp.sum(lanes.T, axis=0, keepdims=True)
        soft_ref[view:view + 1] = jnp.sum(total, axis=0, keepdims=True)


def sweep_kernel(last, tile, weight_ref, own_ref, one_ref, two_ref, three_ref, *refs):
    out_ref = refs[-1]
    blocks = (own_ref, one_ref, two_ref, three_ref)
    _, count, rows = own_ref.shape
    if last:
        cross = [jnp.zeros((8, rows), jnp.float32)] * 2
        out_ref[...] = jnp.zeros(out_ref.shape, jnp.float32)
    for view in range(2):
        weight = [jnp.broadcast_to(weight_ref[2 * at + view:2 * at + view + 1], (8, rows)) for at in range(4)]
        totals = [jnp.zeros((8, rows), jnp.float32)] * 4
        for first in range(0, count, tile):
            part = slice(first, first + tile)
            lanes = []
            for at in range(4):
                scaled = blocks[at][view, part].reshape(-1, 8, rows) * weight[at]
                scaled = scaled.reshape(tile, rows)
                lanes.append(sum(scaled[:, lane:lane + 128] for lane in range(0, rows, 128)))
            scale = 1.0 / jnp.sum(tree_sum(lanes), axis=1, keepdims=True)
            for at in range(4):
                scaled = blocks[at][view, part] * scale
                totals[at] = totals[at] + jnp.sum(scaled.reshape(-1, 8, rows), axis=0)
                if last and at == 0:
                    scaled = scaled * (jnp.log(own_ref[1 - view, part]) * EPS_SINK)
                    cross[1 - view] = cross[1 - view] + jnp.sum(scaled.reshape(-1, 8, rows), axis=0)
            if last:
                line = 10 + 2 * view + first // rows
                out_ref[line:line + 1, first % rows:first % rows + tile] = jnp.broadcast_to(scale, (tile, 128)).T[:1]
        for at in range(4):
            out_ref[2 * at + view:2 * at + view + 1] = jnp.sum(totals[at], axis=0, keepdims=True)
    if last:
        for view in range(2):
            out_ref[8 + view:9 + view] = jnp.sum(cross[view], axis=0, keepdims=True)
    else:
        for at in range(4):
            out_ref[8 + 2 * at:10 + 2 * at] = refs[at][...]


def found_kernel(mine_ref, theirs_ref, soft_ref, out_ref):
    totals = mine_ref[:10] + theirs_ref[:10]
    weights = 1.0 / totals[:8]
    soft = soft_ref[...]
    for view in range(2):
        crossed = totals[8 + view:9 + view] * weights[1 - view:2 - view]
        out_ref[view:view + 1] = jnp.log(soft[view:view + 1]) - crossed / TEMPER
    out_ref[2:10] = mine_ref[10:18]
    out_ref[10:18] = theirs_ref[10:18]
    out_ref[18:26] = weights / TEMPER
    out_ref[26:34] = 1.0 / (TEMPER * soft)


def finish(summed, raw):
    unit, inverse = normalize_rows(raw)
    return project(summed, unit, inverse).astype(jnp.bfloat16)


def column(row):
    return jnp.broadcast_to(row, (128, row.shape[1])).T


def widen(col, lanes):
    return jnp.concatenate([col] * (lanes // 128), axis=1)


def scale_row(found_ref, block, view, half):
    line = 2 + 4 * block + 2 * view + half
    return found_ref[line:line + 1]


def weight_row(found_ref, block, view):
    line = 18 + 2 * block + view
    return found_ref[line:line + 1]


def soft_row(found_ref, block, view):
    line = 26 + 2 * block + view
    return found_ref[line:line + 1]


def pipeline(steps, products_of, factors_of, place, soft_ref, slope_ref, rows):
    def slopes(step, first, last):
        slot = step % 2
        own_of, other_of = factors_of(step)
        for at in range(first, last, 16):
            part = slice(at, at + 16)
            soft = [jnp.exp2(soft_ref[(slot,) + place(view, part)] * (LOG2E / TEMPER)) for view in range(2)]
            taken = [other_of(view, part, soft[view] * soft[view]) for view in range(2)]
            for view in range(2):
                slope = own_of(view, part, soft[view]) - taken[1 - view]
                slope_ref[(slot,) + place(view, part)] = slope.astype(jnp.bfloat16)

    for step in range(-1, steps + 1):
        products = products_of(step + 1 if step + 1 < steps else None, step - 1 if step >= 1 else None)
        cuts = [rows * at // len(products) // 16 * 16 for at in range(len(products) + 1)]
        for at, product in enumerate(products):
            product()
            if 0 <= step < steps:
                slopes(step, cuts[at], cuts[at + 1])


def fetch_rows(sources, rows_ref, sem_ref):
    fetches = [pltpu.make_async_copy(source, rows_ref.at[at], sem_ref.at[at]) for at, source in enumerate(sources)]
    for fetch in fetches:
        fetch.start()
    return fetches


def proto_grad_kernel(tile, own_ref, one_ref, two_ref, three_ref, proto_ref, raw_ref, lead_raw_ref, found_ref,
                      out_ref, loss_ref, col_ref, acc_ref, work_ref, slope_ref, rows_ref, sem_ref):
    fetches = fetch_rows((raw_ref, lead_raw_ref), rows_ref, sem_ref)
    loss_ref[...] = found_ref[:2]
    blocks = (own_ref, one_ref, two_ref, three_ref)
    rows = own_ref.shape[0] // 2
    tiles = proto_ref.shape[0] // tile
    for view in range(2):
        for first in range(0, proto_ref.shape[0], rows):
            col_ref[view, first:first + rows] = column(scale_row(found_ref, 0, view, first // rows))

    def score(step, at):
        first = step % tiles * tile
        proto = proto_ref[first:first + tile]
        work_ref[step % 2, :, at:at + 256] = dot_t(proto, blocks[step // tiles][at:at + 256])

    def gradient(step):
        first = step % tiles * tile
        acc_ref[step // tiles, first:first + tile] = dot_n(slope_ref[step % 2], blocks[step // tiles][...])

    def products_of(ahead, behind):
        scores = [] if ahead is None else [functools.partial(score, ahead, at) for at in range(0, 2 * rows, 256)]
        grads = [] if behind is None else [functools.partial(gradient, behind)]
        half = len(scores) // 2
        return scores[:half] + grads + scores[half:]

    def factors_of(step):
        block = step // tiles
        soft = [jnp.broadcast_to(soft_row(found_ref, block, view), (16, rows)) for view in range(2)]
        weight = [jnp.broadcast_to(weight_row(found_ref, block, view), (16, rows)) for view in range(2)]
        base = step % tiles * tile

        def other_of(view, part, sink):
            return sink * widen(col_ref[view, base + part.start:base + part.stop], rows) * weight[view]

        return (lambda view, part, value: value * soft[view]), other_of

    def place(view, part):
        return part, slice(view * rows, (view + 1) * rows)

    pipeline(len(blocks) * tiles, products_of, factors_of, place, work_ref, slope_ref, tile)
    half = raw_ref.shape[0]
    for at in range(2):
        part = slice(at * half, (at + 1) * half)
        fetches[at].wait()
        out_ref[at] = finish(tree_sum([acc_ref[block, part] for block in range(4)]), rows_ref[at])


def emb_grad_kernel(tile, own_ref, one_ref, two_ref, three_ref, emb_ref, raw_ref, found_ref,
                    out_ref, loss_ref, col_ref, acc_ref, work_ref, slope_ref, rows_ref, sem_ref):
    fetches = fetch_rows((raw_ref.at[0], raw_ref.at[1]), rows_ref, sem_ref)
    loss_ref[...] = found_ref[:2]
    blocks = (own_ref, one_ref, two_ref, three_ref)
    rows = emb_ref.shape[0] // 2
    tiles = own_ref.shape[0] // tile
    for view in range(2):
        col_ref[view] = column(soft_row(found_ref, 0, view))
        col_ref[2 + view] = column(weight_row(found_ref, 0, view))

    def score(step, at):
        first = step % tiles * tile + at
        work_ref[step % 2, :, at:at + 256] = dot_t(emb_ref[...], blocks[step // tiles][first:first + 256])

    def gradient(step):
        block, first = step // tiles, step % tiles * tile
        grad = dot_n(slope_ref[step % 2], blocks[block][first:first + tile])
        if step % tiles:
            grad = grad + acc_ref[block]
        acc_ref[block] = grad

    def products_of(ahead, behind):
        scores = [] if ahead is None else [functools.partial(score, ahead, at) for at in range(0, tile, 256)]
        grads = [] if behind is None else [functools.partial(gradient, behind)]
        return scores[:1] + grads + scores[1:]

    def factors_of(step):
        block, half = step // tiles, step % tiles
        scale = [jnp.broadcast_to(scale_row(found_ref, block, view, half), (16, tile)) for view in range(2)]

        def own_of(view, part, value):
            return value * widen(col_ref[view, part], tile)

        def other_of(view, part, sink):
            return sink * scale[view] * widen(col_ref[2 + view, part], tile)

        return own_of, other_of

    def place(view, part):
        return (slice(view * rows + part.start, view * rows + part.stop),)

    pipeline(len(blocks) * tiles, products_of, factors_of, place, work_ref, slope_ref, rows)
    for view in range(2):
        part = slice(view * rows, (view + 1) * rows)
        total = tree_sum([acc_ref[block, part] for block in range(len(blocks))])
        fetches[view].wait()
        out_ref[view] = finish(total, rows_ref[view])


def own_part_kernel(core_ref, mine_ref, embed_ref, proto_ref, sem_ref):
    @pl.when(core_ref[0] == 0)
    def _():
        copy = pltpu.make_async_copy(mine_ref, embed_ref, sem_ref)
        copy.start()
        copy.wait()

    @pl.when(core_ref[0] == 1)
    def _():
        copy = pltpu.make_async_copy(mine_ref.at[1], proto_ref, sem_ref)
        copy.start()
        copy.wait()


def other_part_kernel(core_ref, theirs_ref, embed_in_ref, proto_in_ref, embed_ref, proto_ref, sem_ref):
    @pl.when(core_ref[0] == 0)
    def _():
        copy = pltpu.make_async_copy(theirs_ref.at[0], proto_ref, sem_ref)
        copy.start()
        copy.wait()

    @pl.when(core_ref[0] == 1)
    def _():
        copy = pltpu.make_async_copy(theirs_ref, embed_ref, sem_ref)
        copy.start()
        copy.wait()


def chip_masks(size, bits):
    return [bits << i for i in range((size // bits).bit_length() - 1)]


def chip_sum(value, axis, size, bits):
    for mask in chip_masks(size, bits):
        value = value + swap(value, axis, size, mask)
    return value


def chip_gather(value, axis, size, bits):
    value = value[None]
    for mask in chip_masks(size, bits):
        value = jnp.concatenate([value, swap(value, axis, size, mask)])
    return value


def scored(flat, proto_b, columns):
    rows, width = flat.shape
    count = proto_b.shape[0]
    shapes = [(2, count, rows // 2), (2, rows // 2)] + [(2, count)] * columns
    return pl.pallas_call(
        functools.partial(score_kernel, min(count, 256)),
        out_shape=[jax.ShapeDtypeStruct(shape, jnp.float32) for shape in shapes],
        in_specs=[VMEM] * 2,
        out_specs=[VMEM] * len(shapes),
        compiler_params=SMALL,
        cost_estimate=pl.CostEstimate(
            flops=2 * rows * count * width, bytes_accessed=2 * (rows + count) * width, transcendentals=rows * count
        ),
    )(flat, proto_b)


def swept(last, weights, sinks, softs):
    _, count, rows = sinks[0].shape
    return pl.pallas_call(
        functools.partial(sweep_kernel, last, 128),
        out_shape=jax.ShapeDtypeStruct((16, rows), jnp.float32),
        in_specs=[VMEM] * (5 + len(softs)),
        out_specs=VMEM,
        compiler_params=SMALL,
        cost_estimate=pl.CostEstimate(flops=32 * rows * count, bytes_accessed=4 * rows * count, transcendentals=0),
    )(weights, *sinks, *softs)


def after(value, first):
    return lax.optimization_barrier((value, first))


def sweeps(samp, proto, flat, own, other):
    proto_b = jnp.concatenate([other, own])
    sink, soft, sums = scored(flat, proto_b, True)
    sums = sums + swap(sums, "samp", samp, 1)
    block, sums = after(flat, sums)
    one = swap(block, "samp", samp, 1)
    sums = sums + swap(sums, "samp", samp, 2)
    block, sums = after(flat, sums)
    two = swap(block, "samp", samp, 2)
    sums = jnp.sum(sink * (1.0 / sums)[:, :, None], axis=1)
    sums = sums + swap(sums, "proto", proto, 2)
    one, sums = after(one, sums)
    three = swap(one, "samp", samp, 2)
    weights = 1.0 / (sums + swap(sums, "proto", proto, 4))

    sinks, softs = [sink], [soft]
    for block in (one, two, three):
        sink, soft = scored(block, proto_b, False)
        sinks.append(sink)
        softs.append(soft)
    for mask in chip_masks(samp, 1):
        weights = jnp.concatenate([weights, swap(weights, "samp", samp, mask)])
    totals = chip_sum(swept(False, weights, sinks, softs), "proto", proto, 2)
    soft_total = totals[8:]

    totals = swept(True, 1.0 / totals[:8], sinks, [])
    got = swap(totals, "proto", proto, 2)
    totals = jnp.concatenate([totals[:10] + got[:10], totals[10:14], got[10:14]])
    found = pl.pallas_call(
        found_kernel,
        out_shape=jax.ShapeDtypeStruct((34, flat.shape[0] // 2), jnp.float32),
        in_specs=[VMEM] * 3,
        out_specs=VMEM,
        compiler_params=SMALL,
    )(totals, swap(totals, "proto", proto, 4), soft_total)
    return found, one, two, three


def gathers(proto, flat, own, other):
    proto_b = jnp.concatenate([own, other])

    def middle(value):
        return lax.ppermute(value, "proto", [(2, 4), (4, 2)])

    one = swap(proto_b, "proto", proto, 2)
    near = middle(proto_b)
    far = middle(one)
    outer_near = swap(near, "proto", proto, 2)
    outer_far = swap(far, "proto", proto, 2)
    chip = lax.axis_index("proto") // 2
    inner = (chip == 1) | (chip == 2)
    two = jnp.where(inner, far, outer_near)
    three = jnp.where(inner, near, outer_far)
    return jnp.zeros((34, flat.shape[0] // 2), jnp.float32), one, two, three


def unit_rows(*raws):
    return pl.pallas_call(
        unit_kernel,
        out_shape=[jax.ShapeDtypeStruct(raw.shape, jnp.bfloat16) for raw in raws],
        in_specs=[VMEM] * len(raws),
        out_specs=[VMEM] * len(raws),
        compiler_params=SMALL,
    )(*raws)


def body(samp, proto, embeddings, prototypes):
    _, per_view, width = embeddings.shape
    count = prototypes.shape[0]
    core = lax.axis_index("proto") % 2
    lead = core == 1
    raw_other = swap(prototypes, "proto", proto, 1)
    flat, own = unit_rows(embeddings.reshape(2 * per_view, width), prototypes)
    other, = unit_rows(raw_other)
    found, *gathered = lax.cond(
        lead, functools.partial(sweeps, samp, proto), functools.partial(gathers, proto), flat, own, other
    )
    taken = swap(found, "proto", proto, 1)
    tile = min(2 * count, 512)

    def grads(kernel, operands, raws, columns, rows, lanes):
        return pl.pallas_call(
            functools.partial(kernel, rows if kernel is proto_grad_kernel else lanes),
            out_shape=(
                jax.ShapeDtypeStruct((2, per_view, width), jnp.bfloat16),
                jax.ShapeDtypeStruct((2, per_view), jnp.float32),
            ),
            in_specs=[VMEM] * len(operands) + [ANY] * len(raws) + [VMEM],
            out_specs=(VMEM,) * 2,
            scratch_shapes=[
                pltpu.VMEM(columns, jnp.float32),
                pltpu.VMEM((4, 2 * count, width), jnp.float32),
                pltpu.VMEM((2, rows, lanes), jnp.float32),
                pltpu.VMEM((2, rows, lanes), jnp.bfloat16),
                pltpu.VMEM((2, per_view, width), jnp.bfloat16),
                pltpu.SemaphoreType.DMA((2,)),
            ],
            compiler_params=PARAMS,
        )(*operands, *raws, found if kernel is proto_grad_kernel else taken)[::-1]

    def proto_grads(flat, own, other, *gathered):
        proto_b = jnp.concatenate([other, own])
        operands = (flat, *gathered, proto_b)
        return grads(proto_grad_kernel, operands, (raw_other, prototypes), (2, 2 * count, 128), 2 * count, 2 * per_view)

    def emb_grads(flat, own, other, *gathered):
        proto_b = jnp.concatenate([own, other])
        operands = (proto_b, *gathered, flat)
        return grads(emb_grad_kernel, operands, (embeddings,), (4, per_view, 128), 2 * per_view, tile)

    loss, mine = lax.cond(lead, proto_grads, emb_grads, flat, own, other, *gathered)
    theirs = swap(mine, "proto", proto, 1)
    outputs = (
        jax.ShapeDtypeStruct(embeddings.shape, jnp.bfloat16),
        jax.ShapeDtypeStruct(prototypes.shape, jnp.bfloat16),
    )
    half_done = pl.pallas_call(
        own_part_kernel,
        out_shape=outputs,
        in_specs=[SMEM, ANY],
        out_specs=(ANY, ANY),
        scratch_shapes=[pltpu.SemaphoreType.DMA],
        compiler_params=SMALL,
    )(core.reshape(1), mine)
    grad_embed, grad_proto = pl.pallas_call(
        other_part_kernel,
        out_shape=outputs,
        in_specs=[SMEM, ANY, ANY, ANY],
        out_specs=(ANY, ANY),
        scratch_shapes=[pltpu.SemaphoreType.DMA],
        input_output_aliases={2: 0, 3: 1},
        compiler_params=SMALL,
    )(core.reshape(1), theirs, *half_done)
    return grad_embed, grad_proto, loss


def solution(mesh):
    samp, proto = mesh.shape["samp"], mesh.shape["proto"]

    def run(embeddings, prototypes):
        paired = samp == 4 and proto == 8 and prototypes.shape[0] == embeddings.shape[1] == 512
        return (body if paired else body_large)(samp, proto, embeddings, prototypes)

    return jax.shard_map(
        run,
        mesh=mesh,
        in_specs=(P(None, "samp", None), P("proto", None)),
        out_specs=(P(None, "samp", None), P("proto", None), P(None, "samp")),
        check_vma=False,
    )
```

time: 203 us -> 58.8 us (0.29)
  waiting for transfers between devices: 94.5 us -> 16.5 us
  blocking collectives: 70.2 us -> 0 us
  starting transfers between devices: 0.08 us -> 21.1 us
  Pallas kernels: 0 us -> 18.9 us
  other arithmetic: 17.6 us -> 0.48 us
  between operations: 14.1 us -> 0.85 us
  matrix products: 4.77 us -> 0 us
    psum x2 -> x0, waiting for transfers between devices: 94.4 us -> none  [the longest x1 53 us: body(): emb_grad = lax.psum(emb_part, 'proto')]
    psum x6 -> x0, blocking collectives: 70.2 us -> none  [the longest x3 48.7 us: body(): totals = lax.psum(jnp.stack([row_sums] + extras), 'proto')]
    ppermute x0 -> x16, starting transfers between devices: none -> 21.1 us  [swap(): return lax.ppermute(value, axis, [(i, i ^ mask) for i in range(size)])]
    pallas_call x0 -> x12, Pallas kernels: none -> 18.9 us  [the longest x1 6.24 us: grads(): pl.pallas_call(functools.partial(kernel, rows if kernel is proto_grad_ker...]
    ppermute x0 -> x16, waiting for transfers between devices: none -> 16.5 us  [swap(): return lax.ppermute(value, axis, [(i, i ^ mask) for i in range(size)])]
    mul x3 -> x0, other arithmetic: 8.27 us -> none  [the longest x1 7.59 us: project(): unit_rows * jnp.sum(unit_rows * summed, axis=-1, keepdims=True)]
    reduce_sum x8 -> x1, other arithmetic: 6.14 us -> 0.35 us  [sweeps(): sums = jnp.sum(sink * (1.0 / sums)[:, :, None], axis=1)]
    dot_general x3 -> x0, matrix products: 4.77 us -> none  [the longest x1 1.81 us: body(): jnp.einsum('vbd,kd->vbk', emb_b, proto_b, preferred_element_type=jnp.floa...]
  transfers between devices with their start and end apart: 2 -> 16, of which waited for: 2 -> 12; matrix products, arithmetic and copies ran while one was open for 4% -> 1% of each run, Pallas kernels for 0% -> 6%
where the time goes in v1:
time: 58.8 us; the launch traced here: 58.6 us
  starting transfers between devices  21.1 us (36%)
  Pallas kernels  18.9 us (32%)
  waiting for transfers between devices  16.5 us (28%)
  between operations  0.85 us (1%)
  local copies, waits for them, and re-layouts  0.63 us (1%)
    ppermute x16, starting transfers between devices, swap(): return lax.ppermute(value, axis, [(i, i ^ mask) for i in range(size)])  21.1 us
    ppermute x16, waiting for transfers between devices, swap(): return lax.ppermute(value, axis, [(i, i ^ mask) for i in range(size)])  16.5 us
    pallas_call x1, Pallas kernels, grads(): pl.pallas_call(functools.partial(kernel, rows if kernel is proto_grad_ker...  6.24 us
    pallas_call x2, Pallas kernels, swept(): pl.pallas_call(functools.partial(sweep_kernel, last, 128), out_shape=jax....  6.21 us
    pallas_call x4, Pallas kernels, scored(): pl.pallas_call(functools.partial(score_kernel, min(count, 256)), out_shap...  3.32 us
    pallas_call x2, Pallas kernels, unit_rows(): pl.pallas_call(unit_kernel, out_shape=[jax.ShapeDtypeStruct(raw.shape, jn...  1.55 us
  transfers between devices with their start and end apart: 16, of which 12 were waited for; matrix products, arithmetic and copies ran while one was open for 1% of the time, Pallas kernels for 6%

profile of v1, /device:TPU:1, one launch (start us, length us, event | category | flops | bytes accessed | tf_op | source)
XLA Modules:
  0.0 58.6 jit_solution(8421187310467388156)
XLA Ops:
  0.8 1.4 %shard_map.49 = (bf16[1024,256]{1,0:T(8,128)(2,1)S(1)}, bf16[512,256]{1,0:T(8,128)(2,1)S(1)}) custom-call(bf16[1024,256]{1,0:T(8,128)(2,1)} %bitcast.2, bf16[512,256]{1,0:T(8,128)(2,1)} %refs_1_.1), custom_call_target="tpu_custom_call" | custom-call | tf_op jit(solution)/shard_map/pallas_call | solution.py:522
  3.1 44.9 %conditional.2 = (f32[34,512]{1,0:T(8,128)S(1)}, bf16[1024,256]{1,0:T(8,128)(2,1)S(1)}, bf16[1024,256]{1,0:T(8,128)(2,1)S(1)}, bf16[1024,256]{1,0:T(8,128)(2,1)S(1)}) conditional(s32[]{:T(128)} %convert_element_type.4, (bf16[512,256]{1,0:T(8,128)(2,1)S(1)}, bf16[512,256]{1,0:T(8,128)(2,1)S(1)}) %tuple.27, (bf16[512,256]{1,0:T(8,128)(2,1)S(1)}, ...), branch_computations={%region_0.1_spmd, %region_1.3_spmd} | conditional | flops 2183197696 | bytes 33776336 | solution.py:539
  3.2 1.0 %branch_1_fun.8 = (f32[2,1024,512]{2,1,0:T(8,128)S(1)}, f32[2,512]{1,0:T(2,128)S(1)}, f32[2,1024]{1,0:T(2,128)S(1)}) custom-call(bf16[1024,256]{1,0:T(8,128)(2,1)S(1)} %get-tuple-element.57.emb_ref, bf16[1024,256]{1,0:T(8,128)(2,1)S(1)} %constant_dynamic-update-slice_fusion.2.proto_ref), custom_call_target="tpu_custom_call" | custom-call | flops 536870912 | bytes 1048576 | tf_op jit(solution)/shard_map/cond/branch_1_fun/pallas_call | solution.py:437
  4.2 2.4 %collective-permute-start.5 = (f32[2,1024]{1,0:T(2,128)S(1)}, f32[2,1024]{1,0:T(2,128)S(1)}, u32[]{:S(2)}, u32[]{:S(2)}) collective-permute-start(f32[2,1024]{1,0:T(2,128)S(1)} %get-tuple-element.49), channel_id=1, source_target_pairs={{0,8},{8,0},{16,24},{24,16},{1,9},{9,1},{17,25},{25,17},{2,10},{10... | collective-permute-start | bytes 24584 | tf_op jit(solution)/shard_map/cond/branch_1_fun/ppermute | solution.py:46
  6.7 1.3 %collective-permute-done.5 = f32[2,1024]{1,0:T(2,128)S(1)} collective-permute-done((f32[2,1024]{1,0:T(2,128)S(1)}, f32[2,1024]{1,0:T(2,128)S(1)}, u32[]{:S(2)}, u32[]{:S(2)}) %collective-permute-start.5) | collective-permute-done | bytes 8224 | tf_op jit(solution)/shard_map/cond/branch_1_fun/ppermute | solution.py:46
  8.0 1.5 %collective-permute-start.6 = (bf16[1024,256]{1,0:T(8,128)(2,1)S(1)}, bf16[1024,256]{1,0:T(8,128)(2,1)S(1)}, u32[]{:S(2)}, u32[]{:S(2)}) collective-permute-start(bf16[1024,256]{1,0:T(8,128)(2,1)S(1)} %get-tuple-element.57.emb_ref), channel_id=1, source_target_pairs={{0,8},{8,0},{16,24},{24,16},{1,9},{9,1},{17,25},{25,17},{2,10},{10... | collective-permute-start | bytes 1572872 | tf_op jit(solution)/shard_map/cond/branch_1_fun/ppermute | solution.py:46
  9.5 1.2 %collective-permute-start.7 = (f32[2,1024]{1,0:T(2,128)S(1)}, f32[2,1024]{1,0:T(2,128)S(1)}, u32[]{:S(2)}, u32[]{:S(2)}) collective-permute-start(f32[2,1024]{1,0:T(2,128)S(1)} %add.18), channel_id=1, source_target_pairs={{0,16},{8,24},{16,0},{24,8},{1,17},{9,25},{17,1},{25,9},{2,18},{10... | collective-permute-start | bytes 24584 | tf_op jit(solution)/shard_map/cond/branch_1_fun/ppermute | solution.py:46
  10.7 1.6 %collective-permute-done.7 = f32[2,1024]{1,0:T(2,128)S(1)} collective-permute-done((f32[2,1024]{1,0:T(2,128)S(1)}, f32[2,1024]{1,0:T(2,128)S(1)}, u32[]{:S(2)}, u32[]{:S(2)}) %collective-permute-start.7) | collective-permute-done | bytes 8224 | tf_op jit(solution)/shard_map/cond/branch_1_fun/ppermute | solution.py:46
  12.3 1.2 %collective-permute-start.12 = (bf16[1024,256]{1,0:T(8,128)(2,1)S(1)}, bf16[1024,256]{1,0:T(8,128)(2,1)S(1)}, u32[]{:S(2)}, u32[]{:S(2)}) collective-permute-start(bf16[1024,256]{1,0:T(8,128)(2,1)S(1)} %get-tuple-element.57.emb_ref), channel_id=1, source_target_pairs={{0,16},{8,24},{16,0},{24,8},{1,17},{9,25},{17,1},{25,9},{2,18},{10... | collective-permute-start | bytes 1572872 | tf_op jit(solution)/shard_map/cond/branch_1_fun/ppermute | solution.py:46
  13.9 1.4 %collective-permute-start.8 = (f32[2,512]{1,0:T(2,128)S(1)}, f32[2,512]{1,0:T(2,128)S(1)}, u32[]{:S(2)}, u32[]{:S(2)}) collective-permute-start(f32[2,512]{1,0:T(2,128)S(1)} %multiply_reduce_fusion), channel_id=1, source_target_pairs={{0,2},{1,3},{2,0},{3,1},{4,6},{5,7},{6,4},{7,5},{8,10},{9,11},{10,... | collective-permute-start | bytes 12296 | tf_op jit(solution)/shard_map/cond/branch_1_fun/ppermute | solution.py:46
  15.2 1.2 %collective-permute-done.8 = f32[2,512]{1,0:T(2,128)S(1)} collective-permute-done((f32[2,512]{1,0:T(2,128)S(1)}, f32[2,512]{1,0:T(2,128)S(1)}, u32[]{:S(2)}, u32[]{:S(2)}) %collective-permute-start.8) | collective-permute-done | bytes 4128 | tf_op jit(solution)/shard_map/cond/branch_1_fun/ppermute | solution.py:46
  16.4 2.7 %collective-permute-start.9 = (f32[2,512]{1,0:T(2,128)S(1)}, f32[2,512]{1,0:T(2,128)S(1)}, u32[]{:S(2)}, u32[]{:S(2)}) collective-permute-start(f32[2,512]{1,0:T(2,128)S(1)} %add.20), channel_id=1, source_target_pairs={{0,4},{1,5},{2,6},{3,7},{4,0},{5,1},{6,2},{7,3},{8,12},{9,13},{10,... | collective-permute-start | bytes 12296 | tf_op jit(solution)/shard_map/cond/branch_1_fun/ppermute | solution.py:46
  19.1 1.0 %collective-permute-start.13 = (bf16[1024,256]{1,0:T(8,128)(2,1)S(1)}, bf16[1024,256]{1,0:T(8,128)(2,1)S(1)}, u32[]{:S(2)}, u32[]{:S(2)}) collective-permute-start(bf16[1024,256]{1,0:T(8,128)(2,1)S(1)} %collective-permute-done.6.emb_ref), channel_id=1, source_target_pairs={{0,16},{8,24},{16,0},{24,8},{1,17},{9,25},{17,1},{25,9},{2,18},{10... | collective-permute-start | bytes 1572872 | tf_op jit(solution)/shard_map/cond/branch_1_fun/ppermute | solution.py:46
  20.2 1.3 %collective-permute-start.10 = (f32[2,512]{1,0:T(2,128)S(1)}, f32[2,512]{1,0:T(2,128)S(1)}, u32[]{:S(2)}, u32[]{:S(2)}) collective-permute-start(f32[2,512]{1,0:T(2,128)S(1)} %add_divide_fusion), channel_id=1, source_target_pairs={{0,8},{8,0},{16,24},{24,16},{1,9},{9,1},{17,25},{25,17},{2,10},{10... | collective-permute-start | bytes 12296 | tf_op jit(solution)/shard_map/cond/branch_1_fun/ppermute | solution.py:46
  22.2 0.9 %collective-permute-done.10 = f32[2,512]{1,0:T(2,128)S(1)} collective-permute-done((f32[2,512]{1,0:T(2,128)S(1)}, f32[2,512]{1,0:T(2,128)S(1)}, u32[]{:S(2)}, u32[]{:S(2)}) %collective-permute-start.10) | collective-permute-done | bytes 4128 | tf_op jit(solution)/shard_map/cond/branch_1_fun/ppermute | solution.py:46
  23.1 1.1 %collective-permute-start.11 = (f32[4,512]{1,0:T(4,128)S(1)}, f32[4,512]{1,0:T(4,128)S(1)}, u32[]{:S(2)}, u32[]{:S(2)}) collective-permute-start(f32[4,512]{1,0:T(4,128)S(1)} %pad_maximum_fusion.2), channel_id=1, source_target_pairs={{0,16},{8,24},{16,0},{24,8},{1,17},{9,25},{17,1},{25,9},{2,18},{10... | collective-permute-start | bytes 24584 | tf_op jit(solution)/shard_map/cond/branch_1_fun/ppermute | solution.py:46
  25.0 2.3 %collective-permute-done.11 = f32[4,512]{1,0:T(4,128)S(1)} collective-permute-done((f32[4,512]{1,0:T(4,128)S(1)}, f32[4,512]{1,0:T(4,128)S(1)}, u32[]{:S(2)}, u32[]{:S(2)}) %collective-permute-start.11) | collective-permute-done | bytes 8224 | tf_op jit(solution)/shard_map/cond/branch_1_fun/ppermute | solution.py:46
  28.0 2.6 %branch_1_fun.12 = f32[16,512]{1,0:T(8,128)S(1)} custom-call(f32[8,512]{1,0:T(8,128)S(1)} %pad_maximum_fusion.1.weight_ref, f32[2,1024,512]{2,1,0:T(8,128)S(1)} %get-tuple-element.51.own_ref, f32[2,1024,512]{2,1,0:T(8,128)S(1)} %get-tuple-element.56.one_ref, f32[2,1024,512]{2,1,0:T(8,128)S(1)} %get-tuple-element.58.two_ref, ...), custom_call_target="tpu_custom_call" | custom-call | flops 16777216 | bytes 2097152 | tf_op jit(solution)/shard_map/cond/branch_1_fun/pallas_call | solution.py:451
  30.7 1.1 %collective-permute-start.14 = (f32[16,512]{1,0:T(8,128)S(1)}, f32[16,512]{1,0:T(8,128)S(1)}, u32[]{:S(2)}, u32[]{:S(2)}) collective-permute-start(f32[16,512]{1,0:T(8,128)S(1)} %branch_1_fun.12), channel_id=1, source_target_pairs={{0,2},{1,3},{2,0},{3,1},{4,6},{5,7},{6,4},{7,5},{8,10},{9,11},{10,... | collective-permute-start | bytes 98312 | tf_op jit(solution)/shard_map/cond/branch_1_fun/ppermute | solution.py:46
  31.8 1.8 %collective-permute-done.14 = f32[16,512]{1,0:T(8,128)S(1)} collective-permute-done((f32[16,512]{1,0:T(8,128)S(1)}, f32[16,512]{1,0:T(8,128)S(1)}, u32[]{:S(2)}, u32[]{:S(2)}) %collective-permute-start.14) | collective-permute-done | bytes 32800 | tf_op jit(solution)/shard_map/cond/branch_1_fun/ppermute | solution.py:46
  33.6 2.2 %collective-permute-start.15 = (f32[16,512]{1,0:T(8,128)S(1)}, f32[16,512]{1,0:T(8,128)S(1)}, u32[]{:S(2)}, u32[]{:S(2)}) collective-permute-start(f32[16,512]{1,0:T(8,128)S(1)} %add.22), channel_id=1, source_target_pairs={{0,4},{1,5},{2,6},{3,7},{4,0},{5,1},{6,2},{7,3},{8,12},{9,13},{10,... | collective-permute-start | bytes 98312 | tf_op jit(solution)/shard_map/cond/branch_1_fun/ppermute | solution.py:46
  35.7 1.5 %collective-permute-done.15 = f32[16,512]{1,0:T(8,128)S(1)} collective-permute-done((f32[16,512]{1,0:T(8,128)S(1)}, f32[16,512]{1,0:T(8,128)S(1)}, u32[]{:S(2)}, u32[]{:S(2)}) %collective-permute-start.15) | collective-permute-done | bytes 32800 | tf_op jit(solution)/shard_map/cond/branch_1_fun/ppermute | solution.py:46
  37.3 3.6 %branch_1_fun.13 = f32[16,512]{1,0:T(8,128)S(1)} custom-call(f32[8,512]{1,0:T(8,128)S(1)} %get-tuple-element.113.weight_ref, f32[2,1024,512]{2,1,0:T(8,128)S(1)} %get-tuple-element.51.own_ref, f32[2,1024,512]{2,1,0:T(8,128)S(1)} %get-tuple-element.56.one_ref, f32[2,1024,512]{2,1,0:T(8,128)S(1)} %get-tuple-element.58.two_ref, ...), custom_call_target="tpu_custom_call" | custom-call | flops 16777216 | bytes 2097152 | tf_op jit(solution)/shard_map/cond/branch_1_fun/pallas_call | solution.py:451
  40.9 1.9 %collective-permute-start.16 = (f32[16,512]{1,0:T(8,128)S(1)}, f32[16,512]{1,0:T(8,128)S(1)}, u32[]{:S(2)}, u32[]{:S(2)}) collective-permute-start(f32[16,512]{1,0:T(8,128)S(1)} %branch_1_fun.13), channel_id=1, source_target_pairs={{0,2},{1,3},{2,0},{3,1},{4,6},{5,7},{6,4},{7,5},{8,10},{9,11},{10,... | collective-permute-start | bytes 98312 | tf_op jit(solution)/shard_map/cond/branch_1_fun/ppermute | solution.py:46
  42.7 1.3 %collective-permute-done.16 = f32[16,512]{1,0:T(8,128)S(1)} collective-permute-done((f32[16,512]{1,0:T(8,128)S(1)}, f32[16,512]{1,0:T(8,128)S(1)}, u32[]{:S(2)}, u32[]{:S(2)}) %collective-permute-start.16) | collective-permute-done | bytes 32800 | tf_op jit(solution)/shard_map/cond/branch_1_fun/ppermute | solution.py:46
  44.0 1.9 %collective-permute-start.17 = (f32[18,512]{1,0:T(8,128)S(1)}, f32[18,512]{1,0:T(8,128)S(1)}, u32[]{:S(2)}, u32[]{:S(2)}) collective-permute-start(f32[18,512]{1,0:T(8,128)S(1)} %pad_maximum_fusion.mine_ref), channel_id=1, source_target_pairs={{0,4},{1,5},{2,6},{3,7},{4,0},{5,1},{6,2},{7,3},{8,12},{9,13},{10,... | collective-permute-start | bytes 110600 | tf_op jit(solution)/shard_map/cond/branch_1_fun/ppermute | solution.py:46
  46.0 2.0 %collective-permute-done.17.theirs_ref = f32[18,512]{1,0:T(8,128)S(1)} collective-permute-done((f32[18,512]{1,0:T(8,128)S(1)}, f32[18,512]{1,0:T(8,128)S(1)}, u32[]{:S(2)}, u32[]{:S(2)}) %collective-permute-start.17) | collective-permute-done | bytes 36896 | tf_op jit(solution)/shard_map/cond/branch_1_fun/ppermute | solution.py:46
  48.1 1.3 %collective-permute-done.19 = f32[34,512]{1,0:T(8,128)S(1)} collective-permute-done((f32[34,512]{1,0:T(8,128)S(1)}, f32[34,512]{1,0:T(8,128)S(1)}, u32[]{:S(2)}, u32[]{:S(2)}) %collective-permute-start.19) | collective-permute-done | bytes 69664 | tf_op jit(solution)/shard_map/ppermute | solution.py:46
  49.4 6.3 %conditional.3 = (f32[2,512]{1,0:T(2,128)}, bf16[2,512,256]{2,1,0:T(8,128)(2,1)S(1)}) conditional(s32[]{:T(128)} %convert_element_type.4, (bf16[512,256]{1,0:T(8,128)(2,1)S(1)}, bf16[512,256]{1,0:T(8,128)(2,1)S(1)}, bf16[1024,256]{1,0:T(8,128)(2,1)S(1)}, bf16[1024,256]{1,0:T(8,128)(2,1)S(1)}, bf16[1024,256]{1,0:T(8,128)(2,1)S(1)}, ...), branch_computations={%region_3.4_spmd, %region_4.5_spmd} | conditional | flops 1048576 | bytes 1048592 | solution.py:575
  49.4 6.2 %branch_1_fun.15 = (bf16[2,512,256]{2,1,0:T(8,128)(2,1)S(1)}, f32[2,512]{1,0:T(2,128)}) custom-call(bf16[1024,256]{1,0:T(8,128)(2,1)S(1)} %get-tuple-element.74.own_ref, bf16[1024,256]{1,0:T(8,128)(2,1)S(1)} %get-tuple-element.75.one_ref, bf16[1024,256]{1,0:T(8,128)(2,1)S(1)} %get-tuple-element.76.two_ref, ...), custom_call_target="tpu_custom_call" | custom-call | tf_op jit(solution)/shard_map/cond/branch_1_fun/pallas_call | solution.py:546
  56.5 1.2 %collective-permute-done.20.theirs_ref = bf16[2,512,256]{2,1,0:T(8,128)(2,1)S(1)} collective-permute-done((bf16[2,512,256]{2,1,0:T(8,128)(2,1)S(1)}, bf16[2,512,256]{2,1,0:T(8,128)(2,1)S(1)}, u32[]{:S(2)}, u32[]{:S(2)}) %collective-permute-start.20) | collective-permute-done | bytes 524320 | tf_op jit(solution)/shard_map/ppermute | solution.py:46
  57.6 0.8 %shard_map.52 = (bf16[2,512,256]{2,1,0:T(8,128)(2,1)}, bf16[512,256]{1,0:T(8,128)(2,1)}) custom-call(s32[1]{0:T(128)} %bitcast.core_ref, bf16[2,512,256]{2,1,0:T(8,128)(2,1)S(1)} %collective-permute-done.20.theirs_ref, bf16[2,512,256]{2,1,0:T(8,128)(2,1)} %get-tuple-element.107.embed_in_ref, ...), custom_call_target="tpu_custom_call", output_to_operand_aliasing={{0}: (2, {}), {1}: (3, {})} | custom-call | tf_op jit(solution)/shard_map/pallas_call | solution.py:589
  (50 shorter events, 4.9 us)
Async XLA Ops:
  0.6 1.8 %collective-permute-start.18 = (bf16[512,256]{1,0:T(8,128)(2,1)}, bf16[512,256]{1,0:T(8,128)(2,1)S(1)}, u32[]{:S(2)}, u32[]{:S(2)}) collective-permute-start(bf16[512,256]{1,0:T(8,128)(2,1)} %refs_1_.1), channel_id=1, source_target_pairs={{0,1},{1,0},{2,3},{3,2},{4,5},{5,4},{6,7},{7,6},{8,9},{9,8},{10,11... | collective-permute-start | bytes 786440 | tf_op jit(solution)/shard_map/ppermute | solution.py:46
  2.4 0.7 %copy-start.8 = (bf16[512,256]{1,0:T(8,128)(2,1)}, bf16[512,256]{1,0:T(8,128)(2,1)S(1)}, u32[]{:S(2)}) copy-start(bf16[512,256]{1,0:T(8,128)(2,1)S(1)} %collective-permute-done.18.refs_0_) | copy-start | bytes 786436
  3.1 46.2 %copy-start.6 = (bf16[2,512,256]{2,1,0:T(8,128)(2,1)S(1)}, bf16[2,512,256]{2,1,0:T(8,128)(2,1)}, u32[]{:S(2)}) copy-start(bf16[2,512,256]{2,1,0:T(8,128)(2,1)} %param.6) | copy-start | bytes 1572868
  3.1 46.2 %copy-start.7 = (bf16[512,256]{1,0:T(8,128)(2,1)S(1)}, bf16[512,256]{1,0:T(8,128)(2,1)}, u32[]{:S(2)}) copy-start(bf16[512,256]{1,0:T(8,128)(2,1)} %refs_1_.1) | copy-start | bytes 786436
  4.2 3.8 %collective-permute-start.5 = (f32[2,1024]{1,0:T(2,128)S(1)}, f32[2,1024]{1,0:T(2,128)S(1)}, u32[]{:S(2)}, u32[]{:S(2)}) collective-permute-start(f32[2,1024]{1,0:T(2,128)S(1)} %get-tuple-element.49), channel_id=1, source_target_pairs={{0,8},{8,0},{16,24},{24,16},{1,9},{9,1},{17,25},{25,17},{2,10},{10... | collective-permute-start | bytes 24584 | tf_op jit(solution)/shard_map/cond/branch_1_fun/ppermute | solution.py:46
  8.0 8.4 %collective-permute-start.6 = (bf16[1024,256]{1,0:T(8,128)(2,1)S(1)}, bf16[1024,256]{1,0:T(8,128)(2,1)S(1)}, u32[]{:S(2)}, u32[]{:S(2)}) collective-permute-start(bf16[1024,256]{1,0:T(8,128)(2,1)S(1)} %get-tuple-element.57.emb_ref), channel_id=1, source_target_pairs={{0,8},{8,0},{16,24},{24,16},{1,9},{9,1},{17,25},{25,17},{2,10},{10... | collective-permute-start | bytes 1572872 | tf_op jit(solution)/shard_map/cond/branch_1_fun/ppermute | solution.py:46
  9.5 2.8 %collective-permute-start.7 = (f32[2,1024]{1,0:T(2,128)S(1)}, f32[2,1024]{1,0:T(2,128)S(1)}, u32[]{:S(2)}, u32[]{:S(2)}) collective-permute-start(f32[2,1024]{1,0:T(2,128)S(1)} %add.18), channel_id=1, source_target_pairs={{0,16},{8,24},{16,0},{24,8},{1,17},{9,25},{17,1},{25,9},{2,18},{10... | collective-permute-start | bytes 24584 | tf_op jit(solution)/shard_map/cond/branch_1_fun/ppermute | solution.py:46
  12.3 11.9 %collective-permute-start.12 = (bf16[1024,256]{1,0:T(8,128)(2,1)S(1)}, bf16[1024,256]{1,0:T(8,128)(2,1)S(1)}, u32[]{:S(2)}, u32[]{:S(2)}) collective-permute-start(bf16[1024,256]{1,0:T(8,128)(2,1)S(1)} %get-tuple-element.57.emb_ref), channel_id=1, source_target_pairs={{0,16},{8,24},{16,0},{24,8},{1,17},{9,25},{17,1},{25,9},{2,18},{10... | collective-permute-start | bytes 1572872 | tf_op jit(solution)/shard_map/cond/branch_1_fun/ppermute | solution.py:46
  13.9 2.5 %collective-permute-start.8 = (f32[2,512]{1,0:T(2,128)S(1)}, f32[2,512]{1,0:T(2,128)S(1)}, u32[]{:S(2)}, u32[]{:S(2)}) collective-permute-start(f32[2,512]{1,0:T(2,128)S(1)} %multiply_reduce_fusion), channel_id=1, source_target_pairs={{0,2},{1,3},{2,0},{3,1},{4,6},{5,7},{6,4},{7,5},{8,10},{9,11},{10,... | collective-permute-start | bytes 12296 | tf_op jit(solution)/shard_map/cond/branch_1_fun/ppermute | solution.py:46
  16.4 14.2 %copy-start.4 = (bf16[1024,256]{1,0:T(8,128)(2,1)}, bf16[1024,256]{1,0:T(8,128)(2,1)S(1)}, u32[]{:S(2)}) copy-start(bf16[1024,256]{1,0:T(8,128)(2,1)S(1)} %collective-permute-done.6.emb_ref) | copy-start | bytes 1572868 | tf_op jit(solution)/shard_map/cond
  16.4 3.7 %collective-permute-start.9 = (f32[2,512]{1,0:T(2,128)S(1)}, f32[2,512]{1,0:T(2,128)S(1)}, u32[]{:S(2)}, u32[]{:S(2)}) collective-permute-start(f32[2,512]{1,0:T(2,128)S(1)} %add.20), channel_id=1, source_target_pairs={{0,4},{1,5},{2,6},{3,7},{4,0},{5,1},{6,2},{7,3},{8,12},{9,13},{10,... | collective-permute-start | bytes 12296 | tf_op jit(solution)/shard_map/cond/branch_1_fun/ppermute | solution.py:46
  19.1 8.1 %collective-permute-start.13 = (bf16[1024,256]{1,0:T(8,128)(2,1)S(1)}, bf16[1024,256]{1,0:T(8,128)(2,1)S(1)}, u32[]{:S(2)}, u32[]{:S(2)}) collective-permute-start(bf16[1024,256]{1,0:T(8,128)(2,1)S(1)} %collective-permute-done.6.emb_ref), channel_id=1, source_target_pairs={{0,16},{8,24},{16,0},{24,8},{1,17},{9,25},{17,1},{25,9},{2,18},{10... | collective-permute-start | bytes 1572872 | tf_op jit(solution)/shard_map/cond/branch_1_fun/ppermute | solution.py:46
  20.2 2.9 %collective-permute-start.10 = (f32[2,512]{1,0:T(2,128)S(1)}, f32[2,512]{1,0:T(2,128)S(1)}, u32[]{:S(2)}, u32[]{:S(2)}) collective-permute-start(f32[2,512]{1,0:T(2,128)S(1)} %add_divide_fusion), channel_id=1, source_target_pairs={{0,8},{8,0},{16,24},{24,16},{1,9},{9,1},{17,25},{25,17},{2,10},{10... | collective-permute-start | bytes 12296 | tf_op jit(solution)/shard_map/cond/branch_1_fun/ppermute | solution.py:46
  23.1 4.1 %collective-permute-start.11 = (f32[4,512]{1,0:T(4,128)S(1)}, f32[4,512]{1,0:T(4,128)S(1)}, u32[]{:S(2)}, u32[]{:S(2)}) collective-permute-start(f32[4,512]{1,0:T(4,128)S(1)} %pad_maximum_fusion.2), channel_id=1, source_target_pairs={{0,16},{8,24},{16,0},{24,8},{1,17},{9,25},{17,1},{25,9},{2,18},{10... | collective-permute-start | bytes 24584 | tf_op jit(solution)/shard_map/cond/branch_1_fun/ppermute | solution.py:46
  24.2 6.5 %copy-start = (bf16[1024,256]{1,0:T(8,128)(2,1)}, bf16[1024,256]{1,0:T(8,128)(2,1)S(1)}, u32[]{:S(2)}) copy-start(bf16[1024,256]{1,0:T(8,128)(2,1)S(1)} %collective-permute-done.12.emb_ref) | copy-start | bytes 1572868 | tf_op jit(solution)/shard_map/cond
  27.2 3.4 %copy-start.2 = (bf16[1024,256]{1,0:T(8,128)(2,1)}, bf16[1024,256]{1,0:T(8,128)(2,1)S(1)}, u32[]{:S(2)}) copy-start(bf16[1024,256]{1,0:T(8,128)(2,1)S(1)} %collective-permute-done.13.emb_ref) | copy-start | bytes 1572868 | tf_op jit(solution)/shard_map/cond
  30.7 2.9 %collective-permute-start.14 = (f32[16,512]{1,0:T(8,128)S(1)}, f32[16,512]{1,0:T(8,128)S(1)}, u32[]{:S(2)}, u32[]{:S(2)}) collective-permute-start(f32[16,512]{1,0:T(8,128)S(1)} %branch_1_fun.12), channel_id=1, source_target_pairs={{0,2},{1,3},{2,0},{3,1},{4,6},{5,7},{6,4},{7,5},{8,10},{9,11},{10,... | collective-permute-start | bytes 98312 | tf_op jit(solution)/shard_map/cond/branch_1_fun/ppermute | solution.py:46
  33.6 3.7 %collective-permute-start.15 = (f32[16,512]{1,0:T(8,128)S(1)}, f32[16,512]{1,0:T(8,128)S(1)}, u32[]{:S(2)}, u32[]{:S(2)}) collective-permute-start(f32[16,512]{1,0:T(8,128)S(1)} %add.22), channel_id=1, source_target_pairs={{0,4},{1,5},{2,6},{3,7},{4,0},{5,1},{6,2},{7,3},{8,12},{9,13},{10,... | collective-permute-start | bytes 98312 | tf_op jit(solution)/shard_map/cond/branch_1_fun/ppermute | solution.py:46
  37.2 10.7 %copy-start.1 = (bf16[1024,256]{1,0:T(8,128)(2,1)S(1)}, bf16[1024,256]{1,0:T(8,128)(2,1)}, u32[]{:S(2)}) copy-start(bf16[1024,256]{1,0:T(8,128)(2,1)} %copy-done) | copy-start | bytes 1572868 | tf_op jit(solution)/shard_map/cond
  37.2 10.7 %copy-start.3 = (bf16[1024,256]{1,0:T(8,128)(2,1)S(1)}, bf16[1024,256]{1,0:T(8,128)(2,1)}, u32[]{:S(2)}) copy-start(bf16[1024,256]{1,0:T(8,128)(2,1)} %copy-done.2) | copy-start | bytes 1572868 | tf_op jit(solution)/shard_map/cond
  37.3 10.7 %copy-start.5 = (bf16[1024,256]{1,0:T(8,128)(2,1)S(1)}, bf16[1024,256]{1,0:T(8,128)(2,1)}, u32[]{:S(2)}) copy-start(bf16[1024,256]{1,0:T(8,128)(2,1)} %copy-done.4) | copy-start | bytes 1572868 | tf_op jit(solution)/shard_map/cond
  40.9 3.2 %collective-permute-start.16 = (f32[16,512]{1,0:T(8,128)S(1)}, f32[16,512]{1,0:T(8,128)S(1)}, u32[]{:S(2)}, u32[]{:S(2)}) collective-permute-start(f32[16,512]{1,0:T(8,128)S(1)} %branch_1_fun.13), channel_id=1, source_target_pairs={{0,2},{1,3},{2,0},{3,1},{4,6},{5,7},{6,4},{7,5},{8,10},{9,11},{10,... | collective-permute-start | bytes 98312 | tf_op jit(solution)/shard_map/cond/branch_1_fun/ppermute | solution.py:46
  44.0 3.9 %collective-permute-start.17 = (f32[18,512]{1,0:T(8,128)S(1)}, f32[18,512]{1,0:T(8,128)S(1)}, u32[]{:S(2)}, u32[]{:S(2)}) collective-permute-start(f32[18,512]{1,0:T(8,128)S(1)} %pad_maximum_fusion.mine_ref), channel_id=1, source_target_pairs={{0,4},{1,5},{2,6},{3,7},{4,0},{5,1},{6,2},{7,3},{8,12},{9,13},{10,... | collective-permute-start | bytes 110600 | tf_op jit(solution)/shard_map/cond/branch_1_fun/ppermute | solution.py:46
  48.0 1.3 %collective-permute-start.19 = (f32[34,512]{1,0:T(8,128)S(1)}, f32[34,512]{1,0:T(8,128)S(1)}, u32[]{:S(2)}, u32[]{:S(2)}) collective-permute-start(f32[34,512]{1,0:T(8,128)S(1)} %get-tuple-element.105), channel_id=1, source_target_pairs={{0,1},{1,0},{2,3},{3,2},{4,5},{5,4},{6,7},{7,6},{8,9},{9,8},{10,11... | collective-permute-start | bytes 208904 | tf_op jit(solution)/shard_map/ppermute | solution.py:46
  55.6 2.0 %collective-permute-start.20 = (bf16[2,512,256]{2,1,0:T(8,128)(2,1)S(1)}, bf16[2,512,256]{2,1,0:T(8,128)(2,1)S(1)}, u32[]{:S(2)}, u32[]{:S(2)}) collective-permute-start(bf16[2,512,256]{2,1,0:T(8,128)(2,1)S(1)} %get-tuple-element.106.mine_ref), channel_id=1, source_target_pairs={{0,1},{1,0},{2,3},{3,2},{4,5},{5,4},{6,7},{7,6},{8,9},{9,8},{10,11... | collective-permute-start | bytes 1572872 | tf_op jit(solution)/shard_map/ppermute | solution.py:46

commit v2 on v1

--- a/solution.py
+++ b/solution.py
@@ -19,6 +19,7 @@
 VMEM = pl.BlockSpec(memory_space=pltpu.VMEM)
 SMEM = pl.BlockSpec(memory_space=pltpu.SMEM)
 ANY = pl.BlockSpec(memory_space=pl.ANY)
+HBM = pl.BlockSpec(memory_space=pltpu.HBM)
 PARAMS = pltpu.CompilerParams(vmem_limit_bytes=24 << 20)
 SMALL = pltpu.CompilerParams(vmem_limit_bytes=8 << 20)
 
@@ -165,7 +166,7 @@
         out_ref[...] = normalize_rows(raw_ref[...])[0].astype(jnp.bfloat16)
 
 
-def score_kernel(tile, emb_ref, proto_ref, sink_ref, soft_ref, *column_refs):
+def score_kernel(tile, emb_ref, proto_ref, sink_ref, *sum_refs):
     rows = emb_ref.shape[0] // 2
     for view in range(2):
         emb = emb_ref[view * rows:(view + 1) * rows]
@@ -174,11 +175,29 @@
             soft = jnp.exp2(dot_t(proto_ref[at:at + tile], emb) * (LOG2E / TEMPER))
             sink = soft * soft
             sink_ref[view, at:at + tile] = sink
-            total = total + jnp.sum(soft.reshape(-1, 8, rows), axis=0)
-            for column_ref in column_refs:
+            if sum_refs:
+                total = total + jnp.sum(soft.reshape(-1, 8, rows), axis=0)
                 lanes = sum(sink[:, lane:lane + 128] for lane in range(0, rows, 128))
-                column_ref[view:view + 1, at:at + tile] = jnp.sum(lanes.T, axis=0, keepdims=True)
-        soft_ref[view:view + 1] = jnp.sum(total, axis=0, keepdims=True)
+                sum_refs[1][view:view + 1, at:at + tile] = jnp.sum(lanes.T, axis=0, keepdims=True)
+        if sum_refs:
+            sum_refs[0][view:view + 1] = jnp.sum(total, axis=0, keepdims=True)
+
+
+def lane_sums(weight_ref, block, view, at, part):
+    values = block[view, part]
+    tile, rows = values.shape
+    weight = jnp.broadcast_to(weight_ref[2 * at + view:2 * at + view + 1], (8, rows))
+    scaled = (values.reshape(-1, 8, rows) * weight).reshape(tile, rows)
+    return sum(scaled[:, lane:lane + 128] for lane in range(0, rows, 128))
+
+
+def column_kernel(tile, weight_ref, own_ref, one_ref, two_ref, out_ref):
+    for view in range(2):
+        for first in range(0, own_ref.shape[1], tile):
+            part = slice(first, first + tile)
+            own, one, two = (lane_sums(weight_ref, block, view, at, part) for at, block in enumerate((own_ref, one_ref, two_ref)))
+            out_ref[0, view, part] = own + one
+            out_ref[1, view, part] = two
 
 
 def sweep_kernel(last, tile, weight_ref, own_ref, one_ref, two_ref, three_ref, *refs):
@@ -189,15 +208,13 @@
         cross = [jnp.zeros((8, rows), jnp.float32)] * 2
         out_ref[...] = jnp.zeros(out_ref.shape, jnp.float32)
     for view in range(2):
-        weight = [jnp.broadcast_to(weight_ref[2 * at + view:2 * at + view + 1], (8, rows)) for at in range(4)]
         totals = [jnp.zeros((8, rows), jnp.float32)] * 4
         for first in range(0, count, tile):
             part = slice(first, first + tile)
-            lanes = []
-            for at in range(4):
-                scaled = blocks[at][view, part].reshape(-1, 8, rows) * weight[at]
-                scaled = scaled.reshape(tile, rows)
-                lanes.append(sum(scaled[:, lane:lane + 128] for lane in range(0, rows, 128)))
+            if last:
+                lanes = [lane_sums(weight_ref, blocks[at], view, at, part) for at in range(4)]
+            else:
+                lanes = [refs[0][0, view, part], refs[0][1, view, part] + lane_sums(weight_ref, three_ref, view, 3, part)]
             scale = 1.0 / jnp.sum(tree_sum(lanes), axis=1, keepdims=True)
             for at in range(4):
                 scaled = blocks[at][view, part] * scale
@@ -213,9 +230,6 @@
     if last:
         for view in range(2):
             out_ref[8 + view:9 + view] = jnp.sum(cross[view], axis=0, keepdims=True)
-    else:
-        for at in range(4):
-            out_ref[8 + 2 * at:10 + 2 * at] = refs[at][...]
 
 
 def found_kernel(mine_ref, theirs_ref, soft_ref, out_ref):
@@ -293,41 +307,44 @@
     loss_ref[...] = found_ref[:2]
     blocks = (own_ref, one_ref, two_ref, three_ref)
     rows = own_ref.shape[0] // 2
-    tiles = proto_ref.shape[0] // tile
+    halves = rows // tile
     for view in range(2):
         for first in range(0, proto_ref.shape[0], rows):
             col_ref[view, first:first + rows] = column(scale_row(found_ref, 0, view, first // rows))
 
-    def score(step, at):
-        first = step % tiles * tile
-        proto = proto_ref[first:first + tile]
-        work_ref[step % 2, :, at:at + 256] = dot_t(proto, blocks[step // tiles][at:at + 256])
+    def emb(step, view):
+        first = view * rows + step % halves * tile
+        return blocks[step // halves][first:first + tile]
+
+    def score(step, view):
+        work_ref[step % 2, :, view * tile:(view + 1) * tile] = dot_t(proto_ref[...], emb(step, view))
 
     def gradient(step):
-        first = step % tiles * tile
-        acc_ref[step // tiles, first:first + tile] = dot_n(slope_ref[step % 2], blocks[step // tiles][...])
+        grad = dot_n(slope_ref[step % 2], jnp.concatenate([emb(step, 0), emb(step, 1)]))
+        if step % halves:
+            grad = grad + acc_ref[step // halves]
+        acc_ref[step // halves] = grad
 
     def products_of(ahead, behind):
-        scores = [] if ahead is None else [functools.partial(score, ahead, at) for at in range(0, 2 * rows, 256)]
+        scores = [] if ahead is None else [functools.partial(score, ahead, view) for view in range(2)]
         grads = [] if behind is None else [functools.partial(gradient, behind)]
-        half = len(scores) // 2
-        return scores[:half] + grads + scores[half:]
+        return scores[:1] + grads + scores[1:]
 
     def factors_of(step):
-        block = step // tiles
-        soft = [jnp.broadcast_to(soft_row(found_ref, block, view), (16, rows)) for view in range(2)]
-        weight = [jnp.broadcast_to(weight_row(found_ref, block, view), (16, rows)) for view in range(2)]
-        base = step % tiles * tile
+        block, first = step // halves, step % halves * tile
+        part = slice(first, first + tile)
+        soft = [jnp.broadcast_to(soft_row(found_ref, block, view)[:, part], (16, tile)) for view in range(2)]
+        weight = [jnp.broadcast_to(weight_row(found_ref, block, view)[:, part], (16, tile)) for view in range(2)]
 
         def other_of(view, part, sink):
-            return sink * widen(col_ref[view, base + part.start:base + part.stop], rows) * weight[view]
+            return sink * widen(col_ref[view, part], tile) * weight[view]
 
         return (lambda view, part, value: value * soft[view]), other_of
 
     def place(view, part):
-        return part, slice(view * rows, (view + 1) * rows)
-
-    pipeline(len(blocks) * tiles, products_of, factors_of, place, work_ref, slope_ref, tile)
+        return part, slice(view * tile, (view + 1) * tile)
+
+    pipeline(len(blocks) * halves, products_of, factors_of, place, work_ref, slope_ref, proto_ref.shape[0])
     half = raw_ref.shape[0]
     for at in range(2):
         part = slice(at * half, (at + 1) * half)
@@ -430,10 +447,10 @@
     return value
 
 
-def scored(flat, proto_b, columns):
+def scored(flat, proto_b, sums):
     rows, width = flat.shape
     count = proto_b.shape[0]
-    shapes = [(2, count, rows // 2), (2, rows // 2)] + [(2, count)] * columns
+    shapes = [(2, count, rows // 2)] + [(2, rows // 2), (2, count)] * sums
     return pl.pallas_call(
         functools.partial(score_kernel, min(count, 256)),
         out_shape=[jax.ShapeDtypeStruct(shape, jnp.float32) for shape in shapes],
@@ -446,16 +463,28 @@
     )(flat, proto_b)
 
 
-def swept(last, weights, sinks, softs):
+def swept(weights, sinks, *sums):
     _, count, rows = sinks[0].shape
     return pl.pallas_call(
-        functools.partial(sweep_kernel, last, 128),
-        out_shape=jax.ShapeDtypeStruct((16, rows), jnp.float32),
-        in_specs=[VMEM] * (5 + len(softs)),
+        functools.partial(sweep_kernel, not sums, 128),
+        out_shape=jax.ShapeDtypeStruct((8 if sums else 16, rows), jnp.float32),
+        in_specs=[VMEM] * (5 + len(sums)),
         out_specs=VMEM,
         compiler_params=SMALL,
         cost_estimate=pl.CostEstimate(flops=32 * rows * count, bytes_accessed=4 * rows * count, transcendentals=0),
-    )(weights, *sinks, *softs)
+    )(weights, *sinks, *sums)
+
+
+def first_sums(weights, sinks):
+    _, count, rows = sinks[0].shape
+    return pl.pallas_call(
+        functools.partial(column_kernel, 128),
+        out_shape=jax.ShapeDtypeStruct((2, 2, count, 128), jnp.float32),
+        in_specs=[VMEM] * 4,
+        out_specs=VMEM,
+        compiler_params=SMALL,
+        cost_estimate=pl.CostEstimate(flops=12 * rows * count, bytes_accessed=4 * rows * count, transcendentals=0),
+    )(weights, *sinks[:3])
 
 
 def after(value, first):
@@ -468,26 +497,21 @@
     sums = sums + swap(sums, "samp", samp, 1)
     block, sums = after(flat, sums)
     one = swap(block, "samp", samp, 1)
+    two = swap(block, "samp", samp, 2)
     sums = sums + swap(sums, "samp", samp, 2)
-    block, sums = after(flat, sums)
-    two = swap(block, "samp", samp, 2)
-    sums = jnp.sum(sink * (1.0 / sums)[:, :, None], axis=1)
+    sums = jnp.concatenate([jnp.sum(sink * (1.0 / sums)[:, :, None], axis=1), soft])
     sums = sums + swap(sums, "proto", proto, 2)
+    sums = sums + swap(sums, "proto", proto, 4)
     one, sums = after(one, sums)
     three = swap(one, "samp", samp, 2)
-    weights = 1.0 / (sums + swap(sums, "proto", proto, 4))
-
-    sinks, softs = [sink], [soft]
-    for block in (one, two, three):
-        sink, soft = scored(block, proto_b, False)
-        sinks.append(sink)
-        softs.append(soft)
-    for mask in chip_masks(samp, 1):
-        weights = jnp.concatenate([weights, swap(weights, "samp", samp, mask)])
-    totals = chip_sum(swept(False, weights, sinks, softs), "proto", proto, 2)
-    soft_total = totals[8:]
-
-    totals = swept(True, 1.0 / totals[:8], sinks, [])
+
+    sinks = [sink] + [scored(block, proto_b, False)[0] for block in (one, two, three)]
+    both = jnp.concatenate([sums, swap(sums, "samp", samp, 2)])
+    sums = jnp.concatenate([both, swap(both, "samp", samp, 1)])
+    weights = 1.0 / jnp.concatenate([sums[at:at + 2] for at in (0, 8, 4, 12)])
+    soft_total = jnp.concatenate([sums[at:at + 2] for at in (2, 10, 6, 14)])
+    totals = chip_sum(swept(weights, sinks, first_sums(weights, sinks)), "proto", proto, 2)
+    totals = swept(1.0 / totals, sinks)
     got = swap(totals, "proto", proto, 2)
     totals = jnp.concatenate([totals[:10] + got[:10], totals[10:14], got[10:14]])
     found = pl.pallas_call(
@@ -536,6 +560,7 @@
     raw_other = swap(prototypes, "proto", proto, 1)
     flat, own = unit_rows(embeddings.reshape(2 * per_view, width), prototypes)
     other, = unit_rows(raw_other)
+    raw_other = swap(after(prototypes, own)[0], "proto", proto, 1)
     found, *gathered = lax.cond(
         lead, functools.partial(sweeps, samp, proto), functools.partial(gathers, proto), flat, own, other
     )
@@ -544,12 +569,12 @@
 
     def grads(kernel, operands, raws, columns, rows, lanes):
         return pl.pallas_call(
-            functools.partial(kernel, rows if kernel is proto_grad_kernel else lanes),
+            functools.partial(kernel, lanes // 2 if kernel is proto_grad_kernel else lanes),
             out_shape=(
                 jax.ShapeDtypeStruct((2, per_view, width), jnp.bfloat16),
                 jax.ShapeDtypeStruct((2, per_view), jnp.float32),
             ),
-            in_specs=[VMEM] * len(operands) + [ANY] * len(raws) + [VMEM],
+            in_specs=[VMEM] * len(operands) + [HBM] * len(raws) + [VMEM],
             out_specs=(VMEM,) * 2,
             scratch_shapes=[
                 pltpu.VMEM(columns, jnp.float32),
@@ -565,7 +590,7 @@
     def proto_grads(flat, own, other, *gathered):
         proto_b = jnp.concatenate([other, own])
         operands = (flat, *gathered, proto_b)
-        return grads(proto_grad_kernel, operands, (raw_other, prototypes), (2, 2 * count, 128), 2 * count, 2 * per_view)
+        return grads(proto_grad_kernel, operands, (raw_other, prototypes), (2, 2 * count, 128), 2 * count, per_view)
 
     def emb_grads(flat, own, other, *gathered):
         proto_b = jnp.concatenate([own, other])

time: 58.8 us -> 57 us (0.969)
  waiting for transfers between devices: 16.5 us -> 15.9 us
    ppermute x16 -> x17, waiting for transfers between devices: 16.5 us -> 15.9 us  [swap(): return lax.ppermute(value, axis, [(i, i ^ mask) for i in range(size)])]
    pallas_call x3 -> x4, Pallas kernels: 12.5 us -> 12 us  [the longest x1 5.88 us: grads(): pl.pallas_call(functools.partial(kernel, lanes // 2 if kernel is proto_gr...]
    ppermute x16 -> x17, starting transfers between devices: 21.1 us -> 20.7 us  [swap(): return lax.ppermute(value, axis, [(i, i ^ mask) for i in range(size)])]
  transfers between devices with their start and end apart: 16 -> 17, of which waited for: 12 -> 11; matrix products, arithmetic and copies ran while one was open for 1% -> 1% of each run, Pallas kernels for 6% -> 21%
where the time goes in v2:
time: 57 us; the launch traced here: 56.7 us
  starting transfers between devices  20.7 us (36%)
  Pallas kernels  18.4 us (32%)
  waiting for transfers between devices  15.9 us (28%)
  between operations  0.86 us (2%)
    ppermute x17, starting transfers between devices, swap(): return lax.ppermute(value, axis, [(i, i ^ mask) for i in range(size)])  20.7 us
    ppermute x17, waiting for transfers between devices, swap(): return lax.ppermute(value, axis, [(i, i ^ mask) for i in range(size)])  15.9 us
    pallas_call x1, Pallas kernels, grads(): pl.pallas_call(functools.partial(kernel, lanes // 2 if kernel is proto_gr...  5.88 us
    pallas_call x2, Pallas kernels, swept(): pl.pallas_call(functools.partial(sweep_kernel, not sums, 128), out_shape=...  5.38 us
    pallas_call x4, Pallas kernels, scored(): pl.pallas_call(functools.partial(score_kernel, min(count, 256)), out_shap...  3.25 us
    pallas_call x2, Pallas kernels, unit_rows(): pl.pallas_call(unit_kernel, out_shape=[jax.ShapeDtypeStruct(raw.shape, jn...  1.55 us
  transfers between devices with their start and end apart: 17, of which 11 were waited for; matrix products, arithmetic and copies ran while one was open for 1% of the time, Pallas kernels for 21%

profile of v2, /device:TPU:1, one launch (start us, length us, event | category | flops | bytes accessed | tf_op | source)
XLA Modules:
  0.0 56.7 jit_solution(8424347220509660264)
XLA Ops:
  0.8 1.4 %shard_map.49 = (bf16[1024,256]{1,0:T(8,128)(2,1)S(1)}, bf16[512,256]{1,0:T(8,128)(2,1)S(1)}) custom-call(bf16[1024,256]{1,0:T(8,128)(2,1)} %bitcast.2, bf16[512,256]{1,0:T(8,128)(2,1)} %refs_1_.1), custom_call_target="tpu_custom_call" | custom-call | tf_op jit(solution)/shard_map/pallas_call | solution.py:546
  2.9 43.6 %conditional.2 = (f32[34,512]{1,0:T(8,128)S(1)}, bf16[1024,256]{1,0:T(8,128)(2,1)S(1)}, bf16[1024,256]{1,0:T(8,128)(2,1)S(1)}, bf16[1024,256]{1,0:T(8,128)(2,1)S(1)}) conditional(s32[]{:T(128)} %convert_element_type.4, (bf16[512,256]{1,0:T(8,128)(2,1)S(1)}, bf16[512,256]{1,0:T(8,128)(2,1)S(1)}) %tuple.27, (bf16[512,256]{1,0:T(8,128)(2,1)S(1)}, ...), branch_computations={%region_0.1_spmd, %region_1.3_spmd} | conditional | flops 2189508608 | bytes 35799760 | solution.py:564
  2.9 1.0 %branch_1_fun.9 = (f32[2,1024,512]{2,1,0:T(8,128)S(1)}, f32[2,512]{1,0:T(2,128)S(1)}, f32[2,1024]{1,0:T(2,128)S(1)}) custom-call(bf16[1024,256]{1,0:T(8,128)(2,1)S(1)} %get-tuple-element.50.emb_ref, bf16[1024,256]{1,0:T(8,128)(2,1)S(1)} %constant_dynamic-update-slice_fusion.2.proto_ref), custom_call_target="tpu_custom_call" | custom-call | flops 536870912 | bytes 1048576 | tf_op jit(solution)/shard_map/cond/branch_1_fun/pallas_call | solution.py:454
  4.0 2.3 %collective-permute-start.5 = (f32[2,1024]{1,0:T(2,128)S(1)}, f32[2,1024]{1,0:T(2,128)S(1)}, u32[]{:S(2)}, u32[]{:S(2)}) collective-permute-start(f32[2,1024]{1,0:T(2,128)S(1)} %get-tuple-element.49), channel_id=1, source_target_pairs={{0,8},{8,0},{16,24},{24,16},{1,9},{9,1},{17,25},{25,17},{2,10},{10... | collective-permute-start | bytes 24584 | tf_op jit(solution)/shard_map/cond/branch_1_fun/ppermute | solution.py:47
  6.3 1.3 %collective-permute-done.5 = f32[2,1024]{1,0:T(2,128)S(1)} collective-permute-done((f32[2,1024]{1,0:T(2,128)S(1)}, f32[2,1024]{1,0:T(2,128)S(1)}, u32[]{:S(2)}, u32[]{:S(2)}) %collective-permute-start.5) | collective-permute-done | bytes 8224 | tf_op jit(solution)/shard_map/cond/branch_1_fun/ppermute | solution.py:47
  7.6 1.5 %collective-permute-start.7 = (f32[2,1024]{1,0:T(2,128)S(1)}, f32[2,1024]{1,0:T(2,128)S(1)}, u32[]{:S(2)}, u32[]{:S(2)}) collective-permute-start(f32[2,1024]{1,0:T(2,128)S(1)} %add.18), channel_id=1, source_target_pairs={{0,16},{8,24},{16,0},{24,8},{1,17},{9,25},{17,1},{25,9},{2,18},{10... | collective-permute-start | bytes 24584 | tf_op jit(solution)/shard_map/cond/branch_1_fun/ppermute | solution.py:47
  9.1 1.2 %collective-permute-start.6 = (bf16[1024,256]{1,0:T(8,128)(2,1)S(1)}, bf16[1024,256]{1,0:T(8,128)(2,1)S(1)}, u32[]{:S(2)}, u32[]{:S(2)}) collective-permute-start(bf16[1024,256]{1,0:T(8,128)(2,1)S(1)} %get-tuple-element.50.emb_ref), channel_id=1, source_target_pairs={{0,8},{8,0},{16,24},{24,16},{1,9},{9,1},{17,25},{25,17},{2,10},{10... | collective-permute-start | bytes 1572872 | tf_op jit(solution)/shard_map/cond/branch_1_fun/ppermute | solution.py:47
  10.9 1.5 %collective-permute-start.8 = (f32[4,512]{1,0:T(4,128)S(1)}, f32[4,512]{1,0:T(4,128)S(1)}, u32[]{:S(2)}, u32[]{:S(2)}) collective-permute-start(f32[4,512]{1,0:T(4,128)S(1)} %pad_maximum_fusion.3), channel_id=1, source_target_pairs={{0,2},{1,3},{2,0},{3,1},{4,6},{5,7},{6,4},{7,5},{8,10},{9,11},{10,... | collective-permute-start | bytes 24584 | tf_op jit(solution)/shard_map/cond/branch_1_fun/ppermute | solution.py:47
  12.4 1.1 %collective-permute-done.8 = f32[4,512]{1,0:T(4,128)S(1)} collective-permute-done((f32[4,512]{1,0:T(4,128)S(1)}, f32[4,512]{1,0:T(4,128)S(1)}, u32[]{:S(2)}, u32[]{:S(2)}) %collective-permute-start.8) | collective-permute-done | bytes 8224 | tf_op jit(solution)/shard_map/cond/branch_1_fun/ppermute | solution.py:47
  13.5 2.8 %collective-permute-start.9 = (f32[4,512]{1,0:T(4,128)S(1)}, f32[4,512]{1,0:T(4,128)S(1)}, u32[]{:S(2)}, u32[]{:S(2)}) collective-permute-start(f32[4,512]{1,0:T(4,128)S(1)} %fusion), channel_id=1, source_target_pairs={{0,4},{1,5},{2,6},{3,7},{4,0},{5,1},{6,2},{7,3},{8,12},{9,13},{10,... | collective-permute-start | bytes 24584 | tf_op jit(solution)/shard_map/cond/branch_1_fun/ppermute | solution.py:47
  16.3 1.0 %collective-permute-done.9 = f32[4,512]{1,0:T(4,128)S(1)} collective-permute-done((f32[4,512]{1,0:T(4,128)S(1)}, f32[4,512]{1,0:T(4,128)S(1)}, u32[]{:S(2)}, u32[]{:S(2)}) %collective-permute-start.9) | collective-permute-done | bytes 8224 | tf_op jit(solution)/shard_map/cond/branch_1_fun/ppermute | solution.py:47
  17.4 1.3 %collective-permute-start.10 = (f32[4,512]{1,0:T(4,128)S(1)}, f32[4,512]{1,0:T(4,128)S(1)}, u32[]{:S(2)}, u32[]{:S(2)}) collective-permute-start(f32[4,512]{1,0:T(4,128)S(1)} %add.21), channel_id=1, source_target_pairs={{0,16},{8,24},{16,0},{24,8},{1,17},{9,25},{17,1},{25,9},{2,18},{10... | collective-permute-start | bytes 24584 | tf_op jit(solution)/shard_map/cond/branch_1_fun/ppermute | solution.py:47
  19.7 0.7 %branch_1_fun.11.two_ref = f32[2,1024,512]{2,1,0:T(8,128)S(1)} custom-call(bf16[1024,256]{1,0:T(8,128)(2,1)S(1)} %collective-permute-done.12.emb_ref, bf16[1024,256]{1,0:T(8,128)(2,1)S(1)} %constant_dynamic-update-slice_fusion.2.proto_ref), custom_call_target="tpu_custom_call" | custom-call | flops 536870912 | bytes 1048576 | tf_op jit(solution)/shard_map/cond/branch_1_fun/pallas_call | solution.py:454
  20.5 1.3 %collective-permute-start.11 = (f32[8,512]{1,0:T(8,128)S(1)}, f32[8,512]{1,0:T(8,128)S(1)}, u32[]{:S(2)}, u32[]{:S(2)}) collective-permute-start(f32[8,512]{1,0:T(8,128)S(1)} %pad_maximum_fusion.1), channel_id=1, source_target_pairs={{0,8},{8,0},{16,24},{24,16},{1,9},{9,1},{17,25},{25,17},{2,10},{10... | collective-permute-start | bytes 49160 | tf_op jit(solution)/shard_map/cond/branch_1_fun/ppermute | solution.py:47
  21.7 1.8 %collective-permute-done.11 = f32[8,512]{1,0:T(8,128)S(1)} collective-permute-done((f32[8,512]{1,0:T(8,128)S(1)}, f32[8,512]{1,0:T(8,128)S(1)}, u32[]{:S(2)}, u32[]{:S(2)}) %collective-permute-start.11) | collective-permute-done | bytes 16416 | tf_op jit(solution)/shard_map/cond/branch_1_fun/ppermute | solution.py:47
  23.5 0.7 %branch_1_fun.13.refs_0_ = f32[2,2,1024,128]{3,2,1,0:T(8,128)S(1)} custom-call(f32[8,512]{1,0:T(8,128)S(1)} %maximum_divide_fusion.weight_ref, f32[2,1024,512]{2,1,0:T(8,128)S(1)} %get-tuple-element.51.own_ref, f32[2,1024,512]{2,1,0:T(8,128)S(1)} %branch_1_fun.10.one_ref, f32[2,1024,512]{2,1,0:T(8,128)S(1)} %branch_1_fun.11.two_ref), custom_call_target="tpu_custom_call" | custom-call | flops 6291456 | bytes 2097152 | tf_op jit(solution)/shard_map/cond/branch_1_fun/pallas_call | solution.py:480
  24.3 2.4 %collective-permute-done.13.emb_ref = bf16[1024,256]{1,0:T(8,128)(2,1)S(1)} collective-permute-done((bf16[1024,256]{1,0:T(8,128)(2,1)S(1)}, bf16[1024,256]{1,0:T(8,128)(2,1)S(1)}, u32[]{:S(2)}, u32[]{:S(2)}) %collective-permute-start.13) | collective-permute-done | bytes 524320 | tf_op jit(solution)/shard_map/cond/branch_1_fun/ppermute | solution.py:47
  27.4 1.7 %branch_1_fun.14 = f32[8,512]{1,0:T(8,128)S(1)} custom-call(f32[8,512]{1,0:T(8,128)S(1)} %maximum_divide_fusion.weight_ref, f32[2,1024,512]{2,1,0:T(8,128)S(1)} %get-tuple-element.51.own_ref, f32[2,1024,512]{2,1,0:T(8,128)S(1)} %branch_1_fun.10.one_ref, f32[2,1024,512]{2,1,0:T(8,128)S(1)} %branch_1_fun.11.two_ref, ...), custom_call_target="tpu_custom_call" | custom-call | flops 16777216 | bytes 2097152 | tf_op jit(solution)/shard_map/cond/branch_1_fun/pallas_call | solution.py:468
  29.2 1.4 %collective-permute-start.14 = (f32[8,512]{1,0:T(8,128)S(1)}, f32[8,512]{1,0:T(8,128)S(1)}, u32[]{:S(2)}, u32[]{:S(2)}) collective-permute-start(f32[8,512]{1,0:T(8,128)S(1)} %branch_1_fun.14), channel_id=1, source_target_pairs={{0,2},{1,3},{2,0},{3,1},{4,6},{5,7},{6,4},{7,5},{8,10},{9,11},{10,... | collective-permute-start | bytes 49160 | tf_op jit(solution)/shard_map/cond/branch_1_fun/ppermute | solution.py:47
  30.6 1.9 %collective-permute-done.14 = f32[8,512]{1,0:T(8,128)S(1)} collective-permute-done((f32[8,512]{1,0:T(8,128)S(1)}, f32[8,512]{1,0:T(8,128)S(1)}, u32[]{:S(2)}, u32[]{:S(2)}) %collective-permute-start.14) | collective-permute-done | bytes 16416 | tf_op jit(solution)/shard_map/cond/branch_1_fun/ppermute | solution.py:47
  32.5 2.4 %collective-permute-start.15 = (f32[8,512]{1,0:T(8,128)S(1)}, f32[8,512]{1,0:T(8,128)S(1)}, u32[]{:S(2)}, u32[]{:S(2)}) collective-permute-start(f32[8,512]{1,0:T(8,128)S(1)} %add.22), channel_id=1, source_target_pairs={{0,4},{1,5},{2,6},{3,7},{4,0},{5,1},{6,2},{7,3},{8,12},{9,13},{10,... | collective-permute-start | bytes 49160 | tf_op jit(solution)/shard_map/cond/branch_1_fun/ppermute | solution.py:47
  34.9 1.1 %collective-permute-done.15 = f32[8,512]{1,0:T(8,128)S(1)} collective-permute-done((f32[8,512]{1,0:T(8,128)S(1)}, f32[8,512]{1,0:T(8,128)S(1)}, u32[]{:S(2)}, u32[]{:S(2)}) %collective-permute-start.15) | collective-permute-done | bytes 16416 | tf_op jit(solution)/shard_map/cond/branch_1_fun/ppermute | solution.py:47
  36.0 3.6 %branch_1_fun.15 = f32[16,512]{1,0:T(8,128)S(1)} custom-call(f32[8,512]{1,0:T(8,128)S(1)} %add_divide_fusion.weight_ref, f32[2,1024,512]{2,1,0:T(8,128)S(1)} %get-tuple-element.51.own_ref, f32[2,1024,512]{2,1,0:T(8,128)S(1)} %branch_1_fun.10.one_ref, f32[2,1024,512]{2,1,0:T(8,128)S(1)} %branch_1_fun.11.two_ref, f32[2,1024,512]{2,1,0:T(8,128)S(1)} %branch_1_fun.12.three_ref), custom_call_target="tpu_custom_call" | custom-call | flops 16777216 | bytes 2097152 | tf_op jit(solution)/shard_map/cond/branch_1_fun/pallas_call | solution.py:468
  39.7 1.4 %collective-permute-start.16 = (f32[16,512]{1,0:T(8,128)S(1)}, f32[16,512]{1,0:T(8,128)S(1)}, u32[]{:S(2)}, u32[]{:S(2)}) collective-permute-start(f32[16,512]{1,0:T(8,128)S(1)} %branch_1_fun.15), channel_id=1, source_target_pairs={{0,2},{1,3},{2,0},{3,1},{4,6},{5,7},{6,4},{7,5},{8,10},{9,11},{10,... | collective-permute-start | bytes 98312 | tf_op jit(solution)/shard_map/cond/branch_1_fun/ppermute | solution.py:47
  41.1 1.4 %collective-permute-done.16 = f32[16,512]{1,0:T(8,128)S(1)} collective-permute-done((f32[16,512]{1,0:T(8,128)S(1)}, f32[16,512]{1,0:T(8,128)S(1)}, u32[]{:S(2)}, u32[]{:S(2)}) %collective-permute-start.16) | collective-permute-done | bytes 32800 | tf_op jit(solution)/shard_map/cond/branch_1_fun/ppermute | solution.py:47
  42.5 2.4 %collective-permute-start.17 = (f32[18,512]{1,0:T(8,128)S(1)}, f32[18,512]{1,0:T(8,128)S(1)}, u32[]{:S(2)}, u32[]{:S(2)}) collective-permute-start(f32[18,512]{1,0:T(8,128)S(1)} %pad_maximum_fusion.mine_ref), channel_id=1, source_target_pairs={{0,4},{1,5},{2,6},{3,7},{4,0},{5,1},{6,2},{7,3},{8,12},{9,13},{10,... | collective-permute-start | bytes 110600 | tf_op jit(solution)/shard_map/cond/branch_1_fun/ppermute | solution.py:47
  45.0 1.5 %collective-permute-done.17.theirs_ref = f32[18,512]{1,0:T(8,128)S(1)} collective-permute-done((f32[18,512]{1,0:T(8,128)S(1)}, f32[18,512]{1,0:T(8,128)S(1)}, u32[]{:S(2)}, u32[]{:S(2)}) %collective-permute-start.17) | collective-permute-done | bytes 36896 | tf_op jit(solution)/shard_map/cond/branch_1_fun/ppermute | solution.py:47
  46.6 1.3 %collective-permute-done.19 = f32[34,512]{1,0:T(8,128)S(1)} collective-permute-done((f32[34,512]{1,0:T(8,128)S(1)}, f32[34,512]{1,0:T(8,128)S(1)}, u32[]{:S(2)}, u32[]{:S(2)}) %collective-permute-start.19) | collective-permute-done | bytes 69664 | tf_op jit(solution)/shard_map/ppermute | solution.py:47
  47.9 5.9 %conditional.3 = (f32[2,512]{1,0:T(2,128)}, bf16[2,512,256]{2,1,0:T(8,128)(2,1)S(1)}) conditional(s32[]{:T(128)} %convert_element_type.4, (bf16[512,256]{1,0:T(8,128)(2,1)S(1)}, bf16[512,256]{1,0:T(8,128)(2,1)S(1)}, bf16[1024,256]{1,0:T(8,128)(2,1)S(1)}, bf16[1024,256]{1,0:T(8,128)(2,1)S(1)}, bf16[1024,256]{1,0:T(8,128)(2,1)S(1)}, ...), branch_computations={%region_3.4_spmd, %region_4.5_spmd} | conditional | flops 1048576 | bytes 1048592 | solution.py:600
  47.9 5.9 %branch_1_fun.17 = (bf16[2,512,256]{2,1,0:T(8,128)(2,1)S(1)}, f32[2,512]{1,0:T(2,128)}) custom-call(bf16[1024,256]{1,0:T(8,128)(2,1)S(1)} %get-tuple-element.66.own_ref, bf16[1024,256]{1,0:T(8,128)(2,1)S(1)} %get-tuple-element.67.one_ref, bf16[1024,256]{1,0:T(8,128)(2,1)S(1)} %get-tuple-element.68.two_ref, ...), custom_call_target="tpu_custom_call" | custom-call | tf_op jit(solution)/shard_map/cond/branch_1_fun/pallas_call | solution.py:571
  54.6 1.2 %collective-permute-done.21.theirs_ref = bf16[2,512,256]{2,1,0:T(8,128)(2,1)S(1)} collective-permute-done((bf16[2,512,256]{2,1,0:T(8,128)(2,1)S(1)}, bf16[2,512,256]{2,1,0:T(8,128)(2,1)S(1)}, u32[]{:S(2)}, u32[]{:S(2)}) %collective-permute-start.21) | collective-permute-done | bytes 524320 | tf_op jit(solution)/shard_map/ppermute | solution.py:47
  55.8 0.8 %shard_map.52 = (bf16[2,512,256]{2,1,0:T(8,128)(2,1)}, bf16[512,256]{1,0:T(8,128)(2,1)}) custom-call(s32[1]{0:T(128)} %bitcast.core_ref, bf16[2,512,256]{2,1,0:T(8,128)(2,1)S(1)} %collective-permute-done.21.theirs_ref, bf16[2,512,256]{2,1,0:T(8,128)(2,1)} %get-tuple-element.101.embed_in_ref, ...), custom_call_target="tpu_custom_call", output_to_operand_aliasing={{0}: (2, {}), {1}: (3, {})} | custom-call | tf_op jit(solution)/shard_map/pallas_call | solution.py:614
  (54 shorter events, 4.2 us)
Async XLA Ops:
  0.6 2.0 %collective-permute-start.18 = (bf16[512,256]{1,0:T(8,128)(2,1)}, bf16[512,256]{1,0:T(8,128)(2,1)S(1)}, u32[]{:S(2)}, u32[]{:S(2)}) collective-permute-start(bf16[512,256]{1,0:T(8,128)(2,1)} %refs_1_.1), channel_id=1, source_target_pairs={{0,1},{1,0},{2,3},{3,2},{4,5},{5,4},{6,7},{7,6},{8,9},{9,8},{10,11... | collective-permute-start | bytes 786440 | tf_op jit(solution)/shard_map/ppermute | solution.py:47
  2.2 44.4 %collective-permute-start.20 = (bf16[512,256]{1,0:T(8,128)(2,1)}, bf16[512,256]{1,0:T(8,128)(2,1)}, u32[]{:S(2)}, u32[]{:S(2)}) collective-permute-start(bf16[512,256]{1,0:T(8,128)(2,1)} %refs_1_.1), channel_id=1, source_target_pairs={{0,1},{1,0},{2,3},{3,2},{4,5},{5,4},{6,7},{7,6},{8,9},{9,8},{10,11... | collective-permute-start | bytes 786440 | tf_op jit(solution)/shard_map/ppermute | solution.py:47
  2.8 45.0 %copy-start.6 = (bf16[2,512,256]{2,1,0:T(8,128)(2,1)S(1)}, bf16[2,512,256]{2,1,0:T(8,128)(2,1)}, u32[]{:S(2)}) copy-start(bf16[2,512,256]{2,1,0:T(8,128)(2,1)} %param.6) | copy-start | bytes 1572868
  2.8 45.0 %copy-start.7 = (bf16[512,256]{1,0:T(8,128)(2,1)S(1)}, bf16[512,256]{1,0:T(8,128)(2,1)}, u32[]{:S(2)}) copy-start(bf16[512,256]{1,0:T(8,128)(2,1)} %refs_1_.1) | copy-start | bytes 786436
  4.0 3.6 %collective-permute-start.5 = (f32[2,1024]{1,0:T(2,128)S(1)}, f32[2,1024]{1,0:T(2,128)S(1)}, u32[]{:S(2)}, u32[]{:S(2)}) collective-permute-start(f32[2,1024]{1,0:T(2,128)S(1)} %get-tuple-element.49), channel_id=1, source_target_pairs={{0,8},{8,0},{16,24},{24,16},{1,9},{9,1},{17,25},{25,17},{2,10},{10... | collective-permute-start | bytes 24584 | tf_op jit(solution)/shard_map/cond/branch_1_fun/ppermute | solution.py:47
  7.6 2.9 %collective-permute-start.7 = (f32[2,1024]{1,0:T(2,128)S(1)}, f32[2,1024]{1,0:T(2,128)S(1)}, u32[]{:S(2)}, u32[]{:S(2)}) collective-permute-start(f32[2,1024]{1,0:T(2,128)S(1)} %add.18), channel_id=1, source_target_pairs={{0,16},{8,24},{16,0},{24,8},{1,17},{9,25},{17,1},{25,9},{2,18},{10... | collective-permute-start | bytes 24584 | tf_op jit(solution)/shard_map/cond/branch_1_fun/ppermute | solution.py:47
  9.1 8.2 %collective-permute-start.6 = (bf16[1024,256]{1,0:T(8,128)(2,1)S(1)}, bf16[1024,256]{1,0:T(8,128)(2,1)S(1)}, u32[]{:S(2)}, u32[]{:S(2)}) collective-permute-start(bf16[1024,256]{1,0:T(8,128)(2,1)S(1)} %get-tuple-element.50.emb_ref), channel_id=1, source_target_pairs={{0,8},{8,0},{16,24},{24,16},{1,9},{9,1},{17,25},{25,17},{2,10},{10... | collective-permute-start | bytes 1572872 | tf_op jit(solution)/shard_map/cond/branch_1_fun/ppermute | solution.py:47
  10.3 9.4 %collective-permute-start.12 = (bf16[1024,256]{1,0:T(8,128)(2,1)S(1)}, bf16[1024,256]{1,0:T(8,128)(2,1)S(1)}, u32[]{:S(2)}, u32[]{:S(2)}) collective-permute-start(bf16[1024,256]{1,0:T(8,128)(2,1)S(1)} %get-tuple-element.50.emb_ref), channel_id=1, source_target_pairs={{0,16},{8,24},{16,0},{24,8},{1,17},{9,25},{17,1},{25,9},{2,18},{10... | collective-permute-start | bytes 1572872 | tf_op jit(solution)/shard_map/cond/branch_1_fun/ppermute | solution.py:47
  10.9 2.6 %collective-permute-start.8 = (f32[4,512]{1,0:T(4,128)S(1)}, f32[4,512]{1,0:T(4,128)S(1)}, u32[]{:S(2)}, u32[]{:S(2)}) collective-permute-start(f32[4,512]{1,0:T(4,128)S(1)} %pad_maximum_fusion.3), channel_id=1, source_target_pairs={{0,2},{1,3},{2,0},{3,1},{4,6},{5,7},{6,4},{7,5},{8,10},{9,11},{10,... | collective-permute-start | bytes 24584 | tf_op jit(solution)/shard_map/cond/branch_1_fun/ppermute | solution.py:47
  13.5 3.8 %collective-permute-start.9 = (f32[4,512]{1,0:T(4,128)S(1)}, f32[4,512]{1,0:T(4,128)S(1)}, u32[]{:S(2)}, u32[]{:S(2)}) collective-permute-start(f32[4,512]{1,0:T(4,128)S(1)} %fusion), channel_id=1, source_target_pairs={{0,4},{1,5},{2,6},{3,7},{4,0},{5,1},{6,2},{7,3},{8,12},{9,13},{10,... | collective-permute-start | bytes 24584 | tf_op jit(solution)/shard_map/cond/branch_1_fun/ppermute | solution.py:47
  17.3 3.1 %copy-start.4 = (bf16[1024,256]{1,0:T(8,128)(2,1)}, bf16[1024,256]{1,0:T(8,128)(2,1)S(1)}, u32[]{:S(2)}) copy-start(bf16[1024,256]{1,0:T(8,128)(2,1)S(1)} %collective-permute-done.6.emb_ref) | copy-start | bytes 1572868 | tf_op jit(solution)/shard_map/cond
  17.4 3.1 %collective-permute-start.10 = (f32[4,512]{1,0:T(4,128)S(1)}, f32[4,512]{1,0:T(4,128)S(1)}, u32[]{:S(2)}, u32[]{:S(2)}) collective-permute-start(f32[4,512]{1,0:T(4,128)S(1)} %add.21), channel_id=1, source_target_pairs={{0,16},{8,24},{16,0},{24,8},{1,17},{9,25},{17,1},{25,9},{2,18},{10... | collective-permute-start | bytes 24584 | tf_op jit(solution)/shard_map/cond/branch_1_fun/ppermute | solution.py:47
  18.7 8.0 %collective-permute-start.13 = (bf16[1024,256]{1,0:T(8,128)(2,1)S(1)}, bf16[1024,256]{1,0:T(8,128)(2,1)S(1)}, u32[]{:S(2)}, u32[]{:S(2)}) collective-permute-start(bf16[1024,256]{1,0:T(8,128)(2,1)S(1)} %collective-permute-done.6.emb_ref), channel_id=1, source_target_pairs={{0,16},{8,24},{16,0},{24,8},{1,17},{9,25},{17,1},{25,9},{2,18},{10... | collective-permute-start | bytes 1572872 | tf_op jit(solution)/shard_map/cond/branch_1_fun/ppermute | solution.py:47
  19.7 4.6 %copy-start = (bf16[1024,256]{1,0:T(8,128)(2,1)}, bf16[1024,256]{1,0:T(8,128)(2,1)S(1)}, u32[]{:S(2)}) copy-start(bf16[1024,256]{1,0:T(8,128)(2,1)S(1)} %collective-permute-done.12.emb_ref) | copy-start | bytes 1572868 | tf_op jit(solution)/shard_map/cond
  20.5 3.1 %collective-permute-start.11 = (f32[8,512]{1,0:T(8,128)S(1)}, f32[8,512]{1,0:T(8,128)S(1)}, u32[]{:S(2)}, u32[]{:S(2)}) collective-permute-start(f32[8,512]{1,0:T(8,128)S(1)} %pad_maximum_fusion.1), channel_id=1, source_target_pairs={{0,8},{8,0},{16,24},{24,16},{1,9},{9,1},{17,25},{25,17},{2,10},{10... | collective-permute-start | bytes 49160 | tf_op jit(solution)/shard_map/cond/branch_1_fun/ppermute | solution.py:47
  26.7 2.5 %copy-start.2 = (bf16[1024,256]{1,0:T(8,128)(2,1)}, bf16[1024,256]{1,0:T(8,128)(2,1)S(1)}, u32[]{:S(2)}) copy-start(bf16[1024,256]{1,0:T(8,128)(2,1)S(1)} %collective-permute-done.13.emb_ref) | copy-start | bytes 1572868 | tf_op jit(solution)/shard_map/cond
  29.2 3.3 %collective-permute-start.14 = (f32[8,512]{1,0:T(8,128)S(1)}, f32[8,512]{1,0:T(8,128)S(1)}, u32[]{:S(2)}, u32[]{:S(2)}) collective-permute-start(f32[8,512]{1,0:T(8,128)S(1)} %branch_1_fun.14), channel_id=1, source_target_pairs={{0,2},{1,3},{2,0},{3,1},{4,6},{5,7},{6,4},{7,5},{8,10},{9,11},{10,... | collective-permute-start | bytes 49160 | tf_op jit(solution)/shard_map/cond/branch_1_fun/ppermute | solution.py:47
  32.5 3.5 %collective-permute-start.15 = (f32[8,512]{1,0:T(8,128)S(1)}, f32[8,512]{1,0:T(8,128)S(1)}, u32[]{:S(2)}, u32[]{:S(2)}) collective-permute-start(f32[8,512]{1,0:T(8,128)S(1)} %add.22), channel_id=1, source_target_pairs={{0,4},{1,5},{2,6},{3,7},{4,0},{5,1},{6,2},{7,3},{8,12},{9,13},{10,... | collective-permute-start | bytes 49160 | tf_op jit(solution)/shard_map/cond/branch_1_fun/ppermute | solution.py:47
  36.0 10.5 %copy-start.1 = (bf16[1024,256]{1,0:T(8,128)(2,1)S(1)}, bf16[1024,256]{1,0:T(8,128)(2,1)}, u32[]{:S(2)}) copy-start(bf16[1024,256]{1,0:T(8,128)(2,1)} %copy-done) | copy-start | bytes 1572868 | tf_op jit(solution)/shard_map/cond
  36.0 10.5 %copy-start.3 = (bf16[1024,256]{1,0:T(8,128)(2,1)S(1)}, bf16[1024,256]{1,0:T(8,128)(2,1)}, u32[]{:S(2)}) copy-start(bf16[1024,256]{1,0:T(8,128)(2,1)} %copy-done.2) | copy-start | bytes 1572868 | tf_op jit(solution)/shard_map/cond
  36.0 10.5 %copy-start.5 = (bf16[1024,256]{1,0:T(8,128)(2,1)S(1)}, bf16[1024,256]{1,0:T(8,128)(2,1)}, u32[]{:S(2)}) copy-start(bf16[1024,256]{1,0:T(8,128)(2,1)} %copy-done.4) | copy-start | bytes 1572868 | tf_op jit(solution)/shard_map/cond
  39.7 2.8 %collective-permute-start.16 = (f32[16,512]{1,0:T(8,128)S(1)}, f32[16,512]{1,0:T(8,128)S(1)}, u32[]{:S(2)}, u32[]{:S(2)}) collective-permute-start(f32[16,512]{1,0:T(8,128)S(1)} %branch_1_fun.15), channel_id=1, source_target_pairs={{0,2},{1,3},{2,0},{3,1},{4,6},{5,7},{6,4},{7,5},{8,10},{9,11},{10,... | collective-permute-start | bytes 98312 | tf_op jit(solution)/shard_map/cond/branch_1_fun/ppermute | solution.py:47
  42.5 3.9 %collective-permute-start.17 = (f32[18,512]{1,0:T(8,128)S(1)}, f32[18,512]{1,0:T(8,128)S(1)}, u32[]{:S(2)}, u32[]{:S(2)}) collective-permute-start(f32[18,512]{1,0:T(8,128)S(1)} %pad_maximum_fusion.mine_ref), channel_id=1, source_target_pairs={{0,4},{1,5},{2,6},{3,7},{4,0},{5,1},{6,2},{7,3},{8,12},{9,13},{10,... | collective-permute-start | bytes 110600 | tf_op jit(solution)/shard_map/cond/branch_1_fun/ppermute | solution.py:47
  46.5 1.3 %collective-permute-start.19 = (f32[34,512]{1,0:T(8,128)S(1)}, f32[34,512]{1,0:T(8,128)S(1)}, u32[]{:S(2)}, u32[]{:S(2)}) collective-permute-start(f32[34,512]{1,0:T(8,128)S(1)} %get-tuple-element.98), channel_id=1, source_target_pairs={{0,1},{1,0},{2,3},{3,2},{4,5},{5,4},{6,7},{7,6},{8,9},{9,8},{10,11... | collective-permute-start | bytes 208904 | tf_op jit(solution)/shard_map/ppermute | solution.py:47
  53.8 2.0 %collective-permute-start.21 = (bf16[2,512,256]{2,1,0:T(8,128)(2,1)S(1)}, bf16[2,512,256]{2,1,0:T(8,128)(2,1)S(1)}, u32[]{:S(2)}, u32[]{:S(2)}) collective-permute-start(bf16[2,512,256]{2,1,0:T(8,128)(2,1)S(1)} %get-tuple-element.100.mine_ref), channel_id=1, source_target_pairs={{0,1},{1,0},{2,3},{3,2},{4,5},{5,4},{6,7},{7,6},{8,9},{9,8},{10,11... | collective-permute-start | bytes 1572872 | tf_op jit(solution)/shard_map/ppermute | solution.py:47

commit v3 on v2

--- a/solution.py
+++ b/solution.py
@@ -183,19 +183,24 @@
             sum_refs[0][view:view + 1] = jnp.sum(total, axis=0, keepdims=True)
 
 
-def lane_sums(weight_ref, block, view, at, part):
+def spread(weight_ref, view):
+    lines = [weight_ref[2 * at + view:2 * at + view + 1] for at in range(4)]
+    return [jnp.broadcast_to(line, (8, line.shape[1])) for line in lines]
+
+
+def lane_sums(weight, block, view, part):
     values = block[view, part]
     tile, rows = values.shape
-    weight = jnp.broadcast_to(weight_ref[2 * at + view:2 * at + view + 1], (8, rows))
     scaled = (values.reshape(-1, 8, rows) * weight).reshape(tile, rows)
     return sum(scaled[:, lane:lane + 128] for lane in range(0, rows, 128))
 
 
 def column_kernel(tile, weight_ref, own_ref, one_ref, two_ref, out_ref):
     for view in range(2):
+        weight = spread(weight_ref, view)
         for first in range(0, own_ref.shape[1], tile):
             part = slice(first, first + tile)
-            own, one, two = (lane_sums(weight_ref, block, view, at, part) for at, block in enumerate((own_ref, one_ref, two_ref)))
+            own, one, two = (lane_sums(weight[at], block, view, part) for at, block in enumerate((own_ref, one_ref, two_ref)))
             out_ref[0, view, part] = own + one
             out_ref[1, view, part] = two
 
@@ -208,13 +213,14 @@
         cross = [jnp.zeros((8, rows), jnp.float32)] * 2
         out_ref[...] = jnp.zeros(out_ref.shape, jnp.float32)
     for view in range(2):
+        weight = spread(weight_ref, view)
         totals = [jnp.zeros((8, rows), jnp.float32)] * 4
         for first in range(0, count, tile):
             part = slice(first, first + tile)
             if last:
-                lanes = [lane_sums(weight_ref, blocks[at], view, at, part) for at in range(4)]
+                lanes = [lane_sums(weight[at], blocks[at], view, part) for at in range(4)]
             else:
-                lanes = [refs[0][0, view, part], refs[0][1, view, part] + lane_sums(weight_ref, three_ref, view, 3, part)]
+                lanes = [refs[0][0, view, part], refs[0][1, view, part] + lane_sums(weight[3], three_ref, view, part)]
             scale = 1.0 / jnp.sum(tree_sum(lanes), axis=1, keepdims=True)
             for at in range(4):
                 scaled = blocks[at][view, part] * scale
@@ -502,11 +508,13 @@
     sums = jnp.concatenate([jnp.sum(sink * (1.0 / sums)[:, :, None], axis=1), soft])
     sums = sums + swap(sums, "proto", proto, 2)
     sums = sums + swap(sums, "proto", proto, 4)
-    one, sums = after(one, sums)
-    three = swap(one, "samp", samp, 2)
-
-    sinks = [sink] + [scored(block, proto_b, False)[0] for block in (one, two, three)]
+    one, two, sums = lax.optimization_barrier((one, two, sums))
+    half = one.shape[0] // 2
+    three = jnp.concatenate([swap(one[:half], "samp", samp, 2), swap(two[half:], "samp", samp, 1)])
+
     both = jnp.concatenate([sums, swap(sums, "samp", samp, 2)])
+    near, far = after(one, both)[0], after(two, both)[0]
+    sinks = [sink] + [scored(block, proto_b, False)[0] for block in (near, far, three)]
     sums = jnp.concatenate([both, swap(both, "samp", samp, 1)])
     weights = 1.0 / jnp.concatenate([sums[at:at + 2] for at in (0, 8, 4, 12)])
     soft_total = jnp.concatenate([sums[at:at + 2] for at in (2, 10, 6, 14)])

time: 57 us -> 56.7 us (level)
    ppermute x17 -> x18, starting transfers between devices: 20.7 us -> 20.3 us  [swap(): return lax.ppermute(value, axis, [(i, i ^ mask) for i in range(size)])]
    ppermute x17 -> x18, waiting for transfers between devices: 15.9 us -> 16.2 us  [swap(): return lax.ppermute(value, axis, [(i, i ^ mask) for i in range(size)])]
  transfers between devices with their start and end apart: 17 -> 18, of which waited for: 11 -> 12; matrix products, arithmetic and copies ran while one was open for 1% -> 1% of each run, Pallas kernels for 21% -> 20%
where the time goes in v3:
time: 56.7 us; the launch traced here: 56.5 us
  starting transfers between devices  20.3 us (36%)
  Pallas kernels  18.2 us (32%)
  waiting for transfers between devices  16.2 us (29%)
  between operations  0.86 us (2%)
    ppermute x18, starting transfers between devices, swap(): return lax.ppermute(value, axis, [(i, i ^ mask) for i in range(size)])  20.3 us
    ppermute x18, waiting for transfers between devices, swap(): return lax.ppermute(value, axis, [(i, i ^ mask) for i in range(size)])  16.2 us
    pallas_call x1, Pallas kernels, grads(): pl.pallas_call(functools.partial(kernel, lanes // 2 if kernel is proto_gr...  5.88 us
    pallas_call x2, Pallas kernels, swept(): pl.pallas_call(functools.partial(sweep_kernel, not sums, 128), out_shape=...  5.21 us
    pallas_call x4, Pallas kernels, scored(): pl.pallas_call(functools.partial(score_kernel, min(count, 256)), out_shap...  3.25 us
    pallas_call x2, Pallas kernels, unit_rows(): pl.pallas_call(unit_kernel, out_shape=[jax.ShapeDtypeStruct(raw.shape, jn...  1.55 us
  transfers between devices with their start and end apart: 18, of which 12 were waited for; matrix products, arithmetic and copies ran while one was open for 1% of the time, Pallas kernels for 20%

profile of v3, /device:TPU:1, one launch (start us, length us, event | category | flops | bytes accessed | tf_op | source)
XLA Modules:
  0.0 56.5 jit_solution(9234876187878635462)
XLA Ops:
  0.8 1.4 %shard_map.49 = (bf16[1024,256]{1,0:T(8,128)(2,1)S(1)}, bf16[512,256]{1,0:T(8,128)(2,1)S(1)}) custom-call(bf16[1024,256]{1,0:T(8,128)(2,1)} %bitcast.2, bf16[512,256]{1,0:T(8,128)(2,1)} %refs_1_.1), custom_call_target="tpu_custom_call" | custom-call | tf_op jit(solution)/shard_map/pallas_call | solution.py:554
  2.9 43.4 %conditional.2 = (f32[34,512]{1,0:T(8,128)S(1)}, bf16[1024,256]{1,0:T(8,128)(2,1)S(1)}, bf16[1024,256]{1,0:T(8,128)(2,1)S(1)}, bf16[1024,256]{1,0:T(8,128)(2,1)S(1)}) conditional(s32[]{:T(128)} %convert_element_type.4, (bf16[512,256]{1,0:T(8,128)(2,1)S(1)}, bf16[512,256]{1,0:T(8,128)(2,1)S(1)}) %tuple.29, (bf16[512,256]{1,0:T(8,128)(2,1)S(1)}, ...), branch_computations={%region_0.1_spmd, %region_1.3_spmd} | conditional | flops 2189508608 | bytes 37896952 | solution.py:572
  2.9 1.0 %branch_1_fun.9 = (f32[2,1024,512]{2,1,0:T(8,128)S(1)}, f32[2,512]{1,0:T(2,128)S(1)}, f32[2,1024]{1,0:T(2,128)S(1)}) custom-call(bf16[1024,256]{1,0:T(8,128)(2,1)S(1)} %get-tuple-element.50.emb_ref, bf16[1024,256]{1,0:T(8,128)(2,1)S(1)} %constant_dynamic-update-slice_fusion.2.proto_ref), custom_call_target="tpu_custom_call" | custom-call | flops 536870912 | bytes 1048576 | tf_op jit(solution)/shard_map/cond/branch_1_fun/pallas_call | solution.py:460
  4.0 2.3 %collective-permute-start.5 = (f32[2,1024]{1,0:T(2,128)S(1)}, f32[2,1024]{1,0:T(2,128)S(1)}, u32[]{:S(2)}, u32[]{:S(2)}) collective-permute-start(f32[2,1024]{1,0:T(2,128)S(1)} %get-tuple-element.49), channel_id=1, source_target_pairs={{0,8},{8,0},{16,24},{24,16},{1,9},{9,1},{17,25},{25,17},{2,10},{10... | collective-permute-start | bytes 24584 | tf_op jit(solution)/shard_map/cond/branch_1_fun/ppermute | solution.py:47
  6.3 1.3 %collective-permute-done.5 = f32[2,1024]{1,0:T(2,128)S(1)} collective-permute-done((f32[2,1024]{1,0:T(2,128)S(1)}, f32[2,1024]{1,0:T(2,128)S(1)}, u32[]{:S(2)}, u32[]{:S(2)}) %collective-permute-start.5) | collective-permute-done | bytes 8224 | tf_op jit(solution)/shard_map/cond/branch_1_fun/ppermute | solution.py:47
  7.6 1.5 %collective-permute-start.8 = (f32[2,1024]{1,0:T(2,128)S(1)}, f32[2,1024]{1,0:T(2,128)S(1)}, u32[]{:S(2)}, u32[]{:S(2)}) collective-permute-start(f32[2,1024]{1,0:T(2,128)S(1)} %add.18), channel_id=1, source_target_pairs={{0,16},{8,24},{16,0},{24,8},{1,17},{9,25},{17,1},{25,9},{2,18},{10... | collective-permute-start | bytes 24584 | tf_op jit(solution)/shard_map/cond/branch_1_fun/ppermute | solution.py:47
  9.1 1.2 %collective-permute-start.6 = (bf16[1024,256]{1,0:T(8,128)(2,1)S(1)}, bf16[1024,256]{1,0:T(8,128)(2,1)S(1)}, u32[]{:S(2)}, u32[]{:S(2)}) collective-permute-start(bf16[1024,256]{1,0:T(8,128)(2,1)S(1)} %get-tuple-element.50.emb_ref), channel_id=1, source_target_pairs={{0,8},{8,0},{16,24},{24,16},{1,9},{9,1},{17,25},{25,17},{2,10},{10... | collective-permute-start | bytes 1572872 | tf_op jit(solution)/shard_map/cond/branch_1_fun/ppermute | solution.py:47
  10.9 1.5 %collective-permute-start.9 = (f32[4,512]{1,0:T(4,128)S(1)}, f32[4,512]{1,0:T(4,128)S(1)}, u32[]{:S(2)}, u32[]{:S(2)}) collective-permute-start(f32[4,512]{1,0:T(4,128)S(1)} %pad_maximum_fusion.3), channel_id=1, source_target_pairs={{0,2},{1,3},{2,0},{3,1},{4,6},{5,7},{6,4},{7,5},{8,10},{9,11},{10,... | collective-permute-start | bytes 24584 | tf_op jit(solution)/shard_map/cond/branch_1_fun/ppermute | solution.py:47
  12.4 1.1 %collective-permute-done.9 = f32[4,512]{1,0:T(4,128)S(1)} collective-permute-done((f32[4,512]{1,0:T(4,128)S(1)}, f32[4,512]{1,0:T(4,128)S(1)}, u32[]{:S(2)}, u32[]{:S(2)}) %collective-permute-start.9) | collective-permute-done | bytes 8224 | tf_op jit(solution)/shard_map/cond/branch_1_fun/ppermute | solution.py:47
  13.5 2.8 %collective-permute-start.10 = (f32[4,512]{1,0:T(4,128)S(1)}, f32[4,512]{1,0:T(4,128)S(1)}, u32[]{:S(2)}, u32[]{:S(2)}) collective-permute-start(f32[4,512]{1,0:T(4,128)S(1)} %fusion), channel_id=1, source_target_pairs={{0,4},{1,5},{2,6},{3,7},{4,0},{5,1},{6,2},{7,3},{8,12},{9,13},{10,... | collective-permute-start | bytes 24584 | tf_op jit(solution)/shard_map/cond/branch_1_fun/ppermute | solution.py:47
  16.3 1.0 %collective-permute-done.10 = f32[4,512]{1,0:T(4,128)S(1)} collective-permute-done((f32[4,512]{1,0:T(4,128)S(1)}, f32[4,512]{1,0:T(4,128)S(1)}, u32[]{:S(2)}, u32[]{:S(2)}) %collective-permute-start.10) | collective-permute-done | bytes 8224 | tf_op jit(solution)/shard_map/cond/branch_1_fun/ppermute | solution.py:47
  17.4 1.0 %collective-permute-done.7.emb_ref = bf16[1024,256]{1,0:T(8,128)(2,1)S(1)} collective-permute-done((bf16[1024,256]{1,0:T(8,128)(2,1)S(1)}, bf16[1024,256]{1,0:T(8,128)(2,1)S(1)}, u32[]{:S(2)}, u32[]{:S(2)}) %collective-permute-start.7) | collective-permute-done | bytes 524320 | tf_op jit(solution)/shard_map/cond/branch_1_fun/ppermute | solution.py:47
  18.7 1.2 %collective-permute-start.13 = (bf16[512,256]{1,0:T(8,128)(2,1)S(1)}, bf16[512,256]{1,0:T(8,128)(2,1)S(1)}, u32[]{:S(2)}, u32[]{:S(2)}) collective-permute-start(bf16[512,256]{1,0:T(8,128)(2,1)S(1)} %slice.32), channel_id=1, source_target_pairs={{0,16},{8,24},{16,0},{24,8},{1,17},{9,25},{17,1},{25,9},{2,18},{10... | collective-permute-start | bytes 786440 | tf_op jit(solution)/shard_map/cond/branch_1_fun/ppermute | solution.py:47
  20.3 0.9 %collective-permute-done.11 = f32[4,512]{1,0:T(4,128)S(1)} collective-permute-done((f32[4,512]{1,0:T(4,128)S(1)}, f32[4,512]{1,0:T(4,128)S(1)}, u32[]{:S(2)}, u32[]{:S(2)}) %collective-permute-start.11) | collective-permute-done | bytes 8224 | tf_op jit(solution)/shard_map/cond/branch_1_fun/ppermute | solution.py:47
  23.2 2.5 %collective-permute-done.12 = f32[8,512]{1,0:T(8,128)S(1)} collective-permute-done((f32[8,512]{1,0:T(8,128)S(1)}, f32[8,512]{1,0:T(8,128)S(1)}, u32[]{:S(2)}, u32[]{:S(2)}) %collective-permute-start.12) | collective-permute-done | bytes 16416 | tf_op jit(solution)/shard_map/cond/branch_1_fun/ppermute | solution.py:47
  25.7 0.7 %branch_1_fun.13.refs_0_ = f32[2,2,1024,128]{3,2,1,0:T(8,128)S(1)} custom-call(f32[8,512]{1,0:T(8,128)S(1)} %maximum_divide_fusion.weight_ref, f32[2,1024,512]{2,1,0:T(8,128)S(1)} %get-tuple-element.51.own_ref, f32[2,1024,512]{2,1,0:T(8,128)S(1)} %branch_1_fun.10.one_ref, f32[2,1024,512]{2,1,0:T(8,128)S(1)} %branch_1_fun.11.two_ref), custom_call_target="tpu_custom_call" | custom-call | flops 6291456 | bytes 2097152 | tf_op jit(solution)/shard_map/cond/branch_1_fun/pallas_call | solution.py:486
  26.6 0.7 %branch_1_fun.12.three_ref = f32[2,1024,512]{2,1,0:T(8,128)S(1)} custom-call(bf16[1024,256]{1,0:T(8,128)(2,1)S(1)} %constant_dynamic-update-slice_fusion.4.emb_ref, bf16[1024,256]{1,0:T(8,128)(2,1)S(1)} %constant_dynamic-update-slice_fusion.2.proto_ref), custom_call_target="tpu_custom_call" | custom-call | flops 536870912 | bytes 1048576 | tf_op jit(solution)/shard_map/cond/branch_1_fun/pallas_call | solution.py:460
  27.3 1.6 %branch_1_fun.14 = f32[8,512]{1,0:T(8,128)S(1)} custom-call(f32[8,512]{1,0:T(8,128)S(1)} %maximum_divide_fusion.weight_ref, f32[2,1024,512]{2,1,0:T(8,128)S(1)} %get-tuple-element.51.own_ref, f32[2,1024,512]{2,1,0:T(8,128)S(1)} %branch_1_fun.10.one_ref, f32[2,1024,512]{2,1,0:T(8,128)S(1)} %branch_1_fun.11.two_ref, ...), custom_call_target="tpu_custom_call" | custom-call | flops 16777216 | bytes 2097152 | tf_op jit(solution)/shard_map/cond/branch_1_fun/pallas_call | solution.py:474
  29.0 1.4 %collective-permute-start.15 = (f32[8,512]{1,0:T(8,128)S(1)}, f32[8,512]{1,0:T(8,128)S(1)}, u32[]{:S(2)}, u32[]{:S(2)}) collective-permute-start(f32[8,512]{1,0:T(8,128)S(1)} %branch_1_fun.14), channel_id=1, source_target_pairs={{0,2},{1,3},{2,0},{3,1},{4,6},{5,7},{6,4},{7,5},{8,10},{9,11},{10,... | collective-permute-start | bytes 49160 | tf_op jit(solution)/shard_map/cond/branch_1_fun/ppermute | solution.py:47
  30.4 1.8 %collective-permute-done.15 = f32[8,512]{1,0:T(8,128)S(1)} collective-permute-done((f32[8,512]{1,0:T(8,128)S(1)}, f32[8,512]{1,0:T(8,128)S(1)}, u32[]{:S(2)}, u32[]{:S(2)}) %collective-permute-start.15) | collective-permute-done | bytes 16416 | tf_op jit(solution)/shard_map/cond/branch_1_fun/ppermute | solution.py:47
  32.3 2.4 %collective-permute-start.16 = (f32[8,512]{1,0:T(8,128)S(1)}, f32[8,512]{1,0:T(8,128)S(1)}, u32[]{:S(2)}, u32[]{:S(2)}) collective-permute-start(f32[8,512]{1,0:T(8,128)S(1)} %add.22), channel_id=1, source_target_pairs={{0,4},{1,5},{2,6},{3,7},{4,0},{5,1},{6,2},{7,3},{8,12},{9,13},{10,... | collective-permute-start | bytes 49160 | tf_op jit(solution)/shard_map/cond/branch_1_fun/ppermute | solution.py:47
  34.7 1.1 %collective-permute-done.16 = f32[8,512]{1,0:T(8,128)S(1)} collective-permute-done((f32[8,512]{1,0:T(8,128)S(1)}, f32[8,512]{1,0:T(8,128)S(1)}, u32[]{:S(2)}, u32[]{:S(2)}) %collective-permute-start.16) | collective-permute-done | bytes 16416 | tf_op jit(solution)/shard_map/cond/branch_1_fun/ppermute | solution.py:47
  35.8 3.6 %branch_1_fun.15 = f32[16,512]{1,0:T(8,128)S(1)} custom-call(f32[8,512]{1,0:T(8,128)S(1)} %add_divide_fusion.weight_ref, f32[2,1024,512]{2,1,0:T(8,128)S(1)} %get-tuple-element.51.own_ref, f32[2,1024,512]{2,1,0:T(8,128)S(1)} %branch_1_fun.10.one_ref, f32[2,1024,512]{2,1,0:T(8,128)S(1)} %branch_1_fun.11.two_ref, f32[2,1024,512]{2,1,0:T(8,128)S(1)} %branch_1_fun.12.three_ref), custom_call_target="tpu_custom_call" | custom-call | flops 16777216 | bytes 2097152 | tf_op jit(solution)/shard_map/cond/branch_1_fun/pallas_call | solution.py:474
  39.4 1.4 %collective-permute-start.17 = (f32[16,512]{1,0:T(8,128)S(1)}, f32[16,512]{1,0:T(8,128)S(1)}, u32[]{:S(2)}, u32[]{:S(2)}) collective-permute-start(f32[16,512]{1,0:T(8,128)S(1)} %branch_1_fun.15), channel_id=1, source_target_pairs={{0,2},{1,3},{2,0},{3,1},{4,6},{5,7},{6,4},{7,5},{8,10},{9,11},{10,... | collective-permute-start | bytes 98312 | tf_op jit(solution)/shard_map/cond/branch_1_fun/ppermute | solution.py:47
  40.8 1.4 %collective-permute-done.17 = f32[16,512]{1,0:T(8,128)S(1)} collective-permute-done((f32[16,512]{1,0:T(8,128)S(1)}, f32[16,512]{1,0:T(8,128)S(1)}, u32[]{:S(2)}, u32[]{:S(2)}) %collective-permute-start.17) | collective-permute-done | bytes 32800 | tf_op jit(solution)/shard_map/cond/branch_1_fun/ppermute | solution.py:47
  42.3 2.4 %collective-permute-start.18 = (f32[18,512]{1,0:T(8,128)S(1)}, f32[18,512]{1,0:T(8,128)S(1)}, u32[]{:S(2)}, u32[]{:S(2)}) collective-permute-start(f32[18,512]{1,0:T(8,128)S(1)} %pad_maximum_fusion.mine_ref), channel_id=1, source_target_pairs={{0,4},{1,5},{2,6},{3,7},{4,0},{5,1},{6,2},{7,3},{8,12},{9,13},{10,... | collective-permute-start | bytes 110600 | tf_op jit(solution)/shard_map/cond/branch_1_fun/ppermute | solution.py:47
  44.7 1.5 %collective-permute-done.18.theirs_ref = f32[18,512]{1,0:T(8,128)S(1)} collective-permute-done((f32[18,512]{1,0:T(8,128)S(1)}, f32[18,512]{1,0:T(8,128)S(1)}, u32[]{:S(2)}, u32[]{:S(2)}) %collective-permute-start.18) | collective-permute-done | bytes 36896 | tf_op jit(solution)/shard_map/cond/branch_1_fun/ppermute | solution.py:47
  46.3 1.3 %collective-permute-done.20 = f32[34,512]{1,0:T(8,128)S(1)} collective-permute-done((f32[34,512]{1,0:T(8,128)S(1)}, f32[34,512]{1,0:T(8,128)S(1)}, u32[]{:S(2)}, u32[]{:S(2)}) %collective-permute-start.20) | collective-permute-done | bytes 69664 | tf_op jit(solution)/shard_map/ppermute | solution.py:47
  47.6 5.9 %conditional.3 = (f32[2,512]{1,0:T(2,128)}, bf16[2,512,256]{2,1,0:T(8,128)(2,1)S(1)}) conditional(s32[]{:T(128)} %convert_element_type.4, (bf16[512,256]{1,0:T(8,128)(2,1)S(1)}, bf16[512,256]{1,0:T(8,128)(2,1)S(1)}, bf16[1024,256]{1,0:T(8,128)(2,1)S(1)}, bf16[1024,256]{1,0:T(8,128)(2,1)S(1)}, bf16[1024,256]{1,0:T(8,128)(2,1)S(1)}, ...), branch_computations={%region_3.4_spmd, %region_4.5_spmd} | conditional | flops 1048576 | bytes 1048592 | solution.py:608
  47.6 5.9 %branch_1_fun.17 = (bf16[2,512,256]{2,1,0:T(8,128)(2,1)S(1)}, f32[2,512]{1,0:T(2,128)}) custom-call(bf16[1024,256]{1,0:T(8,128)(2,1)S(1)} %get-tuple-element.69.own_ref, bf16[1024,256]{1,0:T(8,128)(2,1)S(1)} %get-tuple-element.70.one_ref, bf16[1024,256]{1,0:T(8,128)(2,1)S(1)} %get-tuple-element.71.two_ref, ...), custom_call_target="tpu_custom_call" | custom-call | tf_op jit(solution)/shard_map/cond/branch_1_fun/pallas_call | solution.py:579
  54.3 1.2 %collective-permute-done.22.theirs_ref = bf16[2,512,256]{2,1,0:T(8,128)(2,1)S(1)} collective-permute-done((bf16[2,512,256]{2,1,0:T(8,128)(2,1)S(1)}, bf16[2,512,256]{2,1,0:T(8,128)(2,1)S(1)}, u32[]{:S(2)}, u32[]{:S(2)}) %collective-permute-start.22) | collective-permute-done | bytes 524320 | tf_op jit(solution)/shard_map/ppermute | solution.py:47
  55.5 0.8 %shard_map.52 = (bf16[2,512,256]{2,1,0:T(8,128)(2,1)}, bf16[512,256]{1,0:T(8,128)(2,1)}) custom-call(s32[1]{0:T(128)} %bitcast.core_ref, bf16[2,512,256]{2,1,0:T(8,128)(2,1)S(1)} %collective-permute-done.22.theirs_ref, bf16[2,512,256]{2,1,0:T(8,128)(2,1)} %get-tuple-element.104.embed_in_ref, ...), custom_call_target="tpu_custom_call", output_to_operand_aliasing={{0}: (2, {}), {1}: (3, {})} | custom-call | tf_op jit(solution)/shard_map/pallas_call | solution.py:622
  (60 shorter events, 5.2 us)
Async XLA Ops:
  0.6 2.0 %collective-permute-start.19 = (bf16[512,256]{1,0:T(8,128)(2,1)}, bf16[512,256]{1,0:T(8,128)(2,1)S(1)}, u32[]{:S(2)}, u32[]{:S(2)}) collective-permute-start(bf16[512,256]{1,0:T(8,128)(2,1)} %refs_1_.1), channel_id=1, source_target_pairs={{0,1},{1,0},{2,3},{3,2},{4,5},{5,4},{6,7},{7,6},{8,9},{9,8},{10,11... | collective-permute-start | bytes 786440 | tf_op jit(solution)/shard_map/ppermute | solution.py:47
  2.2 44.2 %collective-permute-start.21 = (bf16[512,256]{1,0:T(8,128)(2,1)}, bf16[512,256]{1,0:T(8,128)(2,1)}, u32[]{:S(2)}, u32[]{:S(2)}) collective-permute-start(bf16[512,256]{1,0:T(8,128)(2,1)} %refs_1_.1), channel_id=1, source_target_pairs={{0,1},{1,0},{2,3},{3,2},{4,5},{5,4},{6,7},{7,6},{8,9},{9,8},{10,11... | collective-permute-start | bytes 786440 | tf_op jit(solution)/shard_map/ppermute | solution.py:47
  2.8 44.8 %copy-start.6 = (bf16[2,512,256]{2,1,0:T(8,128)(2,1)S(1)}, bf16[2,512,256]{2,1,0:T(8,128)(2,1)}, u32[]{:S(2)}) copy-start(bf16[2,512,256]{2,1,0:T(8,128)(2,1)} %param.6) | copy-start | bytes 1572868
  2.8 44.7 %copy-start.7 = (bf16[512,256]{1,0:T(8,128)(2,1)S(1)}, bf16[512,256]{1,0:T(8,128)(2,1)}, u32[]{:S(2)}) copy-start(bf16[512,256]{1,0:T(8,128)(2,1)} %refs_1_.1) | copy-start | bytes 786436
  4.0 3.6 %collective-permute-start.5 = (f32[2,1024]{1,0:T(2,128)S(1)}, f32[2,1024]{1,0:T(2,128)S(1)}, u32[]{:S(2)}, u32[]{:S(2)}) collective-permute-start(f32[2,1024]{1,0:T(2,128)S(1)} %get-tuple-element.49), channel_id=1, source_target_pairs={{0,8},{8,0},{16,24},{24,16},{1,9},{9,1},{17,25},{25,17},{2,10},{10... | collective-permute-start | bytes 24584 | tf_op jit(solution)/shard_map/cond/branch_1_fun/ppermute | solution.py:47
  7.6 2.9 %collective-permute-start.8 = (f32[2,1024]{1,0:T(2,128)S(1)}, f32[2,1024]{1,0:T(2,128)S(1)}, u32[]{:S(2)}, u32[]{:S(2)}) collective-permute-start(f32[2,1024]{1,0:T(2,128)S(1)} %add.18), channel_id=1, source_target_pairs={{0,16},{8,24},{16,0},{24,8},{1,17},{9,25},{17,1},{25,9},{2,18},{10... | collective-permute-start | bytes 24584 | tf_op jit(solution)/shard_map/cond/branch_1_fun/ppermute | solution.py:47
  9.1 8.2 %collective-permute-start.6 = (bf16[1024,256]{1,0:T(8,128)(2,1)S(1)}, bf16[1024,256]{1,0:T(8,128)(2,1)S(1)}, u32[]{:S(2)}, u32[]{:S(2)}) collective-permute-start(bf16[1024,256]{1,0:T(8,128)(2,1)S(1)} %get-tuple-element.50.emb_ref), channel_id=1, source_target_pairs={{0,8},{8,0},{16,24},{24,16},{1,9},{9,1},{17,25},{25,17},{2,10},{10... | collective-permute-start | bytes 1572872 | tf_op jit(solution)/shard_map/cond/branch_1_fun/ppermute | solution.py:47
  10.3 8.0 %collective-permute-start.7 = (bf16[1024,256]{1,0:T(8,128)(2,1)S(1)}, bf16[1024,256]{1,0:T(8,128)(2,1)S(1)}, u32[]{:S(2)}, u32[]{:S(2)}) collective-permute-start(bf16[1024,256]{1,0:T(8,128)(2,1)S(1)} %get-tuple-element.50.emb_ref), channel_id=1, source_target_pairs={{0,16},{8,24},{16,0},{24,8},{1,17},{9,25},{17,1},{25,9},{2,18},{10... | collective-permute-start | bytes 1572872 | tf_op jit(solution)/shard_map/cond/branch_1_fun/ppermute | solution.py:47
  10.9 2.6 %collective-permute-start.9 = (f32[4,512]{1,0:T(4,128)S(1)}, f32[4,512]{1,0:T(4,128)S(1)}, u32[]{:S(2)}, u32[]{:S(2)}) collective-permute-start(f32[4,512]{1,0:T(4,128)S(1)} %pad_maximum_fusion.3), channel_id=1, source_target_pairs={{0,2},{1,3},{2,0},{3,1},{4,6},{5,7},{6,4},{7,5},{8,10},{9,11},{10,... | collective-permute-start | bytes 24584 | tf_op jit(solution)/shard_map/cond/branch_1_fun/ppermute | solution.py:47
  13.5 3.8 %collective-permute-start.10 = (f32[4,512]{1,0:T(4,128)S(1)}, f32[4,512]{1,0:T(4,128)S(1)}, u32[]{:S(2)}, u32[]{:S(2)}) collective-permute-start(f32[4,512]{1,0:T(4,128)S(1)} %fusion), channel_id=1, source_target_pairs={{0,4},{1,5},{2,6},{3,7},{4,0},{5,1},{6,2},{7,3},{8,12},{9,13},{10,... | collective-permute-start | bytes 24584 | tf_op jit(solution)/shard_map/cond/branch_1_fun/ppermute | solution.py:47
  17.3 5.8 %copy-start.4 = (bf16[1024,256]{1,0:T(8,128)(2,1)}, bf16[1024,256]{1,0:T(8,128)(2,1)S(1)}, u32[]{:S(2)}) copy-start(bf16[1024,256]{1,0:T(8,128)(2,1)S(1)} %collective-permute-done.6.emb_ref) | copy-start | bytes 1572868 | tf_op jit(solution)/shard_map/cond
  18.3 4.8 %copy-start = (bf16[1024,256]{1,0:T(8,128)(2,1)}, bf16[1024,256]{1,0:T(8,128)(2,1)S(1)}, u32[]{:S(2)}) copy-start(bf16[1024,256]{1,0:T(8,128)(2,1)S(1)} %collective-permute-done.7.emb_ref) | copy-start | bytes 1572868 | tf_op jit(solution)/shard_map/cond
  18.3 2.9 %collective-permute-start.11 = (f32[4,512]{1,0:T(4,128)S(1)}, f32[4,512]{1,0:T(4,128)S(1)}, u32[]{:S(2)}, u32[]{:S(2)}) collective-permute-start(f32[4,512]{1,0:T(4,128)S(1)} %add.21), channel_id=1, source_target_pairs={{0,16},{8,24},{16,0},{24,8},{1,17},{9,25},{17,1},{25,9},{2,18},{10... | collective-permute-start | bytes 24584 | tf_op jit(solution)/shard_map/cond/branch_1_fun/ppermute | solution.py:47
  18.7 7.8 %collective-permute-start.13 = (bf16[512,256]{1,0:T(8,128)(2,1)S(1)}, bf16[512,256]{1,0:T(8,128)(2,1)S(1)}, u32[]{:S(2)}, u32[]{:S(2)}) collective-permute-start(bf16[512,256]{1,0:T(8,128)(2,1)S(1)} %slice.32), channel_id=1, source_target_pairs={{0,16},{8,24},{16,0},{24,8},{1,17},{9,25},{17,1},{25,9},{2,18},{10... | collective-permute-start | bytes 786440 | tf_op jit(solution)/shard_map/cond/branch_1_fun/ppermute | solution.py:47
  19.9 6.6 %collective-permute-start.14 = (bf16[512,256]{1,0:T(8,128)(2,1)S(1)}, bf16[512,256]{1,0:T(8,128)(2,1)S(1)}, u32[]{:S(2)}, u32[]{:S(2)}) collective-permute-start(bf16[512,256]{1,0:T(8,128)(2,1)S(1)} %slice.33), channel_id=1, source_target_pairs={{0,8},{8,0},{16,24},{24,16},{1,9},{9,1},{17,25},{25,17},{2,10},{10... | collective-permute-start | bytes 786440 | tf_op jit(solution)/shard_map/cond/branch_1_fun/ppermute | solution.py:47
  21.3 4.4 %collective-permute-start.12 = (f32[8,512]{1,0:T(8,128)S(1)}, f32[8,512]{1,0:T(8,128)S(1)}, u32[]{:S(2)}, u32[]{:S(2)}) collective-permute-start(f32[8,512]{1,0:T(8,128)S(1)} %pad_maximum_fusion.1), channel_id=1, source_target_pairs={{0,8},{8,0},{16,24},{24,16},{1,9},{9,1},{17,25},{25,17},{2,10},{10... | collective-permute-start | bytes 49160 | tf_op jit(solution)/shard_map/cond/branch_1_fun/ppermute | solution.py:47
  26.6 2.4 %copy-start.2 = (bf16[1024,256]{1,0:T(8,128)(2,1)}, bf16[1024,256]{1,0:T(8,128)(2,1)S(1)}, u32[]{:S(2)}) copy-start(bf16[1024,256]{1,0:T(8,128)(2,1)S(1)} %constant_dynamic-update-slice_fusion.4.emb_ref) | copy-start | bytes 1572868 | tf_op jit(solution)/shard_map/cond
  29.0 3.3 %collective-permute-start.15 = (f32[8,512]{1,0:T(8,128)S(1)}, f32[8,512]{1,0:T(8,128)S(1)}, u32[]{:S(2)}, u32[]{:S(2)}) collective-permute-start(f32[8,512]{1,0:T(8,128)S(1)} %branch_1_fun.14), channel_id=1, source_target_pairs={{0,2},{1,3},{2,0},{3,1},{4,6},{5,7},{6,4},{7,5},{8,10},{9,11},{10,... | collective-permute-start | bytes 49160 | tf_op jit(solution)/shard_map/cond/branch_1_fun/ppermute | solution.py:47
  32.3 3.5 %collective-permute-start.16 = (f32[8,512]{1,0:T(8,128)S(1)}, f32[8,512]{1,0:T(8,128)S(1)}, u32[]{:S(2)}, u32[]{:S(2)}) collective-permute-start(f32[8,512]{1,0:T(8,128)S(1)} %add.22), channel_id=1, source_target_pairs={{0,4},{1,5},{2,6},{3,7},{4,0},{5,1},{6,2},{7,3},{8,12},{9,13},{10,... | collective-permute-start | bytes 49160 | tf_op jit(solution)/shard_map/cond/branch_1_fun/ppermute | solution.py:47
  35.8 10.4 %copy-start.1 = (bf16[1024,256]{1,0:T(8,128)(2,1)S(1)}, bf16[1024,256]{1,0:T(8,128)(2,1)}, u32[]{:S(2)}) copy-start(bf16[1024,256]{1,0:T(8,128)(2,1)} %copy-done) | copy-start | bytes 1572868 | tf_op jit(solution)/shard_map/cond
  35.8 10.4 %copy-start.3 = (bf16[1024,256]{1,0:T(8,128)(2,1)S(1)}, bf16[1024,256]{1,0:T(8,128)(2,1)}, u32[]{:S(2)}) copy-start(bf16[1024,256]{1,0:T(8,128)(2,1)} %copy-done.2) | copy-start | bytes 1572868 | tf_op jit(solution)/shard_map/cond
  35.8 10.4 %copy-start.5 = (bf16[1024,256]{1,0:T(8,128)(2,1)S(1)}, bf16[1024,256]{1,0:T(8,128)(2,1)}, u32[]{:S(2)}) copy-start(bf16[1024,256]{1,0:T(8,128)(2,1)} %copy-done.4) | copy-start | bytes 1572868 | tf_op jit(solution)/shard_map/cond
  39.4 2.8 %collective-permute-start.17 = (f32[16,512]{1,0:T(8,128)S(1)}, f32[16,512]{1,0:T(8,128)S(1)}, u32[]{:S(2)}, u32[]{:S(2)}) collective-permute-start(f32[16,512]{1,0:T(8,128)S(1)} %branch_1_fun.15), channel_id=1, source_target_pairs={{0,2},{1,3},{2,0},{3,1},{4,6},{5,7},{6,4},{7,5},{8,10},{9,11},{10,... | collective-permute-start | bytes 98312 | tf_op jit(solution)/shard_map/cond/branch_1_fun/ppermute | solution.py:47
  42.3 3.9 %collective-permute-start.18 = (f32[18,512]{1,0:T(8,128)S(1)}, f32[18,512]{1,0:T(8,128)S(1)}, u32[]{:S(2)}, u32[]{:S(2)}) collective-permute-start(f32[18,512]{1,0:T(8,128)S(1)} %pad_maximum_fusion.mine_ref), channel_id=1, source_target_pairs={{0,4},{1,5},{2,6},{3,7},{4,0},{5,1},{6,2},{7,3},{8,12},{9,13},{10,... | collective-permute-start | bytes 110600 | tf_op jit(solution)/shard_map/cond/branch_1_fun/ppermute | solution.py:47
  46.2 1.3 %collective-permute-start.20 = (f32[34,512]{1,0:T(8,128)S(1)}, f32[34,512]{1,0:T(8,128)S(1)}, u32[]{:S(2)}, u32[]{:S(2)}) collective-permute-start(f32[34,512]{1,0:T(8,128)S(1)} %get-tuple-element.101), channel_id=1, source_target_pairs={{0,1},{1,0},{2,3},{3,2},{4,5},{5,4},{6,7},{7,6},{8,9},{9,8},{10,11... | collective-permute-start | bytes 208904 | tf_op jit(solution)/shard_map/ppermute | solution.py:47
  53.5 2.0 %collective-permute-start.22 = (bf16[2,512,256]{2,1,0:T(8,128)(2,1)S(1)}, bf16[2,512,256]{2,1,0:T(8,128)(2,1)S(1)}, u32[]{:S(2)}, u32[]{:S(2)}) collective-permute-start(bf16[2,512,256]{2,1,0:T(8,128)(2,1)S(1)} %get-tuple-element.103.mine_ref), channel_id=1, source_target_pairs={{0,1},{1,0},{2,3},{3,2},{4,5},{5,4},{6,7},{7,6},{8,9},{9,8},{10,11... | collective-permute-start | bytes 1572872 | tf_op jit(solution)/shard_map/ppermute | solution.py:47

commit v4 on v3

--- a/solution.py
+++ b/solution.py
@@ -188,6 +188,21 @@
     return [jnp.broadcast_to(line, (8, line.shape[1])) for line in lines]
 
 
+def fetched_unit_kernel(pieces, *refs):
+    raw_refs, out_refs, held_refs, sem_ref = refs[:2], refs[2:4], refs[4:6], refs[6]
+    copies = []
+    for raw_ref, out_ref, held_ref in zip(raw_refs, out_refs, held_refs):
+        size = raw_ref.shape[0] // pieces
+        for at in range(pieces):
+            part = pl.ds(at * size, size)
+            copy = pltpu.make_async_copy(raw_ref.at[part], held_ref.at[part], sem_ref.at[len(copies)])
+            copy.start()
+            copies.append((copy, held_ref, out_ref, part))
+    for copy, held_ref, out_ref, part in copies:
+        copy.wait()
+        out_ref[part] = normalize_rows(held_ref[part])[0].astype(jnp.bfloat16)
+
+
 def lane_sums(weight, block, view, part):
     values = block[view, part]
     tile, rows = values.shape
@@ -209,9 +224,6 @@
     out_ref = refs[-1]
     blocks = (own_ref, one_ref, two_ref, three_ref)
     _, count, rows = own_ref.shape
-    if last:
-        cross = [jnp.zeros((8, rows), jnp.float32)] * 2
-        out_ref[...] = jnp.zeros(out_ref.shape, jnp.float32)
     for view in range(2):
         weight = spread(weight_ref, view)
         totals = [jnp.zeros((8, rows), jnp.float32)] * 4
@@ -225,29 +237,25 @@
             for at in range(4):
                 scaled = blocks[at][view, part] * scale
                 totals[at] = totals[at] + jnp.sum(scaled.reshape(-1, 8, rows), axis=0)
-                if last and at == 0:
-                    scaled = scaled * (jnp.log(own_ref[1 - view, part]) * EPS_SINK)
-                    cross[1 - view] = cross[1 - view] + jnp.sum(scaled.reshape(-1, 8, rows), axis=0)
             if last:
-                line = 10 + 2 * view + first // rows
+                line = 8 + 2 * view + first // rows
                 out_ref[line:line + 1, first % rows:first % rows + tile] = jnp.broadcast_to(scale, (tile, 128)).T[:1]
         for at in range(4):
             out_ref[2 * at + view:2 * at + view + 1] = jnp.sum(totals[at], axis=0, keepdims=True)
-    if last:
-        for view in range(2):
-            out_ref[8 + view:9 + view] = jnp.sum(cross[view], axis=0, keepdims=True)
+
+
+def pack_kernel(mine_ref, theirs_ref, out_ref):
+    out_ref[:8] = mine_ref[:8] + theirs_ref[:8]
+    out_ref[8:12] = mine_ref[8:12]
+    out_ref[12:16] = theirs_ref[8:12]
 
 
 def found_kernel(mine_ref, theirs_ref, soft_ref, out_ref):
-    totals = mine_ref[:10] + theirs_ref[:10]
-    weights = 1.0 / totals[:8]
     soft = soft_ref[...]
-    for view in range(2):
-        crossed = totals[8 + view:9 + view] * weights[1 - view:2 - view]
-        out_ref[view:view + 1] = jnp.log(soft[view:view + 1]) - crossed / TEMPER
-    out_ref[2:10] = mine_ref[10:18]
-    out_ref[10:18] = theirs_ref[10:18]
-    out_ref[18:26] = weights / TEMPER
+    out_ref[:2] = jnp.log(soft[:2])
+    out_ref[2:10] = mine_ref[8:16]
+    out_ref[10:18] = theirs_ref[8:16]
+    out_ref[18:26] = 1.0 / (TEMPER * (mine_ref[:8] + theirs_ref[:8]))
     out_ref[26:34] = 1.0 / (TEMPER * soft)
 
 
@@ -279,16 +287,19 @@
     return found_ref[line:line + 1]
 
 
-def pipeline(steps, products_of, factors_of, place, soft_ref, slope_ref, rows):
+def pipeline(steps, products_of, factors_of, place, soft_ref, slope_ref, rows, cross_of=None):
     def slopes(step, first, last):
         slot = step % 2
         own_of, other_of = factors_of(step)
         for at in range(first, last, 16):
             part = slice(at, at + 16)
-            soft = [jnp.exp2(soft_ref[(slot,) + place(view, part)] * (LOG2E / TEMPER)) for view in range(2)]
+            scores = [soft_ref[(slot,) + place(view, part)] for view in range(2)]
+            soft = [jnp.exp2(scores[view] * (LOG2E / TEMPER)) for view in range(2)]
             taken = [other_of(view, part, soft[view] * soft[view]) for view in range(2)]
             for view in range(2):
                 slope = own_of(view, part, soft[view]) - taken[1 - view]
+                if cross_of:
+                    cross_of(step, view, part, scores[view] * taken[1 - view])
                 slope_ref[(slot,) + place(view, part)] = slope.astype(jnp.bfloat16)
 
     for step in range(-1, steps + 1):
@@ -359,9 +370,8 @@
 
 
 def emb_grad_kernel(tile, own_ref, one_ref, two_ref, three_ref, emb_ref, raw_ref, found_ref,
-                    out_ref, loss_ref, col_ref, acc_ref, work_ref, slope_ref, rows_ref, sem_ref):
+                    out_ref, loss_ref, col_ref, acc_ref, work_ref, slope_ref, rows_ref, sem_ref, cross_ref):
     fetches = fetch_rows((raw_ref.at[0], raw_ref.at[1]), rows_ref, sem_ref)
-    loss_ref[...] = found_ref[:2]
     blocks = (own_ref, one_ref, two_ref, three_ref)
     rows = emb_ref.shape[0] // 2
     tiles = own_ref.shape[0] // tile
@@ -400,40 +410,49 @@
     def place(view, part):
         return (slice(view * rows + part.start, view * rows + part.stop),)
 
-    pipeline(len(blocks) * tiles, products_of, factors_of, place, work_ref, slope_ref, rows)
+    def cross_of(step, view, part, crossed):
+        lanes = sum(crossed[:, lane:lane + 128] for lane in range(0, tile, 128))
+        if step % tiles:
+            lanes = lanes + cross_ref[step // tiles, view, part]
+        cross_ref[step // tiles, view, part] = lanes
+
+    pipeline(len(blocks) * tiles, products_of, factors_of, place, work_ref, slope_ref, rows, cross_of)
     for view in range(2):
+        crossed = tree_sum([cross_ref[block, view] for block in range(len(blocks))])
+        loss_ref[view:view + 1] = found_ref[view:view + 1] - jnp.sum(crossed.T, axis=0, keepdims=True)
         part = slice(view * rows, (view + 1) * rows)
         total = tree_sum([acc_ref[block, part] for block in range(len(blocks))])
         fetches[view].wait()
         out_ref[view] = finish(total, rows_ref[view])
 
 
-def own_part_kernel(core_ref, mine_ref, embed_ref, proto_ref, sem_ref):
+def copy_all(pairs, sem_ref):
+    copies = [pltpu.make_async_copy(source, target, sem_ref.at[at]) for at, (source, target) in enumerate(pairs)]
+    for copy in copies:
+        copy.start()
+    for copy in copies:
+        copy.wait()
+
+
+def own_part_kernel(core_ref, mine_ref, made_ref, embed_ref, proto_ref, loss_ref, sem_ref):
     @pl.when(core_ref[0] == 0)
     def _():
-        copy = pltpu.make_async_copy(mine_ref, embed_ref, sem_ref)
-        copy.start()
-        copy.wait()
+        copy_all([(mine_ref, embed_ref), (made_ref, loss_ref)], sem_ref)
 
     @pl.when(core_ref[0] == 1)
     def _():
-        copy = pltpu.make_async_copy(mine_ref.at[1], proto_ref, sem_ref)
-        copy.start()
-        copy.wait()
-
-
-def other_part_kernel(core_ref, theirs_ref, embed_in_ref, proto_in_ref, embed_ref, proto_ref, sem_ref):
+        copy_all([(mine_ref.at[1], proto_ref)], sem_ref)
+
+
+def other_part_kernel(core_ref, theirs_ref, made_ref, embed_in_ref, proto_in_ref, loss_in_ref,
+                      embed_ref, proto_ref, loss_ref, sem_ref):
     @pl.when(core_ref[0] == 0)
     def _():
-        copy = pltpu.make_async_copy(theirs_ref.at[0], proto_ref, sem_ref)
-        copy.start()
-        copy.wait()
+        copy_all([(theirs_ref.at[0], proto_ref)], sem_ref)
 
     @pl.when(core_ref[0] == 1)
     def _():
-        copy = pltpu.make_async_copy(theirs_ref, embed_ref, sem_ref)
-        copy.start()
-        copy.wait()
+        copy_all([(theirs_ref, embed_ref), (made_ref, loss_ref)], sem_ref)
 
 
 def chip_masks(size, bits):
@@ -473,7 +492,7 @@
     _, count, rows = sinks[0].shape
     return pl.pallas_call(
         functools.partial(sweep_kernel, not sums, 128),
-        out_shape=jax.ShapeDtypeStruct((8 if sums else 16, rows), jnp.float32),
+        out_shape=jax.ShapeDtypeStruct((8 if sums else 12, rows), jnp.float32),
         in_specs=[VMEM] * (5 + len(sums)),
         out_specs=VMEM,
         compiler_params=SMALL,
@@ -520,8 +539,13 @@
     soft_total = jnp.concatenate([sums[at:at + 2] for at in (2, 10, 6, 14)])
     totals = chip_sum(swept(weights, sinks, first_sums(weights, sinks)), "proto", proto, 2)
     totals = swept(1.0 / totals, sinks)
-    got = swap(totals, "proto", proto, 2)
-    totals = jnp.concatenate([totals[:10] + got[:10], totals[10:14], got[10:14]])
+    totals = pl.pallas_call(
+        pack_kernel,
+        out_shape=jax.ShapeDtypeStruct((16, flat.shape[0] // 2), jnp.float32),
+        in_specs=[VMEM] * 2,
+        out_specs=VMEM,
+        compiler_params=SMALL,
+    )(totals, swap(totals, "proto", proto, 2))
     found = pl.pallas_call(
         found_kernel,
         out_shape=jax.ShapeDtypeStruct((34, flat.shape[0] // 2), jnp.float32),
@@ -566,7 +590,15 @@
     core = lax.axis_index("proto") % 2
     lead = core == 1
     raw_other = swap(prototypes, "proto", proto, 1)
-    flat, own = unit_rows(embeddings.reshape(2 * per_view, width), prototypes)
+    raws = (prototypes, embeddings.reshape(2 * per_view, width))
+    own, flat = pl.pallas_call(
+        functools.partial(fetched_unit_kernel, 2),
+        out_shape=[jax.ShapeDtypeStruct(raw.shape, jnp.bfloat16) for raw in raws],
+        in_specs=[HBM] * 2,
+        out_specs=[VMEM] * 2,
+        scratch_shapes=[pltpu.VMEM(raw.shape, jnp.bfloat16) for raw in raws] + [pltpu.SemaphoreType.DMA((4,))],
+        compiler_params=SMALL,
+    )(*raws)
     other, = unit_rows(raw_other)
     raw_other = swap(after(prototypes, own)[0], "proto", proto, 1)
     found, *gathered = lax.cond(
@@ -591,7 +623,7 @@
                 pltpu.VMEM((2, rows, lanes), jnp.bfloat16),
                 pltpu.VMEM((2, per_view, width), jnp.bfloat16),
                 pltpu.SemaphoreType.DMA((2,)),
-            ],
+            ] + [pltpu.VMEM((4, 2, per_view, 128), jnp.float32)] * (kernel is emb_grad_kernel),
             compiler_params=PARAMS,
         )(*operands, *raws, found if kernel is proto_grad_kernel else taken)[::-1]
 
@@ -607,28 +639,29 @@
 
     loss, mine = lax.cond(lead, proto_grads, emb_grads, flat, own, other, *gathered)
     theirs = swap(mine, "proto", proto, 1)
+    their_loss = swap(loss, "proto", proto, 1)
     outputs = (
         jax.ShapeDtypeStruct(embeddings.shape, jnp.bfloat16),
         jax.ShapeDtypeStruct(prototypes.shape, jnp.bfloat16),
+        jax.ShapeDtypeStruct((2, per_view), jnp.float32),
     )
     half_done = pl.pallas_call(
         own_part_kernel,
         out_shape=outputs,
-        in_specs=[SMEM, ANY],
-        out_specs=(ANY, ANY),
-        scratch_shapes=[pltpu.SemaphoreType.DMA],
-        compiler_params=SMALL,
-    )(core.reshape(1), mine)
-    grad_embed, grad_proto = pl.pallas_call(
+        in_specs=[SMEM, ANY, ANY],
+        out_specs=(ANY,) * 3,
+        scratch_shapes=[pltpu.SemaphoreType.DMA((2,))],
+        compiler_params=SMALL,
+    )(core.reshape(1), mine, loss)
+    return pl.pallas_call(
         other_part_kernel,
         out_shape=outputs,
-        in_specs=[SMEM, ANY, ANY, ANY],
-        out_specs=(ANY, ANY),
-        scratch_shapes=[pltpu.SemaphoreType.DMA],
-        input_output_aliases={2: 0, 3: 1},
-        compiler_params=SMALL,
-    )(core.reshape(1), theirs, *half_done)
-    return grad_embed, grad_proto, loss
+        in_specs=[SMEM] + [ANY] * 5,
+        out_specs=(ANY,) * 3,
+        scratch_shapes=[pltpu.SemaphoreType.DMA((2,))],
+        input_output_aliases={3: 0, 4: 1, 5: 2},
+        compiler_params=SMALL,
+    )(core.reshape(1), theirs, their_loss, *half_done)
 
 
 def solution(mesh):

time: 56.7 us -> 56.7 us (level)
  starting transfers between devices: 20.3 us -> 21.9 us
  Pallas kernels: 18.2 us -> 16.9 us
  waiting for transfers between devices: 16.2 us -> 15.6 us
    ppermute x18 -> x19, starting transfers between devices: 20.3 us -> 21.9 us  [swap(): return lax.ppermute(value, axis, [(i, i ^ mask) for i in range(size)])]
    pallas_call x2 -> x4, Pallas kernels: 1.52 us -> 3.03 us  [the longest x1 1.49 us: body(): pl.pallas_call(functools.partial(fetched_unit_kernel, 2), out_shape=[jax....]
    pallas_call x2 -> x1, Pallas kernels: 1.55 us -> 0.15 us  [unit_rows(): pl.pallas_call(unit_kernel, out_shape=[jax.ShapeDtypeStruct(raw.shape, jn...]
    pallas_call x2, Pallas kernels: 5.21 us -> 4.14 us  [swept(): pl.pallas_call(functools.partial(sweep_kernel, not sums, 128), out_shape=...]
    ppermute x18 -> x19, waiting for transfers between devices: 16.2 us -> 15.6 us  [swap(): return lax.ppermute(value, axis, [(i, i ^ mask) for i in range(size)])]
  transfers between devices with their start and end apart: 18 -> 19, of which waited for: 12 -> 12; matrix products, arithmetic and copies ran while one was open for 1% -> 1% of each run, Pallas kernels for 20% -> 19%
where the time goes in v4:
time: 56.7 us; the launch traced here: 56.2 us
  starting transfers between devices  21.9 us (39%)
  Pallas kernels  16.9 us (30%)
  waiting for transfers between devices  15.6 us (28%)
  between operations  0.89 us (2%)
    ppermute x19, starting transfers between devices, swap(): return lax.ppermute(value, axis, [(i, i ^ mask) for i in range(size)])  21.9 us
    ppermute x19, waiting for transfers between devices, swap(): return lax.ppermute(value, axis, [(i, i ^ mask) for i in range(size)])  15.6 us
    pallas_call x1, Pallas kernels, grads(): pl.pallas_call(functools.partial(kernel, lanes // 2 if kernel is proto_gr...  5.53 us
    pallas_call x2, Pallas kernels, swept(): pl.pallas_call(functools.partial(sweep_kernel, not sums, 128), out_shape=...  4.14 us
    pallas_call x4, Pallas kernels, scored(): pl.pallas_call(functools.partial(score_kernel, min(count, 256)), out_shap...  3.25 us
    pallas_call x1, Pallas kernels, body(): pl.pallas_call(functools.partial(fetched_unit_kernel, 2), out_shape=[jax....  1.49 us
  transfers between devices with their start and end apart: 19, of which 12 were waited for; matrix products, arithmetic and copies ran while one was open for 1% of the time, Pallas kernels for 19%

profile of v4, /device:TPU:1, one launch (start us, length us, event | category | flops | bytes accessed | tf_op | source)
XLA Modules:
  0.0 56.2 jit_solution(17141362922824272041)
XLA Ops:
  0.8 1.5 %shard_map.49 = (bf16[512,256]{1,0:T(8,128)(2,1)S(1)}, bf16[1024,256]{1,0:T(8,128)(2,1)S(1)}) custom-call(bf16[512,256]{1,0:T(8,128)(2,1)} %refs_0_.1, bf16[1024,256]{1,0:T(8,128)(2,1)} %bitcast.2), custom_call_target="tpu_custom_call" | custom-call | tf_op jit(solution)/shard_map/pallas_call | solution.py:594
  3.0 42.0 %conditional.2 = (f32[34,512]{1,0:T(8,128)S(1)}, bf16[1024,256]{1,0:T(8,128)(2,1)S(1)}, bf16[1024,256]{1,0:T(8,128)(2,1)S(1)}, bf16[1024,256]{1,0:T(8,128)(2,1)S(1)}) conditional(s32[]{:T(128)} %convert_element_type.4, (bf16[512,256]{1,0:T(8,128)(2,1)S(1)}, bf16[512,256]{1,0:T(8,128)(2,1)S(1)}) %tuple.28, (bf16[512,256]{1,0:T(8,128)(2,1)S(1)}, ...), branch_computations={%region_0.1_spmd, %region_1.3_spmd} | conditional | flops 2189485056 | bytes 37679864 | solution.py:604
  3.0 1.0 %branch_1_fun.10 = (f32[2,1024,512]{2,1,0:T(8,128)S(1)}, f32[2,512]{1,0:T(2,128)S(1)}, f32[2,1024]{1,0:T(2,128)S(1)}) custom-call(bf16[1024,256]{1,0:T(8,128)(2,1)S(1)} %get-tuple-element.50.emb_ref, bf16[1024,256]{1,0:T(8,128)(2,1)S(1)} %constant_dynamic-update-slice_fusion.2.proto_ref), custom_call_target="tpu_custom_call" | custom-call | flops 536870912 | bytes 1048576 | tf_op jit(solution)/shard_map/cond/branch_1_fun/pallas_call | solution.py:479
  4.0 2.3 %collective-permute-start.5 = (f32[2,1024]{1,0:T(2,128)S(1)}, f32[2,1024]{1,0:T(2,128)S(1)}, u32[]{:S(2)}, u32[]{:S(2)}) collective-permute-start(f32[2,1024]{1,0:T(2,128)S(1)} %get-tuple-element.49), channel_id=1, source_target_pairs={{0,8},{8,0},{16,24},{24,16},{1,9},{9,1},{17,25},{25,17},{2,10},{10... | collective-permute-start | bytes 24584 | tf_op jit(solution)/shard_map/cond/branch_1_fun/ppermute | solution.py:47
  6.4 1.3 %collective-permute-done.5 = f32[2,1024]{1,0:T(2,128)S(1)} collective-permute-done((f32[2,1024]{1,0:T(2,128)S(1)}, f32[2,1024]{1,0:T(2,128)S(1)}, u32[]{:S(2)}, u32[]{:S(2)}) %collective-permute-start.5) | collective-permute-done | bytes 8224 | tf_op jit(solution)/shard_map/cond/branch_1_fun/ppermute | solution.py:47
  7.7 1.5 %collective-permute-start.8 = (f32[2,1024]{1,0:T(2,128)S(1)}, f32[2,1024]{1,0:T(2,128)S(1)}, u32[]{:S(2)}, u32[]{:S(2)}) collective-permute-start(f32[2,1024]{1,0:T(2,128)S(1)} %add.16), channel_id=1, source_target_pairs={{0,16},{8,24},{16,0},{24,8},{1,17},{9,25},{17,1},{25,9},{2,18},{10... | collective-permute-start | bytes 24584 | tf_op jit(solution)/shard_map/cond/branch_1_fun/ppermute | solution.py:47
  9.2 1.2 %collective-permute-start.6 = (bf16[1024,256]{1,0:T(8,128)(2,1)S(1)}, bf16[1024,256]{1,0:T(8,128)(2,1)S(1)}, u32[]{:S(2)}, u32[]{:S(2)}) collective-permute-start(bf16[1024,256]{1,0:T(8,128)(2,1)S(1)} %get-tuple-element.50.emb_ref), channel_id=1, source_target_pairs={{0,8},{8,0},{16,24},{24,16},{1,9},{9,1},{17,25},{25,17},{2,10},{10... | collective-permute-start | bytes 1572872 | tf_op jit(solution)/shard_map/cond/branch_1_fun/ppermute | solution.py:47
  11.0 1.5 %collective-permute-start.9 = (f32[4,512]{1,0:T(4,128)S(1)}, f32[4,512]{1,0:T(4,128)S(1)}, u32[]{:S(2)}, u32[]{:S(2)}) collective-permute-start(f32[4,512]{1,0:T(4,128)S(1)} %pad_maximum_fusion.2), channel_id=1, source_target_pairs={{0,2},{1,3},{2,0},{3,1},{4,6},{5,7},{6,4},{7,5},{8,10},{9,11},{10,... | collective-permute-start | bytes 24584 | tf_op jit(solution)/shard_map/cond/branch_1_fun/ppermute | solution.py:47
  12.5 1.1 %collective-permute-done.9 = f32[4,512]{1,0:T(4,128)S(1)} collective-permute-done((f32[4,512]{1,0:T(4,128)S(1)}, f32[4,512]{1,0:T(4,128)S(1)}, u32[]{:S(2)}, u32[]{:S(2)}) %collective-permute-start.9) | collective-permute-done | bytes 8224 | tf_op jit(solution)/shard_map/cond/branch_1_fun/ppermute | solution.py:47
  13.6 2.8 %collective-permute-start.10 = (f32[4,512]{1,0:T(4,128)S(1)}, f32[4,512]{1,0:T(4,128)S(1)}, u32[]{:S(2)}, u32[]{:S(2)}) collective-permute-start(f32[4,512]{1,0:T(4,128)S(1)} %fusion), channel_id=1, source_target_pairs={{0,4},{1,5},{2,6},{3,7},{4,0},{5,1},{6,2},{7,3},{8,12},{9,13},{10,... | collective-permute-start | bytes 24584 | tf_op jit(solution)/shard_map/cond/branch_1_fun/ppermute | solution.py:47
  16.4 1.0 %collective-permute-done.10 = f32[4,512]{1,0:T(4,128)S(1)} collective-permute-done((f32[4,512]{1,0:T(4,128)S(1)}, f32[4,512]{1,0:T(4,128)S(1)}, u32[]{:S(2)}, u32[]{:S(2)}) %collective-permute-start.10) | collective-permute-done | bytes 8224 | tf_op jit(solution)/shard_map/cond/branch_1_fun/ppermute | solution.py:47
  17.5 1.0 %collective-permute-done.7.emb_ref = bf16[1024,256]{1,0:T(8,128)(2,1)S(1)} collective-permute-done((bf16[1024,256]{1,0:T(8,128)(2,1)S(1)}, bf16[1024,256]{1,0:T(8,128)(2,1)S(1)}, u32[]{:S(2)}, u32[]{:S(2)}) %collective-permute-start.7) | collective-permute-done | bytes 524320 | tf_op jit(solution)/shard_map/cond/branch_1_fun/ppermute | solution.py:47
  18.8 1.2 %collective-permute-start.13 = (bf16[512,256]{1,0:T(8,128)(2,1)S(1)}, bf16[512,256]{1,0:T(8,128)(2,1)S(1)}, u32[]{:S(2)}, u32[]{:S(2)}) collective-permute-start(bf16[512,256]{1,0:T(8,128)(2,1)S(1)} %slice.24), channel_id=1, source_target_pairs={{0,16},{8,24},{16,0},{24,8},{1,17},{9,25},{17,1},{25,9},{2,18},{10... | collective-permute-start | bytes 786440 | tf_op jit(solution)/shard_map/cond/branch_1_fun/ppermute | solution.py:47
  20.4 0.9 %collective-permute-done.11 = f32[4,512]{1,0:T(4,128)S(1)} collective-permute-done((f32[4,512]{1,0:T(4,128)S(1)}, f32[4,512]{1,0:T(4,128)S(1)}, u32[]{:S(2)}, u32[]{:S(2)}) %collective-permute-start.11) | collective-permute-done | bytes 8224 | tf_op jit(solution)/shard_map/cond/branch_1_fun/ppermute | solution.py:47
  22.5 0.7 %branch_1_fun.12.two_ref = f32[2,1024,512]{2,1,0:T(8,128)S(1)} custom-call(bf16[1024,256]{1,0:T(8,128)(2,1)S(1)} %collective-permute-done.7.emb_ref, bf16[1024,256]{1,0:T(8,128)(2,1)S(1)} %constant_dynamic-update-slice_fusion.2.proto_ref), custom_call_target="tpu_custom_call" | custom-call | flops 536870912 | bytes 1048576 | tf_op jit(solution)/shard_map/cond/branch_1_fun/pallas_call | solution.py:479
  23.3 2.5 %collective-permute-done.12 = f32[8,512]{1,0:T(8,128)S(1)} collective-permute-done((f32[8,512]{1,0:T(8,128)S(1)}, f32[8,512]{1,0:T(8,128)S(1)}, u32[]{:S(2)}, u32[]{:S(2)}) %collective-permute-start.12) | collective-permute-done | bytes 16416 | tf_op jit(solution)/shard_map/cond/branch_1_fun/ppermute | solution.py:47
  25.8 0.7 %branch_1_fun.14.refs_0_ = f32[2,2,1024,128]{3,2,1,0:T(8,128)S(1)} custom-call(f32[8,512]{1,0:T(8,128)S(1)} %maximum_divide_fusion.weight_ref, f32[2,1024,512]{2,1,0:T(8,128)S(1)} %get-tuple-element.51.own_ref, f32[2,1024,512]{2,1,0:T(8,128)S(1)} %branch_1_fun.11.one_ref, f32[2,1024,512]{2,1,0:T(8,128)S(1)} %branch_1_fun.12.two_ref), custom_call_target="tpu_custom_call" | custom-call | flops 6291456 | bytes 2097152 | tf_op jit(solution)/shard_map/cond/branch_1_fun/pallas_call | solution.py:505
  27.4 1.6 %branch_1_fun.15 = f32[8,512]{1,0:T(8,128)S(1)} custom-call(f32[8,512]{1,0:T(8,128)S(1)} %maximum_divide_fusion.weight_ref, f32[2,1024,512]{2,1,0:T(8,128)S(1)} %get-tuple-element.51.own_ref, f32[2,1024,512]{2,1,0:T(8,128)S(1)} %branch_1_fun.11.one_ref, f32[2,1024,512]{2,1,0:T(8,128)S(1)} %branch_1_fun.12.two_ref, ...), custom_call_target="tpu_custom_call" | custom-call | flops 16777216 | bytes 2097152 | tf_op jit(solution)/shard_map/cond/branch_1_fun/pallas_call | solution.py:493
  29.0 1.4 %collective-permute-start.15 = (f32[8,512]{1,0:T(8,128)S(1)}, f32[8,512]{1,0:T(8,128)S(1)}, u32[]{:S(2)}, u32[]{:S(2)}) collective-permute-start(f32[8,512]{1,0:T(8,128)S(1)} %branch_1_fun.15), channel_id=1, source_target_pairs={{0,2},{1,3},{2,0},{3,1},{4,6},{5,7},{6,4},{7,5},{8,10},{9,11},{10,... | collective-permute-start | bytes 49160 | tf_op jit(solution)/shard_map/cond/branch_1_fun/ppermute | solution.py:47
  30.5 1.8 %collective-permute-done.15 = f32[8,512]{1,0:T(8,128)S(1)} collective-permute-done((f32[8,512]{1,0:T(8,128)S(1)}, f32[8,512]{1,0:T(8,128)S(1)}, u32[]{:S(2)}, u32[]{:S(2)}) %collective-permute-start.15) | collective-permute-done | bytes 16416 | tf_op jit(solution)/shard_map/cond/branch_1_fun/ppermute | solution.py:47
  32.3 2.4 %collective-permute-start.16 = (f32[8,512]{1,0:T(8,128)S(1)}, f32[8,512]{1,0:T(8,128)S(1)}, u32[]{:S(2)}, u32[]{:S(2)}) collective-permute-start(f32[8,512]{1,0:T(8,128)S(1)} %add.20), channel_id=1, source_target_pairs={{0,4},{1,5},{2,6},{3,7},{4,0},{5,1},{6,2},{7,3},{8,12},{9,13},{10,... | collective-permute-start | bytes 49160 | tf_op jit(solution)/shard_map/cond/branch_1_fun/ppermute | solution.py:47
  34.7 1.1 %collective-permute-done.16 = f32[8,512]{1,0:T(8,128)S(1)} collective-permute-done((f32[8,512]{1,0:T(8,128)S(1)}, f32[8,512]{1,0:T(8,128)S(1)}, u32[]{:S(2)}, u32[]{:S(2)}) %collective-permute-start.16) | collective-permute-done | bytes 16416 | tf_op jit(solution)/shard_map/cond/branch_1_fun/ppermute | solution.py:47
  35.9 2.5 %branch_1_fun.16.mine_ref = f32[12,512]{1,0:T(8,128)S(1)} custom-call(f32[8,512]{1,0:T(8,128)S(1)} %add_divide_fusion.weight_ref, f32[2,1024,512]{2,1,0:T(8,128)S(1)} %get-tuple-element.51.own_ref, f32[2,1024,512]{2,1,0:T(8,128)S(1)} %branch_1_fun.11.one_ref, f32[2,1024,512]{2,1,0:T(8,128)S(1)} %branch_1_fun.12.two_ref, ...), custom_call_target="tpu_custom_call" | custom-call | flops 16777216 | bytes 2097152 | tf_op jit(solution)/shard_map/cond/branch_1_fun/pallas_call | solution.py:493
  38.4 1.4 %collective-permute-start.17 = (f32[12,512]{1,0:T(8,128)S(1)}, f32[12,512]{1,0:T(8,128)S(1)}, u32[]{:S(2)}, u32[]{:S(2)}) collective-permute-start(f32[12,512]{1,0:T(8,128)S(1)} %branch_1_fun.16.mine_ref), channel_id=1, source_target_pairs={{0,2},{1,3},{2,0},{3,1},{4,6},{5,7},{6,4},{7,5},{8,10},{9,11},{10,... | collective-permute-start | bytes 73736 | tf_op jit(solution)/shard_map/cond/branch_1_fun/ppermute | solution.py:47
  39.8 1.4 %collective-permute-done.17.theirs_ref = f32[12,512]{1,0:T(8,128)S(1)} collective-permute-done((f32[12,512]{1,0:T(8,128)S(1)}, f32[12,512]{1,0:T(8,128)S(1)}, u32[]{:S(2)}, u32[]{:S(2)}) %collective-permute-start.17) | collective-permute-done | bytes 24608 | tf_op jit(solution)/shard_map/cond/branch_1_fun/ppermute | solution.py:47
  41.3 2.4 %collective-permute-start.18 = (f32[16,512]{1,0:T(8,128)S(1)}, f32[16,512]{1,0:T(8,128)S(1)}, u32[]{:S(2)}, u32[]{:S(2)}) collective-permute-start(f32[16,512]{1,0:T(8,128)S(1)} %branch_1_fun.17.mine_ref), channel_id=1, source_target_pairs={{0,4},{1,5},{2,6},{3,7},{4,0},{5,1},{6,2},{7,3},{8,12},{9,13},{10,... | collective-permute-start | bytes 98312 | tf_op jit(solution)/shard_map/cond/branch_1_fun/ppermute | solution.py:47
  43.6 1.3 %collective-permute-done.18.theirs_ref = f32[16,512]{1,0:T(8,128)S(1)} collective-permute-done((f32[16,512]{1,0:T(8,128)S(1)}, f32[16,512]{1,0:T(8,128)S(1)}, u32[]{:S(2)}, u32[]{:S(2)}) %collective-permute-start.18) | collective-permute-done | bytes 32800 | tf_op jit(solution)/shard_map/cond/branch_1_fun/ppermute | solution.py:47
  45.1 1.3 %collective-permute-done.20 = f32[34,512]{1,0:T(8,128)S(1)} collective-permute-done((f32[34,512]{1,0:T(8,128)S(1)}, f32[34,512]{1,0:T(8,128)S(1)}, u32[]{:S(2)}, u32[]{:S(2)}) %collective-permute-start.20) | collective-permute-done | bytes 69664 | tf_op jit(solution)/shard_map/ppermute | solution.py:47
  46.3 5.6 %conditional.3 = (f32[2,512]{1,0:T(2,128)S(1)}, bf16[2,512,256]{2,1,0:T(8,128)(2,1)S(1)}) conditional(s32[]{:T(128)} %convert_element_type.4, (bf16[512,256]{1,0:T(8,128)(2,1)S(1)}, bf16[512,256]{1,0:T(8,128)(2,1)S(1)}, bf16[1024,256]{1,0:T(8,128)(2,1)S(1)}, bf16[1024,256]{1,0:T(8,128)(2,1)S(1)}, bf16[1024,256]{1,0:T(8,128)(2,1)S(1)}, ...), branch_computations={%region_3.4_spmd, %region_4.5_spmd} | conditional | flops 1048576 | bytes 1048592 | solution.py:640
  46.4 5.5 %branch_1_fun.19 = (bf16[2,512,256]{2,1,0:T(8,128)(2,1)S(1)}, f32[2,512]{1,0:T(2,128)S(1)}) custom-call(bf16[1024,256]{1,0:T(8,128)(2,1)S(1)} %get-tuple-element.69.own_ref, bf16[1024,256]{1,0:T(8,128)(2,1)S(1)} %get-tuple-element.70.one_ref, bf16[1024,256]{1,0:T(8,128)(2,1)S(1)} %get-tuple-element.71.two_ref, ...), custom_call_target="tpu_custom_call" | custom-call | tf_op jit(solution)/shard_map/cond/branch_1_fun/pallas_call | solution.py:611
  51.9 1.7 %collective-permute-start.22 = (bf16[2,512,256]{2,1,0:T(8,128)(2,1)S(1)}, bf16[2,512,256]{2,1,0:T(8,128)(2,1)S(1)}, u32[]{:S(2)}, u32[]{:S(2)}) collective-permute-start(bf16[2,512,256]{2,1,0:T(8,128)(2,1)S(1)} %get-tuple-element.102.mine_ref), channel_id=1, source_target_pairs={{0,1},{1,0},{2,3},{3,2},{4,5},{5,4},{6,7},{7,6},{8,9},{9,8},{10,11... | collective-permute-start | bytes 1572872 | tf_op jit(solution)/shard_map/ppermute | solution.py:47
  55.2 0.8 %shard_map.52 = (bf16[2,512,256]{2,1,0:T(8,128)(2,1)}, bf16[512,256]{1,0:T(8,128)(2,1)}, f32[2,512]{1,0:T(2,128)}) custom-call(s32[1]{0:T(128)} %bitcast.core_ref, bf16[2,512,256]{2,1,0:T(8,128)(2,1)S(1)} %collective-permute-done.22.theirs_ref, ...), custom_call_target="tpu_custom_call", output_to_operand_aliasing={{0}: (3, {}), {1}: (4, {}), {2}: (5, {})} | custom-call | tf_op jit(solution)/shard_map/pallas_call | solution.py:656
  (59 shorter events, 5.9 us)
Async XLA Ops:
  0.6 2.1 %collective-permute-start.19 = (bf16[512,256]{1,0:T(8,128)(2,1)}, bf16[512,256]{1,0:T(8,128)(2,1)S(1)}, u32[]{:S(2)}, u32[]{:S(2)}) collective-permute-start(bf16[512,256]{1,0:T(8,128)(2,1)} %refs_0_.1), channel_id=1, source_target_pairs={{0,1},{1,0},{2,3},{3,2},{4,5},{5,4},{6,7},{7,6},{8,9},{9,8},{10,11... | collective-permute-start | bytes 786440 | tf_op jit(solution)/shard_map/ppermute | solution.py:47
  2.2 42.8 %collective-permute-start.21 = (bf16[512,256]{1,0:T(8,128)(2,1)}, bf16[512,256]{1,0:T(8,128)(2,1)}, u32[]{:S(2)}, u32[]{:S(2)}) collective-permute-start(bf16[512,256]{1,0:T(8,128)(2,1)} %refs_0_.1), channel_id=1, source_target_pairs={{0,1},{1,0},{2,3},{3,2},{4,5},{5,4},{6,7},{7,6},{8,9},{9,8},{10,11... | collective-permute-start | bytes 786440 | tf_op jit(solution)/shard_map/ppermute | solution.py:47
  2.9 43.4 %copy-start.6 = (bf16[2,512,256]{2,1,0:T(8,128)(2,1)S(1)}, bf16[2,512,256]{2,1,0:T(8,128)(2,1)}, u32[]{:S(2)}) copy-start(bf16[2,512,256]{2,1,0:T(8,128)(2,1)} %param.6) | copy-start | bytes 1572868
  2.9 43.4 %copy-start.7 = (bf16[512,256]{1,0:T(8,128)(2,1)S(1)}, bf16[512,256]{1,0:T(8,128)(2,1)}, u32[]{:S(2)}) copy-start(bf16[512,256]{1,0:T(8,128)(2,1)} %refs_0_.1) | copy-start | bytes 786436
  4.0 3.6 %collective-permute-start.5 = (f32[2,1024]{1,0:T(2,128)S(1)}, f32[2,1024]{1,0:T(2,128)S(1)}, u32[]{:S(2)}, u32[]{:S(2)}) collective-permute-start(f32[2,1024]{1,0:T(2,128)S(1)} %get-tuple-element.49), channel_id=1, source_target_pairs={{0,8},{8,0},{16,24},{24,16},{1,9},{9,1},{17,25},{25,17},{2,10},{10... | collective-permute-start | bytes 24584 | tf_op jit(solution)/shard_map/cond/branch_1_fun/ppermute | solution.py:47
  7.7 2.9 %collective-permute-start.8 = (f32[2,1024]{1,0:T(2,128)S(1)}, f32[2,1024]{1,0:T(2,128)S(1)}, u32[]{:S(2)}, u32[]{:S(2)}) collective-permute-start(f32[2,1024]{1,0:T(2,128)S(1)} %add.16), channel_id=1, source_target_pairs={{0,16},{8,24},{16,0},{24,8},{1,17},{9,25},{17,1},{25,9},{2,18},{10... | collective-permute-start | bytes 24584 | tf_op jit(solution)/shard_map/cond/branch_1_fun/ppermute | solution.py:47
  9.2 8.2 %collective-permute-start.6 = (bf16[1024,256]{1,0:T(8,128)(2,1)S(1)}, bf16[1024,256]{1,0:T(8,128)(2,1)S(1)}, u32[]{:S(2)}, u32[]{:S(2)}) collective-permute-start(bf16[1024,256]{1,0:T(8,128)(2,1)S(1)} %get-tuple-element.50.emb_ref), channel_id=1, source_target_pairs={{0,8},{8,0},{16,24},{24,16},{1,9},{9,1},{17,25},{25,17},{2,10},{10... | collective-permute-start | bytes 1572872 | tf_op jit(solution)/shard_map/cond/branch_1_fun/ppermute | solution.py:47
  10.4 8.0 %collective-permute-start.7 = (bf16[1024,256]{1,0:T(8,128)(2,1)S(1)}, bf16[1024,256]{1,0:T(8,128)(2,1)S(1)}, u32[]{:S(2)}, u32[]{:S(2)}) collective-permute-start(bf16[1024,256]{1,0:T(8,128)(2,1)S(1)} %get-tuple-element.50.emb_ref), channel_id=1, source_target_pairs={{0,16},{8,24},{16,0},{24,8},{1,17},{9,25},{17,1},{25,9},{2,18},{10... | collective-permute-start | bytes 1572872 | tf_op jit(solution)/shard_map/cond/branch_1_fun/ppermute | solution.py:47
  11.0 2.6 %collective-permute-start.9 = (f32[4,512]{1,0:T(4,128)S(1)}, f32[4,512]{1,0:T(4,128)S(1)}, u32[]{:S(2)}, u32[]{:S(2)}) collective-permute-start(f32[4,512]{1,0:T(4,128)S(1)} %pad_maximum_fusion.2), channel_id=1, source_target_pairs={{0,2},{1,3},{2,0},{3,1},{4,6},{5,7},{6,4},{7,5},{8,10},{9,11},{10,... | collective-permute-start | bytes 24584 | tf_op jit(solution)/shard_map/cond/branch_1_fun/ppermute | solution.py:47
  13.6 3.8 %collective-permute-start.10 = (f32[4,512]{1,0:T(4,128)S(1)}, f32[4,512]{1,0:T(4,128)S(1)}, u32[]{:S(2)}, u32[]{:S(2)}) collective-permute-start(f32[4,512]{1,0:T(4,128)S(1)} %fusion), channel_id=1, source_target_pairs={{0,4},{1,5},{2,6},{3,7},{4,0},{5,1},{6,2},{7,3},{8,12},{9,13},{10,... | collective-permute-start | bytes 24584 | tf_op jit(solution)/shard_map/cond/branch_1_fun/ppermute | solution.py:47
  17.4 5.8 %copy-start.4 = (bf16[1024,256]{1,0:T(8,128)(2,1)}, bf16[1024,256]{1,0:T(8,128)(2,1)S(1)}, u32[]{:S(2)}) copy-start(bf16[1024,256]{1,0:T(8,128)(2,1)S(1)} %collective-permute-done.6.emb_ref) | copy-start | bytes 1572868 | tf_op jit(solution)/shard_map/cond
  18.4 4.8 %copy-start = (bf16[1024,256]{1,0:T(8,128)(2,1)}, bf16[1024,256]{1,0:T(8,128)(2,1)S(1)}, u32[]{:S(2)}) copy-start(bf16[1024,256]{1,0:T(8,128)(2,1)S(1)} %collective-permute-done.7.emb_ref) | copy-start | bytes 1572868 | tf_op jit(solution)/shard_map/cond
  18.4 2.9 %collective-permute-start.11 = (f32[4,512]{1,0:T(4,128)S(1)}, f32[4,512]{1,0:T(4,128)S(1)}, u32[]{:S(2)}, u32[]{:S(2)}) collective-permute-start(f32[4,512]{1,0:T(4,128)S(1)} %add.19), channel_id=1, source_target_pairs={{0,16},{8,24},{16,0},{24,8},{1,17},{9,25},{17,1},{25,9},{2,18},{10... | collective-permute-start | bytes 24584 | tf_op jit(solution)/shard_map/cond/branch_1_fun/ppermute | solution.py:47
  18.8 7.8 %collective-permute-start.13 = (bf16[512,256]{1,0:T(8,128)(2,1)S(1)}, bf16[512,256]{1,0:T(8,128)(2,1)S(1)}, u32[]{:S(2)}, u32[]{:S(2)}) collective-permute-start(bf16[512,256]{1,0:T(8,128)(2,1)S(1)} %slice.24), channel_id=1, source_target_pairs={{0,16},{8,24},{16,0},{24,8},{1,17},{9,25},{17,1},{25,9},{2,18},{10... | collective-permute-start | bytes 786440 | tf_op jit(solution)/shard_map/cond/branch_1_fun/ppermute | solution.py:47
  20.0 6.6 %collective-permute-start.14 = (bf16[512,256]{1,0:T(8,128)(2,1)S(1)}, bf16[512,256]{1,0:T(8,128)(2,1)S(1)}, u32[]{:S(2)}, u32[]{:S(2)}) collective-permute-start(bf16[512,256]{1,0:T(8,128)(2,1)S(1)} %slice.25), channel_id=1, source_target_pairs={{0,8},{8,0},{16,24},{24,16},{1,9},{9,1},{17,25},{25,17},{2,10},{10... | collective-permute-start | bytes 786440 | tf_op jit(solution)/shard_map/cond/branch_1_fun/ppermute | solution.py:47
  21.3 4.4 %collective-permute-start.12 = (f32[8,512]{1,0:T(8,128)S(1)}, f32[8,512]{1,0:T(8,128)S(1)}, u32[]{:S(2)}, u32[]{:S(2)}) collective-permute-start(f32[8,512]{1,0:T(8,128)S(1)} %pad_maximum_fusion), channel_id=1, source_target_pairs={{0,8},{8,0},{16,24},{24,16},{1,9},{9,1},{17,25},{25,17},{2,10},{10... | collective-permute-start | bytes 49160 | tf_op jit(solution)/shard_map/cond/branch_1_fun/ppermute | solution.py:47
  26.7 2.4 %copy-start.2 = (bf16[1024,256]{1,0:T(8,128)(2,1)}, bf16[1024,256]{1,0:T(8,128)(2,1)S(1)}, u32[]{:S(2)}) copy-start(bf16[1024,256]{1,0:T(8,128)(2,1)S(1)} %constant_dynamic-update-slice_fusion.4.emb_ref) | copy-start | bytes 1572868 | tf_op jit(solution)/shard_map/cond
  29.0 3.3 %collective-permute-start.15 = (f32[8,512]{1,0:T(8,128)S(1)}, f32[8,512]{1,0:T(8,128)S(1)}, u32[]{:S(2)}, u32[]{:S(2)}) collective-permute-start(f32[8,512]{1,0:T(8,128)S(1)} %branch_1_fun.15), channel_id=1, source_target_pairs={{0,2},{1,3},{2,0},{3,1},{4,6},{5,7},{6,4},{7,5},{8,10},{9,11},{10,... | collective-permute-start | bytes 49160 | tf_op jit(solution)/shard_map/cond/branch_1_fun/ppermute | solution.py:47
  32.3 3.5 %collective-permute-start.16 = (f32[8,512]{1,0:T(8,128)S(1)}, f32[8,512]{1,0:T(8,128)S(1)}, u32[]{:S(2)}, u32[]{:S(2)}) collective-permute-start(f32[8,512]{1,0:T(8,128)S(1)} %add.20), channel_id=1, source_target_pairs={{0,4},{1,5},{2,6},{3,7},{4,0},{5,1},{6,2},{7,3},{8,12},{9,13},{10,... | collective-permute-start | bytes 49160 | tf_op jit(solution)/shard_map/cond/branch_1_fun/ppermute | solution.py:47
  35.9 9.1 %copy-start.1 = (bf16[1024,256]{1,0:T(8,128)(2,1)S(1)}, bf16[1024,256]{1,0:T(8,128)(2,1)}, u32[]{:S(2)}) copy-start(bf16[1024,256]{1,0:T(8,128)(2,1)} %copy-done) | copy-start | bytes 1572868 | tf_op jit(solution)/shard_map/cond
  35.9 9.1 %copy-start.3 = (bf16[1024,256]{1,0:T(8,128)(2,1)S(1)}, bf16[1024,256]{1,0:T(8,128)(2,1)}, u32[]{:S(2)}) copy-start(bf16[1024,256]{1,0:T(8,128)(2,1)} %copy-done.2) | copy-start | bytes 1572868 | tf_op jit(solution)/shard_map/cond
  35.9 9.1 %copy-start.5 = (bf16[1024,256]{1,0:T(8,128)(2,1)S(1)}, bf16[1024,256]{1,0:T(8,128)(2,1)}, u32[]{:S(2)}) copy-start(bf16[1024,256]{1,0:T(8,128)(2,1)} %copy-done.4) | copy-start | bytes 1572868 | tf_op jit(solution)/shard_map/cond
  38.4 2.8 %collective-permute-start.17 = (f32[12,512]{1,0:T(8,128)S(1)}, f32[12,512]{1,0:T(8,128)S(1)}, u32[]{:S(2)}, u32[]{:S(2)}) collective-permute-start(f32[12,512]{1,0:T(8,128)S(1)} %branch_1_fun.16.mine_ref), channel_id=1, source_target_pairs={{0,2},{1,3},{2,0},{3,1},{4,6},{5,7},{6,4},{7,5},{8,10},{9,11},{10,... | collective-permute-start | bytes 73736 | tf_op jit(solution)/shard_map/cond/branch_1_fun/ppermute | solution.py:47
  41.3 3.7 %collective-permute-start.18 = (f32[16,512]{1,0:T(8,128)S(1)}, f32[16,512]{1,0:T(8,128)S(1)}, u32[]{:S(2)}, u32[]{:S(2)}) collective-permute-start(f32[16,512]{1,0:T(8,128)S(1)} %branch_1_fun.17.mine_ref), channel_id=1, source_target_pairs={{0,4},{1,5},{2,6},{3,7},{4,0},{5,1},{6,2},{7,3},{8,12},{9,13},{10,... | collective-permute-start | bytes 98312 | tf_op jit(solution)/shard_map/cond/branch_1_fun/ppermute | solution.py:47
  45.0 1.3 %collective-permute-start.20 = (f32[34,512]{1,0:T(8,128)S(1)}, f32[34,512]{1,0:T(8,128)S(1)}, u32[]{:S(2)}, u32[]{:S(2)}) collective-permute-start(f32[34,512]{1,0:T(8,128)S(1)} %get-tuple-element.100), channel_id=1, source_target_pairs={{0,1},{1,0},{2,3},{3,2},{4,5},{5,4},{6,7},{7,6},{8,9},{9,8},{10,11... | collective-permute-start | bytes 208904 | tf_op jit(solution)/shard_map/ppermute | solution.py:47
  51.9 3.3 %collective-permute-start.22 = (bf16[2,512,256]{2,1,0:T(8,128)(2,1)S(1)}, bf16[2,512,256]{2,1,0:T(8,128)(2,1)S(1)}, u32[]{:S(2)}, u32[]{:S(2)}) collective-permute-start(bf16[2,512,256]{2,1,0:T(8,128)(2,1)S(1)} %get-tuple-element.102.mine_ref), channel_id=1, source_target_pairs={{0,1},{1,0},{2,3},{3,2},{4,5},{5,4},{6,7},{7,6},{8,9},{9,8},{10,11... | collective-permute-start | bytes 1572872 | tf_op jit(solution)/shard_map/ppermute | solution.py:47
  53.6 1.5 %collective-permute-start.23 = (f32[2,512]{1,0:T(2,128)S(1)}, f32[2,512]{1,0:T(2,128)S(1)}, u32[]{:S(2)}, u32[]{:S(2)}) collective-permute-start(f32[2,512]{1,0:T(2,128)S(1)} %get-tuple-element.103.made_ref), channel_id=1, source_target_pairs={{0,1},{1,0},{2,3},{3,2},{4,5},{5,4},{6,7},{7,6},{8,9},{9,8},{10,11... | collective-permute-start | bytes 12296 | tf_op jit(solution)/shard_map/ppermute | solution.py:47
